TPU v7x, 512 devices: a whole 4x8x8 slice. The times are simulated.
512 devices in a mesh: cube: 4 (over z_lo), facet: 32 (over y, z_hi, core), dp: 4 (over x).
Axes of the slice: x: 4, y: 8, z: 8 (z_hi: 2, z_lo: 4; z = z_hi * 4 + z_lo), core: 2. Of those that a mesh axis runs over, the one named last changes fastest.
Arguments:
- image: float32 [4, 1536, 2560], P('cube', 'facet'), may hold values from 0 to 2
- dual: bfloat16 [4, 4, 1536, 2560], P(None, 'cube', 'facet'), may hold values from -5 to 5
- payload: bfloat16 [4, 8192, 16, 128], P('cube', ('facet', 'dp')), may hold values from -6 to 6
- vis_weight: bfloat16 [4, 8192, 16], P('cube', ('facet', 'dp')), may hold values from 0.25 to 2
- freq_start: int32 [4, 8192], P('cube', ('facet', 'dp')), may hold values from 0 to 2559
- tile_slot: int32 [4, 8192], P('cube', ('facet', 'dp')), may hold values from 0 to 5, as said below
- live: int32 [4, 128], P('cube', ('facet', 'dp')), may hold values from 1 to 64, as said below
Outputs:
- image_next: float32 [4, 1536, 2560], P('cube', 'facet')
- dual_next: bfloat16 [4, 4, 1536, 2560], P(None, 'cube', 'facet')
Inputs may be any that keep to these rules, and one draw needn't show every extreme that they name: `tile_slot`: A block's tile lies in its own facet or the one above; blocks of the first facet use their own facet only. The live blocks of a worker are its first slots; in every draw some worker of each channel has all 64 slots live.
All inputs are finite; a program needn't handle non-finite values.
Results may differ from a plain program's by a relative error of at most 0.011.
Values may be sent and summed in bfloat16 or wider, within the bound.
No kernel may reach another device: no remote copies, remote signals or barrier semaphores. Data moves between devices by JAX's collectives and lax.ppermute only.
A program may use at most 64 MiB of HBM per device.

v0:
```python
import math

import jax
import jax.numpy as jnp
from jax import lax
from jax.sharding import PartitionSpec as P

GROUP = 8


LOWPASS = (
    0.2303778133088964,
    0.7148465705529155,
    0.6308807679298587,
    -0.027983769416859854,
    -0.18703481171909309,
    0.030841381835560764,
    0.0328830116668852,
    -0.010597401785069032,
)
HIGHPASS = (
    -0.010597401785069032,
    -0.0328830116668852,
    0.030841381835560764,
    0.18703481171909309,
    -0.027983769416859854,
    -0.6308807679298587,
    0.7148465705529155,
    -0.2303778133088964,
)
TAU_STEP = 0.5
SIGMA_STEP = 0.5
RADIUS = 3.0


def shifted(block, axis, distance):
    devices = range(lax.axis_size(axis))
    route = [(i - distance, i) for i in devices if i - distance in devices]
    return lax.ppermute(block, axis, route)


def forward_axis(padded, filter_taps, along, length):
    summed = filter_taps[0] * lax.slice_in_dim(padded, 7, 7 + length, axis=along)
    for k in range(1, 8):
        summed = summed + filter_taps[k] * lax.slice_in_dim(
            padded, 7 - k, 7 - k + length, axis=along
        )
    return summed


def backward_axis(padded, filter_taps, along, length):
    summed = filter_taps[0] * lax.slice_in_dim(padded, 0, length, axis=along)
    for k in range(1, 8):
        summed = summed + filter_taps[k] * lax.slice_in_dim(padded, k, k + length, axis=along)
    return summed


def analyze(padded, height, breadth):
    subbands = []
    for row_taps in (LOWPASS, HIGHPASS):
        filtered = forward_axis(padded, row_taps, 0, height)
        for col_taps in (LOWPASS, HIGHPASS):
            subbands.append(forward_axis(filtered, col_taps, 1, breadth))
    return jnp.stack(subbands)


def synthesize(coefficients, leading, height):
    breadth = coefficients.shape[-1]
    summed = jnp.zeros((height, breadth), jnp.float32)
    for a, row_taps in enumerate((LOWPASS, HIGHPASS)):
        for b, col_taps in enumerate((LOWPASS, HIGHPASS)):
            subband = coefficients[2 * a + b]
            across = backward_axis(jnp.pad(subband, ((0, 0), (0, 7))), col_taps, 1, breadth)
            summed = summed + backward_axis(
                jnp.pad(across, ((leading, 7), (0, 0))), row_taps, 0, height
            )
    return summed


def freq_table(breadth, count):
    columns = jnp.arange(breadth, dtype=jnp.int32)
    freqs = jnp.arange(count, dtype=jnp.int32)
    angles = (columns[:, None] * freqs[None, :] % breadth).astype(jnp.float32) * (
        2.0 * math.pi / breadth
    )
    return jnp.concatenate([jnp.cos(angles), -jnp.sin(angles)], 1).astype(jnp.bfloat16)


def block_terms(tile_block, payload, weights, starts, live_mask, spectrum_table, breadth):
    columns = jnp.arange(breadth, dtype=jnp.int32)
    phases = (starts[:, None] * columns[None, :] % breadth).astype(jnp.float32) * (
        2.0 * math.pi / breadth
    )
    cosine = jnp.cos(phases)[:, None, :]
    minus_sine = -jnp.sin(phases)[:, None, :]
    pixels = tile_block.astype(jnp.float32)
    stacked = jnp.concatenate([pixels * cosine, pixels * minus_sine], 1).astype(jnp.bfloat16)
    spectra = jnp.einsum("gtw,wk->gtk", stacked, spectrum_table, preferred_element_type=jnp.float32)
    height = tile_block.shape[1]
    half_width = spectrum_table.shape[1] // 2
    upper_half = spectra[:, :height]
    lower_half = spectra[:, height:]
    norm_scale = 1.0 / math.sqrt(breadth)
    model_vis = (
        jnp.concatenate(
            [
                upper_half[..., :half_width] - lower_half[..., half_width:],
                upper_half[..., half_width:] + lower_half[..., :half_width],
            ],
            -1,
        )
        * norm_scale
    )
    factor = live_mask.astype(jnp.float32)[:, None, None] * weights.astype(jnp.float32)[:, :, None]
    misfit = factor * (model_vis - payload.astype(jnp.float32))
    paired = jnp.concatenate(
        [misfit, jnp.concatenate([misfit[..., half_width:], -misfit[..., :half_width]], -1)], 1
    ).astype(jnp.bfloat16)
    adjoint_rows = jnp.einsum(
        "gtk,wk->gtw", paired, spectrum_table, preferred_element_type=jnp.float32
    )
    return (cosine * adjoint_rows[:, :height] + minus_sine * adjoint_rows[:, height:]) * norm_scale


def on_device(image, dual, payload, vis_weight, freq_start, tile_slot, live):
    own_rows = image[0]
    height, breadth = own_rows.shape
    blocks = payload.shape[1]
    tile_rows = payload.shape[2]
    spectrum_table = freq_table(breadth, payload.shape[3] // 2)
    pixels = own_rows.astype(jnp.bfloat16)
    rows_above = shifted(pixels, "facet", 1)
    extended = jnp.concatenate([rows_above, pixels], 0)
    slot_index = jnp.arange(blocks, dtype=jnp.int32)
    live_mask = (slot_index < live[0, 0]).astype(jnp.int32)
    records = (payload[0], vis_weight[0])
    labels = (freq_start[0], tile_slot[0], live_mask)
    last_live = jnp.max(labels[2] * (slot_index + 1))
    rounds = (last_live + GROUP - 1) // GROUP

    def advance(step_index, gradient):
        first_slot = step_index * GROUP
        window_items = [
            lax.dynamic_slice_in_dim(values, first_slot, GROUP, 0) for values in records + labels
        ]
        offsets = window_items[3] * tile_rows
        tile_block = jnp.stack(
            [lax.dynamic_slice_in_dim(extended, offsets[i], tile_rows, 0) for i in range(GROUP)]
        )
        term_rows = block_terms(
            tile_block,
            window_items[0],
            window_items[1],
            window_items[2],
            window_items[4],
            spectrum_table,
            breadth,
        )
        for i in range(GROUP):
            current = lax.dynamic_slice_in_dim(gradient, offsets[i], tile_rows, 0)
            gradient = lax.dynamic_update_slice_in_dim(
                gradient, current + term_rows[i], offsets[i], 0
            )
        return gradient

    gradient = lax.fori_loop(0, rounds, advance, jnp.zeros((2 * height, breadth), jnp.float32))
    current_dual = dual[:, 0].astype(jnp.float32)
    synthesized = synthesize(current_dual, 7, height + 7)
    summed_grad = lax.psum(gradient.astype(jnp.bfloat16), "dp").astype(jnp.float32)
    summed_grad = summed_grad.at[height - 7 :].add(synthesized)
    from_below = shifted(summed_grad[:height], "facet", -1)
    updated = jnp.maximum(own_rows - TAU_STEP * (summed_grad[height:] + from_below), 0.0)
    extrapolated = 2.0 * updated - own_rows
    prior_rows = shifted(extrapolated[height - 7 :], "facet", 1)
    stretched = jnp.pad(jnp.concatenate([prior_rows, extrapolated], 0), ((0, 0), (7, 0)))
    shifted_dual = current_dual + SIGMA_STEP * analyze(stretched, height, breadth)
    squares = lax.psum((shifted_dual * shifted_dual).astype(jnp.bfloat16), "cube").astype(
        jnp.float32
    )
    dual_next = (shifted_dual * (RADIUS / jnp.maximum(jnp.sqrt(squares), RADIUS))).astype(
        jnp.bfloat16
    )
    return (updated[None], dual_next[:, None])


def solution(mesh):
    return jax.shard_map(
        on_device,
        mesh=mesh,
        in_specs=(
            P("cube", "facet", None),
            P(None, "cube", "facet", None),
            P("cube", ("facet", "dp"), None, None),
            P("cube", ("facet", "dp"), None),
            P("cube", ("facet", "dp")),
            P("cube", ("facet", "dp")),
            P("cube", ("facet", "dp")),
        ),
        out_specs=(P("cube", "facet", None), P(None, "cube", "facet", None)),
        check_vma=False,
    )
```

profile of v0, /device:TPU:1, one launch (start us, length us, event | category | flops | bytes accessed | tf_op | source)
XLA Modules:
  0.0 505.6 jit_solution(15277366514695893870)
XLA Ops:
  7.2 1.1 bitcast_convert_fusion
  8.4 12.0 %collective-permute-start = (bf16[48,2560]{1,0:T(8,128)(2,1)S(1)}, bf16[48,2560]{1,0:T(8,128)(2,1)S(1)}, u32[]{:S(2)}, u32[]{:S(2)}) collective-permute-start(bf16[48,2560]{1,0:T(8,128)(2,1)S(1)} %bitcast_convert_fusion), channel_id=1, source_target_pairs={{0,4},{4,8},{8,12},{12,16},{16,20},{20,24},{24,28},{28,32},{32,36}... | collective-permute-start | bytes 737288 | tf_op jit(solution)/shard_map/ppermute | solution.py:39
  20.4 2.8 negate_convert_fusion
  23.4 1.1 slice_bitcast_fusion.8
  24.5 2.8 multiply_add_fusion.2
  29.9 194.4 %while.13 = (s32[]{:T(128)}, f32[96,2560]{1,0:T(8,128)S(1)}, s32[]{:T(128)}, s32[64]{0:T(128)S(1)}, s32[64]{0:T(128)S(1)}, /*index=5*/s32[64]{0:T(128)S(1)}, bf1...) while((s32[]{:T(128)}, f32[96,2560]{1,0:T(8,128)S(1)}, ...), condition=%wide.region_2.3_spmd, body=%wide.region_1.2_spmd.sunk | while | flops 341975360 | bytes 20170876 | solution.py:166
  47.6 0.9 fusion.150
  50.1 1.7 dynamic_update_slice.56
  52.5 1.7 dynamic_update_slice.57
  55.0 1.7 dynamic_update_slice.58
  57.4 1.7 dynamic_update_slice.59
  59.8 1.7 dynamic_update_slice.60
  62.3 1.7 dynamic_update_slice.61
  64.7 1.7 dynamic_update_slice.62
  67.2 1.7 dynamic_update_slice.63
  86.6 0.9 fusion.150
  89.1 1.7 dynamic_update_slice.56
  91.6 1.7 dynamic_update_slice.57
  94.0 1.7 dynamic_update_slice.58
  96.4 1.7 dynamic_update_slice.59
  98.9 1.7 dynamic_update_slice.60
  101.3 1.7 dynamic_update_slice.61
  103.8 1.5 dynamic_update_slice.62
  106.0 1.5 dynamic_update_slice.63
  125.2 0.9 fusion.150
  127.6 1.7 dynamic_update_slice.56
  130.1 1.7 dynamic_update_slice.57
  132.5 1.7 dynamic_update_slice.58
  135.0 1.7 dynamic_update_slice.59
  137.4 1.7 dynamic_update_slice.60
  139.9 1.7 dynamic_update_slice.61
  142.3 1.7 dynamic_update_slice.62
  144.7 1.7 dynamic_update_slice.63
  164.2 0.9 fusion.150
  166.7 1.7 dynamic_update_slice.56
  169.1 1.7 dynamic_update_slice.57
  171.6 1.7 dynamic_update_slice.58
  174.0 1.7 dynamic_update_slice.59
  176.4 1.7 dynamic_update_slice.60
  178.9 1.7 dynamic_update_slice.61
  181.3 1.7 dynamic_update_slice.62
  183.8 1.7 dynamic_update_slice.63
  205.7 1.7 dynamic_update_slice.56
  208.2 1.7 dynamic_update_slice.57
  210.6 1.7 dynamic_update_slice.58
  213.1 1.7 dynamic_update_slice.59
  215.5 1.5 dynamic_update_slice.60
  217.7 1.7 dynamic_update_slice.61
  220.1 1.7 dynamic_update_slice.62
  222.6 1.7 dynamic_update_slice.63
  225.7 2.8 multiply_add_fusion.4
  228.5 158.3 %all-reduce.12.cloned.1.call-done = bf16[96,2560]{1,0:T(8,128)(2,1)} async-done(((bf16[96,2560]{1,0:T(8,128)(2,1)}), bf16[96,2560]{1,0:T(8,128)(2,1)}) %all-reduce.12.cloned.1.call-update) | async-done | bytes 491536 | tf_op jit(solution)/shard_map/psum | solution.py:169
  386.8 1.1 convert_element_type.97
  388.0 5.6 %fusion.53 = f32[55,2560]{1,0:T(8,128)S(1)} fusion(f32[48,2560]{1,0:T(8,128)} %get-tuple-element.209, f32[48,2560]{1,0:T(8,128)} %get-tuple-element.208, f32[48,2560]{1,0:T(8,128)S(1)} %copy-done.5, f32[48,2560]{1,0:T(8,128)S(1)} %copy-done.4, f32[96,2560]{1,0:T(8,128)S(1)} %convert_element_type.97), kind=kLoop, calls=%fused_computation.126 | loop fusion | flops 9011200 | bytes 3092480 | tf_op jit(solution)/shard_map/add | solution.py:170
  394.4 4.7 collective-permute-start.1
  399.1 16.7 %collective-permute-done.1 = f32[48,2560]{1,0:T(8,128)S(1)} collective-permute-done((f32[48,2560]{1,0:T(8,128)S(1)}, f32[48,2560]{1,0:T(8,128)S(1)}, u32[]{:S(2)}, u32[]{:S(2)}) %collective-permute-start.1) | collective-permute-done | bytes 491552 | tf_op jit(solution)/shard_map/ppermute | solution.py:39
  415.9 0.9 bitcast_subtract_fusion
  416.8 2.1 collective-permute-start.2
  418.9 1.3 collective-permute-done.2
  421.2 1.0 add_bitcast_fusion.3
  422.1 1.0 add_bitcast_fusion.1
  423.9 1.2 multiply_convert_fusion.1
  425.2 70.4 %all-reduce.14.cloned.1.call-done = bf16[4,48,2560]{2,1,0:T(8,128)(2,1)} async-done(((bf16[4,48,2560]{2,1,0:T(8,128)(2,1)}), bf16[4,48,2560]{2,1,0:T(8,128)(2,1)}) %all-reduce.14.cloned.1.call-update) | async-done | bytes 983056 | tf_op jit(solution)/shard_map/psum | solution.py:177
  495.5 3.3 fusion.36
  (182 shorter events, 50.6 us)
Async XLA Ops:
  7.2 16.1 %copy-start = (bf16[4,1,48,2560]{3,2,1,0:T(8,128)(2,1)S(1)}, bf16[4,1,48,2560]{3,2,1,0:T(8,128)(2,1)}, u32[]{:S(2)}) copy-start(bf16[4,1,48,2560]{3,2,1,0:T(8,128)(2,1)} %param.12) | copy-start | bytes 2949124
  7.2 379.6 %all-reduce.12.cloned.1.call-start = ((), (), s32[]{:S(2)}) async-start(), calls=%async_computation | async-start | bytes 983040 | tf_op jit(solution)/shard_map/psum | solution.py:169
  8.4 21.4 %collective-permute-start = (bf16[48,2560]{1,0:T(8,128)(2,1)S(1)}, bf16[48,2560]{1,0:T(8,128)(2,1)S(1)}, u32[]{:S(2)}, u32[]{:S(2)}) collective-permute-start(bf16[48,2560]{1,0:T(8,128)(2,1)S(1)} %bitcast_convert_fusion), channel_id=1, source_target_pairs={{0,4},{4,8},{8,12},{12,16},{16,20},{20,24},{24,28},{28,32},{32,36}... | collective-permute-start | bytes 737288 | tf_op jit(solution)/shard_map/ppermute | solution.py:39
  24.5 4.7 copy-start.9
  27.4 2.5 copy-start.8
  27.4 2.5 copy-start.10
  224.3 1.2 copy-start.6
  224.3 1.3 copy-start.7
  225.2 162.8 %copy-start.4 = (f32[48,2560]{1,0:T(8,128)S(1)}, f32[48,2560]{1,0:T(8,128)}, u32[]{:S(2)}) copy-start(f32[48,2560]{1,0:T(8,128)} %get-tuple-element.206) | copy-start | bytes 1474564
  225.2 162.8 %copy-start.5 = (f32[48,2560]{1,0:T(8,128)S(1)}, f32[48,2560]{1,0:T(8,128)}, u32[]{:S(2)}) copy-start(f32[48,2560]{1,0:T(8,128)} %get-tuple-element.207) | copy-start | bytes 1474564
  225.2 270.3 %all-reduce.14.cloned.1.call-start = ((), (), s32[]{:S(2)}) async-start(), calls=%async_computation.1 | async-start | bytes 1966080 | tf_op jit(solution)/shard_map/psum | solution.py:177
  387.9 27.9 %copy-start.3 = (f32[1,48,2560]{2,1,0:T(8,128)S(1)}, f32[1,48,2560]{2,1,0:T(8,128)}, u32[]{:S(2)}) copy-start(f32[1,48,2560]{2,1,0:T(8,128)} %param.11) | copy-start | bytes 1474564
  394.4 21.5 %collective-permute-start.1 = (f32[48,2560]{1,0:T(8,128)S(1)}, f32[48,2560]{1,0:T(8,128)S(1)}, u32[]{:S(2)}, u32[]{:S(2)}) collective-permute-start(f32[48,2560]{1,0:T(8,128)S(1)} %slice.606), channel_id=1, source_target_pairs={{4,0},{8,4},{12,8},{16,12},{20,16},{24,20},{28,24},{32,28},{36,32}... | collective-permute-start | bytes 1474568 | tf_op jit(solution)/shard_map/ppermute | solution.py:39
  416.8 3.4 collective-permute-start.2
  422.1 1.8 copy-start.1
  423.1 0.8 copy-start.2
Sparse Core Ops, SparseCore 0:
  225.3 161.4 all-reduce.11
  425.3 70.2 all-reduce.13
where the time goes:
time: 510 us; the launch traced here: 506 us
  waiting for transfers between devices  247 us (48%)
  local copies, waits for them, and re-layouts  78 us (15%)
  loops' own time  77 us (15%)
  other arithmetic  64.2 us (13%)
  starting transfers between devices  18.9 us (4%)
  between operations  15.6 us (3%)
  matrix products  5.2 us (1%)
    psum x1, waiting for transfers between devices, on_device(): lax.psum(gradient.astype(jnp.bfloat16), 'dp').astype(jnp.float32)  158 us
    another operation x1, loops' own time, on_device(): lax.fori_loop(0, rounds, advance, jnp.zeros((2 * height, breadth), jnp.fl...  77 us
    psum x1, waiting for transfers between devices, on_device(): lax.psum((shifted_dual * shifted_dual).astype(jnp.bfloat16), 'cube')  70.4 us
    dynamic_update_slice x40, local copies, waits for them, and re-layouts, advance(): lax.dynamic_update_slice_in_dim(gradient, current + term_rows[i], offsets...  68.8 us
    add x40, other arithmetic, advance(): current + term_rows[i]  27.9 us
    ppermute x3, starting transfers between devices, shifted(): return lax.ppermute(block, axis, route)  18.8 us
    ppermute x3, waiting for transfers between devices, shifted(): return lax.ppermute(block, axis, route)  18 us
  transfers between devices with their start and end apart: 5, of which 4 were waited for; matrix products, arithmetic and copies ran while one was open for 2% of the time, Pallas kernels for 0%

commit v1 on v0

v1 whole, which is shorter than its diff:
```python
import functools
import math

import jax
import jax.numpy as jnp
import numpy as np
from jax import lax
from jax.experimental import pallas as pl
from jax.experimental.pallas import tpu as pltpu
from jax.sharding import PartitionSpec as P

LOWPASS = (
    0.2303778133088964,
    0.7148465705529155,
    0.6308807679298587,
    -0.027983769416859854,
    -0.18703481171909309,
    0.030841381835560764,
    0.0328830116668852,
    -0.010597401785069032,
)
HIGHPASS = (
    -0.010597401785069032,
    -0.0328830116668852,
    0.030841381835560764,
    0.18703481171909309,
    -0.027983769416859854,
    -0.6308807679298587,
    0.7148465705529155,
    -0.2303778133088964,
)
TAU_STEP = 0.5
SIGMA_STEP = 0.5
RADIUS = 3.0

W = 2560
TILE = 16
FR = 48
BLK = 64
PER = FR // TILE
Q = 20
R = 128
DP = 4
PART = W // DP
HALO = 128
SPAN = PART + HALO
CHUNKS = W // 64
UNROLL = 4
NORM = 1.0 / math.sqrt(W)
C1, C2 = math.cos(2 * math.pi / 5), math.cos(4 * math.pi / 5)
S1, S2 = math.sin(2 * math.pi / 5), math.sin(4 * math.pi / 5)


def tables():
    x = np.arange(W).reshape(R, Q).T
    angles = (x[:, :, None] * np.arange(R)[None, None, :] % W) * (2.0 * math.pi / W)
    table = np.concatenate([np.cos(angles), -np.sin(angles)], -1).astype(jnp.bfloat16)
    y = np.arange(PART)
    order = np.zeros((PART, PART), np.float32)
    order[y, (y % Q) * 32 + y // Q] = 1.0
    return table, order.astype(jnp.bfloat16)


def times_i(value, sign):
    re, im = value
    return (-im, re) if sign > 0 else (im, -re)


def plus(u, v):
    return (u[0] + v[0], u[1] + v[1])


def minus(u, v):
    return (u[0] - v[0], u[1] - v[1])


def dft4(x, sign):
    a, b = plus(x[0], x[2]), minus(x[0], x[2])
    c, d = plus(x[1], x[3]), times_i(minus(x[1], x[3]), sign)
    return [plus(a, c), plus(b, d), minus(a, c), minus(b, d)]


def dft5(x, sign):
    t1, t2 = plus(x[1], x[4]), plus(x[2], x[3])
    t3, t4 = minus(x[1], x[4]), minus(x[2], x[3])
    m1 = tuple(z + C1 * u + C2 * v for z, u, v in zip(x[0], t1, t2))
    m2 = tuple(z + C2 * u + C1 * v for z, u, v in zip(x[0], t1, t2))
    n1 = times_i(tuple(S1 * u + S2 * v for u, v in zip(t3, t4)), sign)
    n2 = times_i(tuple(S2 * u - S1 * v for u, v in zip(t3, t4)), sign)
    return [plus(x[0], plus(t1, t2)), plus(m1, n1), plus(m2, n2), minus(m2, n2), minus(m1, n1)]


def dft20(x, sign):
    columns = [dft4([x[(5 * a + 4 * b) % 20] for a in range(4)], sign) for b in range(5)]
    out = [None] * 20
    for c in range(4):
        line = dft5([columns[b][c] for b in range(5)], sign)
        for e in range(5):
            out[(5 * c + 16 * e) % 20] = line[e]
    return out


def facet_pass(
    base,
    starts_ref,
    slots_ref,
    live_ref,
    pixels_ref,
    payload_ref,
    weight_ref,
    table_ref,
    order_ref,
    out_ref,
    re_ref,
    im_ref,
    spec_ref,
    grad_ref,
    list_ref,
):
    lane = lax.broadcasted_iota(jnp.int32, (1, 128), 1)
    low = lane < 64
    half = lane % 64
    quarter = lane // 32

    def collect(b, count):
        slot = slots_ref[b] - base
        list_ref[count] = b
        return count + jnp.where((slot >= 0) & (slot < PER), 1, 0)

    count = lax.fori_loop(0, live_ref[0], collect, 0)
    for u in range(UNROLL):
        list_ref[count + u] = list_ref[0]

    stacked = jnp.concatenate(
        [pixels_ref[:, PART * g : PART * (g + 1)] for g in range(4)], 0
    )
    sorted_rows = jnp.dot(stacked, order_ref[...], preferred_element_type=jnp.float32)
    for j in range(5):
        tiles = [sorted_rows[FR * g : FR * (g + 1), 128 * j : 128 * (j + 1)] for g in range(4)]
        for p in range(4):
            turned = [
                tiles[g] if g == p else pltpu.roll(tiles[g], (32 * (g - p)) % 128, 1)
                for g in range(4)
            ]
            rows = turned[3]
            for g in range(3):
                rows = jnp.where(quarter == g, turned[g], rows)
            q = 4 * j + p
            partial = jnp.dot(
                rows.astype(jnp.bfloat16), table_ref[q], preferred_element_type=jnp.float32
            )
            re_ref[q] = partial[:, :R]
            im_ref[q] = partial[:, R:]

    def forward(i, carry):
        rows = pl.ds(pl.multiple_of(i * 8, 8), 8)
        spectrum = dft20([(re_ref[q, rows, :], im_ref[q, rows, :]) for q in range(Q)], -1)
        for k, (re, im) in enumerate(spectrum):
            re, im = re * NORM, im * NORM
            spec_ref[2 * k, rows, :] = jnp.where(low, re, pltpu.roll(im, 64, 1))
            spec_ref[2 * k + 1, rows, :] = jnp.where(low, pltpu.roll(re, 64, 1), im)
        return carry

    lax.fori_loop(0, FR // 8, forward, 0)
    spec_ref[CHUNKS] = spec_ref[0]
    grad_ref[...] = jnp.zeros_like(grad_ref)

    def blocks(step, carry):
        found = []
        for u in range(UNROLL):
            place = step * UNROLL + u
            b = list_ref[place]
            start = starts_ref[b]
            slot = jnp.clip(slots_ref[b] - base, 0, PER - 1)
            chunk = start // 64
            offset = start % 64
            rows = pl.ds(pl.multiple_of(slot * TILE, TILE), TILE)
            first = pltpu.roll(spec_ref[chunk, rows, :], (128 - offset) % 128, 1)
            second = pltpu.roll(spec_ref[chunk + 1, rows, :], 64 - offset, 1)
            model = jnp.where(half < 64 - offset, first, second)
            factor = weight_ref[b].astype(jnp.float32) * jnp.where(place < count, 1.0, 0.0)
            misfit = factor * (model - payload_ref[b].astype(jnp.float32))
            lower = jnp.where(half >= offset, pltpu.roll(misfit, offset, 1), 0.0)
            upper = jnp.where(half < offset, pltpu.roll(misfit, 64 + offset, 1), 0.0)
            found.append((chunk, rows, lower, upper))
        for chunk, rows, lower, upper in found:
            grad_ref[chunk, rows, :] += lower
            grad_ref[chunk + 1, rows, :] += upper
        return carry

    lax.fori_loop(0, (count + UNROLL - 1) // UNROLL, blocks, 0)
    grad_ref[0] += grad_ref[CHUNKS]

    def backward(i, carry):
        rows = pl.ds(pl.multiple_of(i * 8, 8), 8)
        spectrum = []
        for k in range(Q):
            even, odd = grad_ref[2 * k, rows, :], grad_ref[2 * k + 1, rows, :]
            spectrum.append(
                (
                    jnp.where(low, even, pltpu.roll(odd, 64, 1)),
                    jnp.where(low, pltpu.roll(even, 64, 1), odd),
                )
            )
        for q, (re, im) in enumerate(dft20(spectrum, 1)):
            re_ref[q, rows, :] = re * NORM
            im_ref[q, rows, :] = im * NORM
        return carry

    lax.fori_loop(0, FR // 8, backward, 0)
    for j in range(5):
        places = [[] for _ in range(4)]
        for p in range(4):
            q = 4 * j + p
            pair = jnp.concatenate([re_ref[q], im_ref[q]], 1).astype(jnp.bfloat16)
            rows = lax.dot_general(
                pair, table_ref[q], (((1,), (1,)), ((), ())), preferred_element_type=jnp.float32
            )
            for g in range(4):
                places[g].append(rows if g == p else pltpu.roll(rows, (32 * (p - g)) % 128, 1))
        for g in range(4):
            tile = places[g][3]
            for p in range(3):
                tile = jnp.where(quarter == p, places[g][p], tile)
            spec_ref[5 * g + j] = tile
    mixed = jnp.concatenate(
        [jnp.concatenate([spec_ref[5 * g + j] for j in range(5)], 1) for g in range(4)], 0
    ).astype(jnp.bfloat16)
    natural = lax.dot_general(
        mixed, order_ref[...], (((1,), (1,)), ((), ())), preferred_element_type=jnp.float32
    ).astype(jnp.bfloat16)
    out_ref[0, :, :HALO] = jnp.zeros((FR, HALO), jnp.bfloat16)
    for g in range(4):
        rows = natural[FR * g : FR * (g + 1)]
        out_ref[g, :, HALO:] = rows
        if g < 3:
            out_ref[g + 1, :, :HALO] = rows[:, PART - HALO :]


def facet_terms(base, pixels, payload, weights, starts, slots, live, table, order):
    smem = pl.BlockSpec(memory_space=pltpu.SMEM)
    vmem = pl.BlockSpec(memory_space=pltpu.VMEM)
    return pl.pallas_call(
        functools.partial(facet_pass, base),
        out_shape=jax.ShapeDtypeStruct((DP, FR, SPAN), jnp.bfloat16),
        in_specs=[smem] * 3 + [vmem] * 5,
        out_specs=vmem,
        scratch_shapes=[
            pltpu.VMEM((Q, FR, R), jnp.float32),
            pltpu.VMEM((Q, FR, R), jnp.float32),
            pltpu.VMEM((CHUNKS + 1, FR, 128), jnp.float32),
            pltpu.VMEM((CHUNKS + 1, FR, 128), jnp.float32),
            pltpu.SMEM((BLK + UNROLL,), jnp.int32),
        ],
        compiler_params=pltpu.CompilerParams(vmem_limit_bytes=32 * 1024 * 1024),
        cost_estimate=pl.CostEstimate(
            flops=2 * 10**9, bytes_accessed=4 * 10**6, transcendentals=0
        ),
        name=f"facet_terms_{base}",
    )(starts, slots, live, pixels, payload, weights, table, order)


def hop(block, distance):
    devices = range(lax.axis_size("facet"))
    route = [(i - distance, i) for i in devices if i - distance in devices]
    return lax.ppermute(block, "facet", route)


def gathered_sum(parts):
    mixed = lax.all_to_all(parts, "dp", 0, 0)
    return jnp.sum(mixed.astype(jnp.float32), 0)


def synthesize(dual):
    summed = jnp.zeros((FR + 8, SPAN), jnp.float32)
    for a, row_taps in enumerate((LOWPASS, HIGHPASS)):
        across = jnp.zeros((FR, SPAN), jnp.float32)
        for b, col_taps in enumerate((LOWPASS, HIGHPASS)):
            for k in range(8):
                across = across + col_taps[k] * dual[2 * a + b][:, k : k + SPAN]
        padded = jnp.pad(across, ((8, 7), (0, 0)))
        for k in range(8):
            summed = summed + row_taps[k] * padded[k : k + FR + 8]
    return summed


def analyze(extra):
    subbands = []
    for row_taps in (LOWPASS, HIGHPASS):
        filtered = sum(row_taps[k] * extra[8 - k : 8 - k + FR] for k in range(8))
        for col_taps in (LOWPASS, HIGHPASS):
            subbands.append(
                sum(col_taps[k] * filtered[:, HALO - k : HALO - k + PART] for k in range(8))
            )
    return jnp.stack(subbands)


def on_device(image, dual, payload, vis_weight, freq_start, tile_slot, live):
    table, order = tables()
    table, order = jnp.asarray(table), jnp.asarray(order)
    position = lax.axis_index("dp")
    facet = lax.axis_index("facet")
    own_rows = image[0]
    pixels = own_rows.astype(jnp.bfloat16)
    rows_above = hop(pixels, 1)
    weights = jnp.broadcast_to(vis_weight[0][:, :, None], payload.shape[1:])
    blocks = (payload[0], weights, freq_start[0], tile_slot[0], live[0], table, order)

    left = position * PART
    own_dual = lax.dynamic_slice_in_dim(
        jnp.pad(dual[:, 0], ((0, 0), (0, 0), (HALO, 128))), left, SPAN + 128, 2
    ).astype(jnp.float32)
    own_image = lax.dynamic_slice_in_dim(
        jnp.pad(own_rows, ((0, 0), (HALO, 0))), left, SPAN, 1
    )
    synth = synthesize(own_dual)

    own_terms = facet_terms(PER, pixels, *blocks)
    own_sum = gathered_sum(own_terms) + synth[8:]
    last_rows = hop(own_sum[FR - 8 :].astype(jnp.bfloat16), 1)
    upper_terms = facet_terms(0, rows_above, *blocks)
    upper_sum = gathered_sum(upper_terms) + jnp.pad(synth[:8], ((FR - 8, 0), (0, 0)))
    from_below = hop(upper_sum.astype(jnp.bfloat16), -1)

    total = own_sum + from_below.astype(jnp.float32)
    above = last_rows.astype(jnp.float32) + upper_sum[FR - 8 :]
    image_above = lax.dynamic_slice_in_dim(
        jnp.pad(rows_above[FR - 8 :], ((0, 0), (HALO, 0))), left, SPAN, 1
    ).astype(jnp.float32)
    old = jnp.concatenate([image_above, own_image], 0)
    new = jnp.maximum(old - TAU_STEP * jnp.concatenate([above, total], 0), 0.0)
    column = lax.broadcasted_iota(jnp.int32, old.shape, 1) + left
    row = lax.broadcasted_iota(jnp.int32, old.shape, 0)
    inside = (column >= HALO) & ((row >= 8) | (facet > 0))
    extra = jnp.where(inside, 2.0 * new - old, 0.0)

    shifted = own_dual[:, :, HALO : HALO + PART] + SIGMA_STEP * analyze(extra)
    squares = lax.all_gather((shifted * shifted).astype(jnp.bfloat16), "cube")
    norms = jnp.sqrt(jnp.sum(squares.astype(jnp.float32), 0))
    dual_part = (shifted * (RADIUS / jnp.maximum(norms, RADIUS))).astype(jnp.bfloat16)
    dual_next = lax.all_gather(dual_part, "dp", axis=2, tiled=True)
    descent = lax.all_gather(total[:, HALO:].astype(jnp.bfloat16), "dp", axis=1, tiled=True)
    updated = jnp.maximum(own_rows - TAU_STEP * descent.astype(jnp.float32), 0.0)
    return (updated[None], dual_next[:, None])


def solution(mesh):
    return jax.shard_map(
        on_device,
        mesh=mesh,
        in_specs=(
            P("cube", "facet", None),
            P(None, "cube", "facet", None),
            P("cube", ("facet", "dp"), None, None),
            P("cube", ("facet", "dp"), None),
            P("cube", ("facet", "dp")),
            P("cube", ("facet", "dp")),
            P("cube", ("facet", "dp")),
        ),
        out_specs=(P("cube", "facet", None), P(None, "cube", "facet", None)),
        check_vma=False,
    )
```

time: 510 us -> 112 us (0.22)
  the two profiles are of different devices: /device:TPU:1 before, /device:TPU:32 now
where the time goes in v1:
time: 112 us; the launch traced here: 111 us
  blocking collectives  48.5 us (43%)
  starting transfers between devices  29.8 us (27%)
  Pallas kernels  9.71 us (9%)
  local copies, waits for them, and re-layouts  8.18 us (7%)
  waiting for transfers between devices  7.7 us (7%)
  other arithmetic  6.02 us (5%)
  between operations  1.56 us (1%)
    all_gather x1, blocking collectives, on_device(): squares = lax.all_gather((shifted * shifted).astype(jnp.bfloat16), 'cube')  20.6 us
    ppermute x3, starting transfers between devices, hop(): return lax.ppermute(block, 'facet', route)  20.5 us
    all_gather x1, blocking collectives, on_device(): dual_next = lax.all_gather(dual_part, 'dp', axis=2, tiled=True)  15.6 us
    all_gather x1, blocking collectives, on_device(): lax.all_gather(total[:, HALO:].astype(jnp.bfloat16), 'dp', axis=1, tiled=...  12.3 us
    pallas_call x2, Pallas kernels, facet_terms(): pl.pallas_call(functools.partial(facet_pass, base), out_shape=jax.ShapeDt...  9.71 us
    all_to_all x2, starting transfers between devices, gathered_sum(): mixed = lax.all_to_all(parts, 'dp', 0, 0)  9.25 us
    unnamed x35, local copies, waits for them, and re-layouts  7.12 us
    all_to_all x2, waiting for transfers between devices, gathered_sum(): mixed = lax.all_to_all(parts, 'dp', 0, 0)  5.76 us
  transfers between devices with their start and end apart: 5, of which 2 were waited for; matrix products, arithmetic and copies ran while one was open for 4% of the time, Pallas kernels for 9%

profile of v1, /device:TPU:32, one launch (start us, length us, event | category | flops | bytes accessed | tf_op | source)
XLA Modules:
  0.0 111.4 jit_solution(14424328404153710677)
XLA Ops:
  0.6 1.1 bitcast_convert_fusion.pixels_ref
  1.7 1.9 %collective-permute-start = (bf16[48,2560]{1,0:T(8,128)(2,1)S(1)}, bf16[48,2560]{1,0:T(8,128)(2,1)S(1)}, u32[]{:S(2)}, u32[]{:S(2)}) collective-permute-start(bf16[48,2560]{1,0:T(8,128)(2,1)S(1)} %bitcast_convert_fusion.pixels_ref), channel_id=1, source_target_pairs={{0,4},{4,8},{8,12},{12,16},{16,20},{20,24},{24,28},{28,32},{32,36}... | collective-permute-start | bytes 737288 | tf_op jit(solution)/shard_map/ppermute | solution.py:266
  3.6 0.8 copy.13
  5.1 0.2 broadcast_in_dim.16.weight_ref
  5.3 0.0 copy-start
  5.3 0.9 copy-done
  6.2 0.0 copy-start.2
  6.2 0.7 copy-done.2
  6.9 0.0 copy-start.4
  6.9 0.7 copy-done.4
  7.5 0.0 copy-start.6
  7.5 1.3 %copy-done.6 = bf16[20,128,256]{2,1,0:T(8,128)(2,1)S(1)} copy-done((bf16[20,128,256]{2,1,0:T(8,128)(2,1)S(1)}, bf16[20,128,256]{2,1,0:T(8,128)(2,1)}, u32[]{:S(2)}) %copy-start.6) | copy-done | bytes 1310744
  8.8 0.0 copy-start.8
  8.8 1.1 %copy-done.8 = bf16[640,640]{1,0:T(8,128)(2,1)S(1)} copy-done((bf16[640,640]{1,0:T(8,128)(2,1)S(1)}, bf16[640,640]{1,0:T(8,128)(2,1)}, u32[]{:S(2)}) %copy-start.8) | copy-done | bytes 819224
  10.0 0.0 copy-start.14
  10.0 4.9 %facet_terms_3.1 = bf16[4,48,768]{2,1,0:T(8,128)(2,1)} custom-call(s32[64]{0:T(128)S(1)} %bitcast.36, s32[64]{0:T(128)S(1)} %bitcast.38, s32[1]{0:T(128)} %bitcast.32.live_ref, bf16[48,2560]{1,0:T(8,128)(2,1)S(1)} %bitcast_convert_fusion.pixels_ref, bf16[64,16,128]{2,1,0:T(8,128)(2,1)S(1)} %bitcast.34, bf16[64,16,128]{2,1,0:T(8,128)(2,1)S(1)} %broadcast_in_dim.16.weight_ref, ...), custom_call_target="tpu_custom_call" | custom-call | flops 2000000000 | bytes 4000000 | tf_op jit(solution)/shard_map/facet_terms_3/pallas_call | solution.py:243
  14.8 4.3 %all-to-all-start = ((bf16[4,48,768]{2,1,0:T(8,128)(2,1)}), bf16[4,48,768]{2,1,0:T(8,128)(2,1)}, u32[]{:S(2)}, u32[]{:S(2)}) async-start(bf16[4,48,768]{2,1,0:T(8,128)(2,1)} %facet_terms_3.1), calls=%async_computation | async-start | bytes 589824 | tf_op jit(solution)/shard_map/all_to_all | solution.py:270
  19.1 0.0 copy-done.14
  19.2 0.0 copy-start.10
  19.3 0.6 fusion.37
  19.9 0.2 copy-done.10
  20.1 0.0 copy-start.12
  20.1 0.0 copy-start.1
  20.1 0.0 copy-start.3
  20.1 0.0 copy-start.7
  20.1 0.0 copy-start.9
  20.1 0.6 fusion.52
  20.7 0.4 copy-done.12
  21.1 0.3 fusion.16
  21.4 0.0 copy-start.15
  21.5 0.0 collective-permute-done.pixels_ref
  21.5 0.0 copy-done.1
  21.5 0.0 copy-done.3
  21.5 0.0 copy-done.5
  21.5 0.1 copy-done.7
  21.6 0.2 copy-done.9
  21.9 4.9 %facet_terms_0.1 = bf16[4,48,768]{2,1,0:T(8,128)(2,1)} custom-call(s32[64]{0:T(128)S(1)} %bitcast.37, s32[64]{0:T(128)S(1)} %bitcast.39, s32[1]{0:T(128)} %bitcast.33.live_ref, bf16[48,2560]{1,0:T(8,128)(2,1)S(1)} %collective-permute-done.pixels_ref, bf16[64,16,128]{2,1,0:T(8,128)(2,1)S(1)} %bitcast.35, ...), custom_call_target="tpu_custom_call" | custom-call | flops 2000000000 | bytes 4000000 | tf_op jit(solution)/shard_map/facet_terms_0/pallas_call | solution.py:243
  26.7 0.0 copy-done.15
  26.7 0.0 all-to-all-done
  26.7 0.0 copy-start.16
  26.7 4.9 %all-to-all-start.1 = ((bf16[4,48,768]{2,1,0:T(8,128)(2,1)}), bf16[4,48,768]{2,1,0:T(8,128)(2,1)S(1)}, u32[]{:S(2)}, u32[]{:S(2)}) async-start(bf16[4,48,768]{2,1,0:T(8,128)(2,1)} %facet_terms_0.1), calls=%async_computation.1 | async-start | bytes 589824 | tf_op jit(solution)/shard_map/all_to_all | solution.py:270
  31.7 1.1 convert_reduce_fusion.2
  32.8 5.8 %all-to-all-done.1 = bf16[4,48,768]{2,1,0:T(8,128)(2,1)S(1)} async-done(((bf16[4,48,768]{2,1,0:T(8,128)(2,1)}), bf16[4,48,768]{2,1,0:T(8,128)(2,1)S(1)}, u32[]{:S(2)}, u32[]{:S(2)}) %all-to-all-start.1) | async-done | bytes 294944 | tf_op jit(solution)/shard_map/all_to_all | solution.py:270
  38.6 0.0 slice-done
  38.6 11.9 %collective-permute-start.1 = (bf16[48,768]{1,0:T(8,128)(2,1)S(1)}, bf16[48,768]{1,0:T(8,128)(2,1)S(1)}, u32[]{:S(2)}, u32[]{:S(2)}) collective-permute-start(bf16[48,768]{1,0:T(8,128)(2,1)S(1)} %get-tuple-element.8), channel_id=1, source_target_pairs={{4,0},{8,4},{12,8},{16,12},{20,16},{24,20},{28,24},{32,28},{36,32}... | collective-permute-start | bytes 221192 | tf_op jit(solution)/shard_map/ppermute | solution.py:266
  50.5 1.9 %collective-permute-done.1 = bf16[48,768]{1,0:T(8,128)(2,1)S(1)} collective-permute-done((bf16[48,768]{1,0:T(8,128)(2,1)S(1)}, bf16[48,768]{1,0:T(8,128)(2,1)S(1)}, u32[]{:S(2)}, u32[]{:S(2)}) %collective-permute-start.1) | collective-permute-done | bytes 73760 | tf_op jit(solution)/shard_map/ppermute | solution.py:266
  52.5 0.0 copy-done.16
  52.5 6.7 %collective-permute-start.2 = (bf16[8,768]{1,0:T(8,128)(2,1)S(1)}, bf16[8,768]{1,0:T(8,128)(2,1)S(1)}, u32[]{:S(2)}, u32[]{:S(2)}) collective-permute-start(bf16[8,768]{1,0:T(8,128)(2,1)S(1)} %slice.775), channel_id=1, source_target_pairs={{0,4},{4,8},{8,12},{12,16},{16,20},{20,24},{24,28},{28,32},{32,36}... | collective-permute-start | bytes 36872 | tf_op jit(solution)/shard_map/ppermute | solution.py:266
  59.2 12.3 %all_gather.12 = bf16[48,2560]{1,0:T(8,128)(2,1)S(1)} all-gather(bf16[48,640]{1,0:T(8,128)(2,1)S(1)} %slice.774), channel_id=1, replica_groups=mesh['cube'=4,'facet'=32,'dp'=4] {'dp'}, dimensions={1}, use_global_device_ids=true | all-gather | bytes 307200 | tf_op jit(solution)/shard_map/all_gather | solution.py:342
  71.5 0.0 copy-done.13
  71.5 0.9 maximum_bitcast_fusion
  72.4 0.0 collective-permute-done.2
  72.4 0.1 fusion.36
  72.5 0.2 multiply_add_fusion.1
  72.7 0.0 copy-start.11
  72.7 0.3 add_bitcast_fusion.3
  73.0 0.3 add_bitcast_fusion.1
  73.3 0.5 copy-done.11
  73.8 0.1 multiply_convert_fusion.1
  73.9 20.6 %all-gather = bf16[16,48,640]{2,1,0:T(8,128)(2,1)S(1)} all-gather(bf16[4,48,640]{2,1,0:T(8,128)(2,1)S(1)} %multiply_convert_fusion.1), channel_id=2, replica_groups=mesh['cube'=4,'facet'=32,'dp'=4] {'cube'}, dimensions={0}, use_global_device_ids=true | all-gather | bytes 1228800 | tf_op jit(solution)/shard_map/all_gather | solution.py:338
  94.5 0.1 convert_reduce_fusion
  94.7 0.2 multiply_convert_fusion
  94.9 15.6 %all_gather.15 = bf16[4,48,2560]{2,1,0:T(8,128)(2,1)S(1)} all-gather(bf16[4,48,640]{2,1,0:T(8,128)(2,1)S(1)} %multiply_convert_fusion), channel_id=1, replica_groups=mesh['cube'=4,'facet'=32,'dp'=4] {'dp'}, dimensions={2}, use_global_device_ids=true | all-gather | bytes 1228800 | tf_op jit(solution)/shard_map/all_gather | solution.py:341
  110.5 0.9 copy.17
  (16 shorter events, 0.3 us)
Async XLA Ops:
  1.7 19.8 %collective-permute-start = (bf16[48,2560]{1,0:T(8,128)(2,1)S(1)}, bf16[48,2560]{1,0:T(8,128)(2,1)S(1)}, u32[]{:S(2)}, u32[]{:S(2)}) collective-permute-start(bf16[48,2560]{1,0:T(8,128)(2,1)S(1)} %bitcast_convert_fusion.pixels_ref), channel_id=1, source_target_pairs={{0,4},{4,8},{8,12},{12,16},{16,20},{20,24},{24,28},{28,32},{32,36}... | collective-permute-start | bytes 737288 | tf_op jit(solution)/shard_map/ppermute | solution.py:266
  5.3 1.0 copy-start
  6.2 0.7 copy-start.2
  6.9 0.7 copy-start.4
  7.5 1.3 %copy-start.6 = (bf16[20,128,256]{2,1,0:T(8,128)(2,1)S(1)}, bf16[20,128,256]{2,1,0:T(8,128)(2,1)}, u32[]{:S(2)}) copy-start(bf16[20,128,256]{2,1,0:T(8,128)(2,1)} %constant.54.clone.table_ref) | copy-start | bytes 3932164
  8.8 1.1 %copy-start.8 = (bf16[640,640]{1,0:T(8,128)(2,1)S(1)}, bf16[640,640]{1,0:T(8,128)(2,1)}, u32[]{:S(2)}) copy-start(bf16[640,640]{1,0:T(8,128)(2,1)} %constant.7.clone.order_ref) | copy-start | bytes 2457604
  10.0 9.2 %copy-start.14 = (bf16[4,1,48,2560]{3,2,1,0:T(8,128)(2,1)S(1)}, bf16[4,1,48,2560]{3,2,1,0:T(8,128)(2,1)}, u32[]{:S(2)}) copy-start(bf16[4,1,48,2560]{3,2,1,0:T(8,128)(2,1)} %param.10) | copy-start | bytes 2949124
  14.8 11.9 %all-to-all-start = ((bf16[4,48,768]{2,1,0:T(8,128)(2,1)}), bf16[4,48,768]{2,1,0:T(8,128)(2,1)}, u32[]{:S(2)}, u32[]{:S(2)}) async-start(bf16[4,48,768]{2,1,0:T(8,128)(2,1)} %facet_terms_3.1), calls=%async_computation | async-start | bytes 589824 | tf_op jit(solution)/shard_map/all_to_all | solution.py:270
  19.2 0.8 copy-start.10
  20.1 1.0 copy-start.12
  20.1 1.4 %copy-start.1 = (bf16[1,64,16,128]{3,2,1,0:T(8,128)(2,1)S(1)}, bf16[1,64,16,128]{3,2,1,0:T(8,128)(2,1)}, u32[]{:S(2)}) copy-start(bf16[1,64,16,128]{3,2,1,0:T(8,128)(2,1)} %param.11) | copy-start | bytes 786436
  20.1 1.4 %copy-start.3 = (s32[1,64]{1,0:T(1,128)S(1)}, s32[1,64]{1,0:T(1,128)}, u32[]{:S(2)}) copy-start(s32[1,64]{1,0:T(1,128)} %param.13) | copy-start | bytes 772
  20.1 1.4 %copy-start.5 = (s32[1,64]{1,0:T(1,128)S(1)}, s32[1,64]{1,0:T(1,128)}, u32[]{:S(2)}) copy-start(s32[1,64]{1,0:T(1,128)} %param.14) | copy-start | bytes 772
  20.1 1.6 %copy-start.7 = (bf16[20,128,256]{2,1,0:T(8,128)(2,1)S(1)}, bf16[20,128,256]{2,1,0:T(8,128)(2,1)}, u32[]{:S(2)}) copy-start(bf16[20,128,256]{2,1,0:T(8,128)(2,1)} %constant.54.clone.table_ref) | copy-start | bytes 3932164
  20.1 1.8 %copy-start.9 = (bf16[640,640]{1,0:T(8,128)(2,1)S(1)}, bf16[640,640]{1,0:T(8,128)(2,1)}, u32[]{:S(2)}) copy-start(bf16[640,640]{1,0:T(8,128)(2,1)} %constant.7.clone.order_ref) | copy-start | bytes 2457604
  21.4 5.3 %copy-start.15 = (f32[56,768]{1,0:T(8,128)}, f32[56,768]{1,0:T(8,128)S(1)}, u32[]{:S(2)}) copy-start(f32[56,768]{1,0:T(8,128)S(1)} %fusion.16) | copy-start | bytes 516100
  26.7 11.9 %slice-start = ((f32[56,768]{1,0:T(8,128)}), f32[8,768]{1,0:T(8,128)S(1)}, s32[]{:S(2)}) async-start(f32[56,768]{1,0:T(8,128)} %copy-done.15), calls=%async_computation.2 | async-start | bytes 49152 | tf_op jit(solution)/shard_map/slice | solution.py:322
  26.7 25.8 %copy-start.16 = (f32[56,768]{1,0:T(8,128)S(1)}, f32[56,768]{1,0:T(8,128)}, u32[]{:S(2)}) copy-start(f32[56,768]{1,0:T(8,128)} %copy-done.15) | copy-start | bytes 516100
  26.7 11.8 %all-to-all-start.1 = ((bf16[4,48,768]{2,1,0:T(8,128)(2,1)}), bf16[4,48,768]{2,1,0:T(8,128)(2,1)S(1)}, u32[]{:S(2)}, u32[]{:S(2)}) async-start(bf16[4,48,768]{2,1,0:T(8,128)(2,1)} %facet_terms_0.1), calls=%async_computation.1 | async-start | bytes 589824 | tf_op jit(solution)/shard_map/all_to_all | solution.py:270
  31.7 39.9 %copy-start.13 = (f32[1,48,2560]{2,1,0:T(8,128)S(1)}, f32[1,48,2560]{2,1,0:T(8,128)}, u32[]{:S(2)}) copy-start(f32[1,48,2560]{2,1,0:T(8,128)} %param.9) | copy-start | bytes 1474564
  38.6 13.9 %collective-permute-start.1 = (bf16[48,768]{1,0:T(8,128)(2,1)S(1)}, bf16[48,768]{1,0:T(8,128)(2,1)S(1)}, u32[]{:S(2)}, u32[]{:S(2)}) collective-permute-start(bf16[48,768]{1,0:T(8,128)(2,1)S(1)} %get-tuple-element.8), channel_id=1, source_target_pairs={{4,0},{8,4},{12,8},{16,12},{20,16},{24,20},{28,24},{32,28},{36,32}... | collective-permute-start | bytes 221192 | tf_op jit(solution)/shard_map/ppermute | solution.py:266
  52.5 19.9 %collective-permute-start.2 = (bf16[8,768]{1,0:T(8,128)(2,1)S(1)}, bf16[8,768]{1,0:T(8,128)(2,1)S(1)}, u32[]{:S(2)}, u32[]{:S(2)}) collective-permute-start(bf16[8,768]{1,0:T(8,128)(2,1)S(1)} %slice.775), channel_id=1, source_target_pairs={{0,4},{4,8},{8,12},{12,16},{16,20},{20,24},{24,28},{28,32},{32,36}... | collective-permute-start | bytes 36872 | tf_op jit(solution)/shard_map/ppermute | solution.py:266
  72.7 1.1 copy-start.11

commit v2 on v1

--- a/solution.py
+++ b/solution.py
@@ -55,10 +55,7 @@
     x = np.arange(W).reshape(R, Q).T
     angles = (x[:, :, None] * np.arange(R)[None, None, :] % W) * (2.0 * math.pi / W)
     table = np.concatenate([np.cos(angles), -np.sin(angles)], -1).astype(jnp.bfloat16)
-    y = np.arange(PART)
-    order = np.zeros((PART, PART), np.float32)
-    order[y, (y % Q) * 32 + y // Q] = 1.0
-    return table, order.astype(jnp.bfloat16)
+    return table
 
 
 def times_i(value, sign):
@@ -100,41 +97,62 @@
     return out
 
 
+def residue_order():
+    y = lax.broadcasted_iota(jnp.int32, (PART, 128), 0)
+    group = ((y.astype(jnp.float32) + 0.5) * (1.0 / Q)).astype(jnp.int32)
+    target = (y - Q * group) * 32 + group
+    lane = lax.broadcasted_iota(jnp.int32, (PART, 128), 1)
+    tiles = [jnp.where(target == lane + 128 * j, 1.0, 0.0) for j in range(PART // 128)]
+    return jnp.concatenate(tiles, 1).astype(jnp.bfloat16)
+
+
 def facet_pass(
     base,
+    starts_hbm,
+    slots_hbm,
+    live_hbm,
+    weight_hbm,
+    payload_hbm,
+    table_hbm,
+    pixels_ref,
+    out_ref,
     starts_ref,
     slots_ref,
     live_ref,
-    pixels_ref,
+    list_ref,
+    weight_ref,
     payload_ref,
-    weight_ref,
     table_ref,
     order_ref,
-    out_ref,
     re_ref,
     im_ref,
     spec_ref,
     grad_ref,
-    list_ref,
+    sems,
 ):
+    pairs = [
+        (table_hbm, table_ref),
+        (starts_hbm, starts_ref),
+        (slots_hbm, slots_ref),
+        (live_hbm, live_ref),
+        (weight_hbm, weight_ref),
+        (payload_hbm, payload_ref),
+    ]
+    copies = [pltpu.make_async_copy(s, d, sems.at[i]) for i, (s, d) in enumerate(pairs)]
+    for copy in copies:
+        copy.start()
+
     lane = lax.broadcasted_iota(jnp.int32, (1, 128), 1)
     low = lane < 64
-    half = lane % 64
-    quarter = lane // 32
-
-    def collect(b, count):
-        slot = slots_ref[b] - base
-        list_ref[count] = b
-        return count + jnp.where((slot >= 0) & (slot < PER), 1, 0)
-
-    count = lax.fori_loop(0, live_ref[0], collect, 0)
-    for u in range(UNROLL):
-        list_ref[count + u] = list_ref[0]
-
+    half = lane & 63
+    quarter = lane >> 5
+
+    order_ref[...] = residue_order()
     stacked = jnp.concatenate(
         [pixels_ref[:, PART * g : PART * (g + 1)] for g in range(4)], 0
     )
     sorted_rows = jnp.dot(stacked, order_ref[...], preferred_element_type=jnp.float32)
+    copies[0].wait()
     for j in range(5):
         tiles = [sorted_rows[FR * g : FR * (g + 1), 128 * j : 128 * (j + 1)] for g in range(4)]
         for p in range(4):
@@ -164,22 +182,44 @@
     lax.fori_loop(0, FR // 8, forward, 0)
     spec_ref[CHUNKS] = spec_ref[0]
     grad_ref[...] = jnp.zeros_like(grad_ref)
+    for copy in copies[1:]:
+        copy.wait()
+
+    def collect(b, count):
+        slot = slots_ref[0, b] - base
+        list_ref[count] = b
+        return count + jnp.where((slot >= 0) & (slot < PER), 1, 0)
+
+    count = lax.fori_loop(0, live_ref[0, 0], collect, 0)
+    for u in range(UNROLL):
+        list_ref[count + u] = list_ref[0]
+    weights = weight_ref[...].astype(jnp.float32)
+    slot_lane = lax.broadcasted_iota(jnp.int32, (1, BLK), 1)
+    ones = jnp.ones((BLK, 128), jnp.bfloat16)
 
     def blocks(step, carry):
+        places = [step * UNROLL + u for u in range(UNROLL)]
+        numbers = [list_ref[place] for place in places]
+        picked = [
+            jnp.where(slot_lane == jnp.where(place < count, b, -1), weights, 0.0)
+            for place, b in zip(places, numbers)
+        ]
+        factors = jnp.dot(
+            jnp.concatenate(picked, 0).astype(jnp.bfloat16), ones, preferred_element_type=jnp.float32
+        )
         found = []
-        for u in range(UNROLL):
-            place = step * UNROLL + u
-            b = list_ref[place]
-            start = starts_ref[b]
-            slot = jnp.clip(slots_ref[b] - base, 0, PER - 1)
-            chunk = start // 64
-            offset = start % 64
+        for u, b in enumerate(numbers):
+            start = starts_ref[0, b]
+            slot = jnp.clip(slots_ref[0, b] - base, 0, PER - 1)
+            chunk = start >> 6
+            offset = start & 63
             rows = pl.ds(pl.multiple_of(slot * TILE, TILE), TILE)
-            first = pltpu.roll(spec_ref[chunk, rows, :], (128 - offset) % 128, 1)
+            first = pltpu.roll(spec_ref[chunk, rows, :], (128 - offset) & 127, 1)
             second = pltpu.roll(spec_ref[chunk + 1, rows, :], 64 - offset, 1)
             model = jnp.where(half < 64 - offset, first, second)
-            factor = weight_ref[b].astype(jnp.float32) * jnp.where(place < count, 1.0, 0.0)
-            misfit = factor * (model - payload_ref[b].astype(jnp.float32))
+            misfit = factors[TILE * u : TILE * (u + 1)] * (
+                model - payload_ref[b].astype(jnp.float32)
+            )
             lower = jnp.where(half >= offset, pltpu.roll(misfit, offset, 1), 0.0)
             upper = jnp.where(half < offset, pltpu.roll(misfit, 64 + offset, 1), 0.0)
             found.append((chunk, rows, lower, upper))
@@ -237,27 +277,35 @@
             out_ref[g + 1, :, :HALO] = rows[:, PART - HALO :]
 
 
-def facet_terms(base, pixels, payload, weights, starts, slots, live, table, order):
-    smem = pl.BlockSpec(memory_space=pltpu.SMEM)
+def facet_terms(base, pixels, starts, slots, live, weights, payload, table):
+    hbm = pl.BlockSpec(memory_space=pltpu.HBM)
     vmem = pl.BlockSpec(memory_space=pltpu.VMEM)
     return pl.pallas_call(
         functools.partial(facet_pass, base),
         out_shape=jax.ShapeDtypeStruct((DP, FR, SPAN), jnp.bfloat16),
-        in_specs=[smem] * 3 + [vmem] * 5,
+        in_specs=[hbm] * 6 + [vmem],
         out_specs=vmem,
         scratch_shapes=[
+            pltpu.SMEM((1, BLK), jnp.int32),
+            pltpu.SMEM((1, BLK), jnp.int32),
+            pltpu.SMEM((1, 1), jnp.int32),
+            pltpu.SMEM((BLK + UNROLL,), jnp.int32),
+            pltpu.VMEM((TILE, BLK), jnp.bfloat16),
+            pltpu.VMEM((BLK, TILE, 128), jnp.bfloat16),
+            pltpu.VMEM((Q, R, 2 * R), jnp.bfloat16),
+            pltpu.VMEM((PART, PART), jnp.bfloat16),
             pltpu.VMEM((Q, FR, R), jnp.float32),
             pltpu.VMEM((Q, FR, R), jnp.float32),
             pltpu.VMEM((CHUNKS + 1, FR, 128), jnp.float32),
             pltpu.VMEM((CHUNKS + 1, FR, 128), jnp.float32),
-            pltpu.SMEM((BLK + UNROLL,), jnp.int32),
+            pltpu.SemaphoreType.DMA((6,)),
         ],
         compiler_params=pltpu.CompilerParams(vmem_limit_bytes=32 * 1024 * 1024),
         cost_estimate=pl.CostEstimate(
             flops=2 * 10**9, bytes_accessed=4 * 10**6, transcendentals=0
         ),
         name=f"facet_terms_{base}",
-    )(starts, slots, live, pixels, payload, weights, table, order)
+    )(starts, slots, live, weights, payload, table, pixels)
 
 
 def hop(block, distance):
@@ -296,15 +344,13 @@
 
 
 def on_device(image, dual, payload, vis_weight, freq_start, tile_slot, live):
-    table, order = tables()
-    table, order = jnp.asarray(table), jnp.asarray(order)
+    table = jnp.asarray(tables())
     position = lax.axis_index("dp")
     facet = lax.axis_index("facet")
     own_rows = image[0]
     pixels = own_rows.astype(jnp.bfloat16)
     rows_above = hop(pixels, 1)
-    weights = jnp.broadcast_to(vis_weight[0][:, :, None], payload.shape[1:])
-    blocks = (payload[0], weights, freq_start[0], tile_slot[0], live[0], table, order)
+    blocks = (freq_start, tile_slot, live, vis_weight[0].T, payload[0], table)
 
     left = position * PART
     own_dual = lax.dynamic_slice_in_dim(
@@ -317,10 +363,13 @@
 
     own_terms = facet_terms(PER, pixels, *blocks)
     own_sum = gathered_sum(own_terms) + synth[8:]
-    last_rows = hop(own_sum[FR - 8 :].astype(jnp.bfloat16), 1)
     upper_terms = facet_terms(0, rows_above, *blocks)
     upper_sum = gathered_sum(upper_terms) + jnp.pad(synth[:8], ((FR - 8, 0), (0, 0)))
-    from_below = hop(upper_sum.astype(jnp.bfloat16), -1)
+    sent_up, sent_down = lax.optimization_barrier(
+        (upper_sum.astype(jnp.bfloat16), own_sum[FR - 8 :].astype(jnp.bfloat16))
+    )
+    from_below = hop(sent_up, -1)
+    last_rows = hop(sent_down, 1)
 
     total = own_sum + from_below.astype(jnp.float32)
     above = last_rows.astype(jnp.float32) + upper_sum[FR - 8 :]
@@ -338,9 +387,11 @@
     squares = lax.all_gather((shifted * shifted).astype(jnp.bfloat16), "cube")
     norms = jnp.sqrt(jnp.sum(squares.astype(jnp.float32), 0))
     dual_part = (shifted * (RADIUS / jnp.maximum(norms, RADIUS))).astype(jnp.bfloat16)
-    dual_next = lax.all_gather(dual_part, "dp", axis=2, tiled=True)
-    descent = lax.all_gather(total[:, HALO:].astype(jnp.bfloat16), "dp", axis=1, tiled=True)
-    updated = jnp.maximum(own_rows - TAU_STEP * descent.astype(jnp.float32), 0.0)
+    own_part = jnp.concatenate([dual_part, total[None, :, HALO:].astype(jnp.bfloat16)], 0)
+    parts = lax.all_to_all(jnp.broadcast_to(own_part, (DP,) + own_part.shape), "dp", 0, 0)
+    whole = jnp.concatenate([parts[d] for d in range(DP)], -1)
+    dual_next = whole[:4]
+    updated = jnp.maximum(own_rows - TAU_STEP * whole[4].astype(jnp.float32), 0.0)
     return (updated[None], dual_next[:, None])
 
 

time: 112 us -> 105 us (0.938)
  the two profiles are of different devices: /device:TPU:32 before, /device:TPU:17 now
where the time goes in v2:
time: 105 us; the launch traced here: 104 us
  blocking collectives  38.3 us (36%)
  starting transfers between devices  26.5 us (25%)
  waiting for transfers between devices  14.4 us (14%)
  Pallas kernels  9.41 us (9%)
  other arithmetic  8.81 us (8%)
  local copies, waits for them, and re-layouts  5.26 us (5%)
  between operations  1.62 us (2%)
    all_gather x1, blocking collectives, on_device(): squares = lax.all_gather((shifted * shifted).astype(jnp.bfloat16), 'cube')  20.6 us
    ppermute x3, starting transfers between devices, hop(): return lax.ppermute(block, 'facet', route)  18.6 us
    all_to_all x1, blocking collectives, on_device(): lax.all_to_all(jnp.broadcast_to(own_part, (DP,) + own_part.shape), 'dp',...  17.7 us
    pallas_call x2, Pallas kernels, facet_terms(): pl.pallas_call(functools.partial(facet_pass, base), out_shape=jax.ShapeDt...  9.41 us
    all_to_all x2, starting transfers between devices, gathered_sum(): mixed = lax.all_to_all(parts, 'dp', 0, 0)  7.93 us
    ppermute x3, waiting for transfers between devices, hop(): return lax.ppermute(block, 'facet', route)  7.64 us
    all_to_all x2, waiting for transfers between devices, gathered_sum(): mixed = lax.all_to_all(parts, 'dp', 0, 0)  6.79 us
    unnamed x30, local copies, waits for them, and re-layouts  4.31 us
  transfers between devices with their start and end apart: 5, of which 3 were waited for; matrix products, arithmetic and copies ran while one was open for 5% of the time, Pallas kernels for 5%

profile of v2, /device:TPU:17, one launch (start us, length us, event | category | flops | bytes accessed | tf_op | source)
XLA Modules:
  0.0 104.3 jit_solution(8776489014038016374)
XLA Ops:
  0.6 1.1 %bitcast_convert_fusion.pixels_ref = bf16[48,2560]{1,0:T(8,128)(2,1)S(1)} fusion(f32[1,48,2560]{2,1,0:T(8,128)} %param.8), kind=kLoop, calls=%fused_computation.157 | loop fusion | flops 122880 | bytes 737280 | tf_op jit(solution)/shard_map/convert_element_type | solution.py:351
  1.7 11.2 %collective-permute-start = (bf16[48,2560]{1,0:T(8,128)(2,1)S(1)}, bf16[48,2560]{1,0:T(8,128)(2,1)S(1)}, u32[]{:S(2)}, u32[]{:S(2)}) collective-permute-start(bf16[48,2560]{1,0:T(8,128)(2,1)S(1)} %bitcast_convert_fusion.pixels_ref), channel_id=1, source_target_pairs={{0,4},{4,8},{8,12},{12,16},{16,20},{20,24},{24,28},{28,32},{32,36}... | collective-permute-start | bytes 737288 | tf_op jit(solution)/shard_map/ppermute | solution.py:314
  13.5 0.0 copy-start
  13.6 0.9 copy-done
  14.5 0.0 copy-start.2
  14.5 0.7 copy-done.2
  15.2 0.7 copy-done.4
  15.8 0.0 copy-start.6
  15.8 0.7 copy-done.6
  16.5 0.0 copy-start.8
  16.5 1.3 %copy-done.8 = bf16[20,128,256]{2,1,0:T(8,128)(2,1)S(1)} copy-done((bf16[20,128,256]{2,1,0:T(8,128)(2,1)S(1)}, bf16[20,128,256]{2,1,0:T(8,128)(2,1)}, u32[]{:S(2)}) %copy-start.8) | copy-done | bytes 1310744
  17.8 0.0 copy-start.11
  17.8 4.8 %facet_terms_3.1 = bf16[4,48,768]{2,1,0:T(8,128)(2,1)} custom-call(s32[1,64]{1,0:T(1,128)S(1)} %copy-done.4, s32[1,64]{1,0:T(1,128)S(1)} %copy-done.6, s32[1,1]{1,0:T(1,128)S(6)} %copy.10.live_hbm, bf16[16,64]{1,0:T(8,128)(2,1)S(1)} %bitcast.39, bf16[64,16,128]{2,1,0:T(8,128)(2,1)S(1)} %bitcast.37, bf16[20,128,256]{2,1,0:T(8,128)(2,1)S(1)} %copy-done.8, ...), custom_call_target="tpu_custom_call" | custom-call | flops 2000000000 | bytes 4000000 | tf_op jit(solution)/shard_map/facet_terms_3/pallas_call | solution.py:283
  22.6 4.3 %all-to-all-start.1 = ((bf16[4,48,768]{2,1,0:T(8,128)(2,1)}), bf16[4,48,768]{2,1,0:T(8,128)(2,1)S(1)}, u32[]{:S(2)}, u32[]{:S(2)}) async-start(bf16[4,48,768]{2,1,0:T(8,128)(2,1)} %facet_terms_3.1), calls=%async_computation.1 | async-start | bytes 589824 | tf_op jit(solution)/shard_map/all_to_all | solution.py:318
  27.0 0.0 copy-done.11
  27.0 0.1 fusion.1
  27.1 0.6 fusion.38
  27.7 0.0 copy-start.10
  27.7 0.6 fusion.53
  28.3 0.0 copy-start.1
  28.3 0.0 copy-start.3
  28.3 0.0 copy-start.5
  28.4 0.0 copy-start.7
  28.4 0.0 copy-start.9
  28.4 1.0 fusion.17
  29.4 0.5 compare_or_fusion
  29.9 0.0 copy-done.10
  29.9 0.7 pad_dynamic-slice_fusion.1
  30.6 2.1 %all-to-all-done.1 = bf16[4,48,768]{2,1,0:T(8,128)(2,1)S(1)} async-done(((bf16[4,48,768]{2,1,0:T(8,128)(2,1)}), bf16[4,48,768]{2,1,0:T(8,128)(2,1)S(1)}, u32[]{:S(2)}, u32[]{:S(2)}) %all-to-all-start.1) | async-done | bytes 294944 | tf_op jit(solution)/shard_map/all_to_all | solution.py:318
  32.7 0.7 convert_reduce_fusion.1
  33.4 0.0 collective-permute-done.pixels_ref
  33.4 0.0 copy-done.1
  33.4 0.0 copy-done.3
  33.4 0.0 copy-done.5
  33.4 0.0 copy-done.7
  33.4 0.0 copy-done.9
  33.4 4.6 %facet_terms_0.1 = bf16[4,48,768]{2,1,0:T(8,128)(2,1)} custom-call(s32[1,64]{1,0:T(1,128)S(1)} %copy-done.5, s32[1,64]{1,0:T(1,128)S(1)} %copy-done.7, s32[1,1]{1,0:T(1,128)S(6)} %copy.10.live_hbm, bf16[16,64]{1,0:T(8,128)(2,1)S(1)} %bitcast.40, bf16[64,16,128]{2,1,0:T(8,128)(2,1)S(1)} %bitcast.38, bf16[20,128,256]{2,1,0:T(8,128)(2,1)S(1)} %copy-done.9, ...), custom_call_target="tpu_custom_call" | custom-call | flops 2000000000 | bytes 4000000 | tf_op jit(solution)/shard_map/facet_terms_0/pallas_call | solution.py:283
  38.0 0.0 slice-start
  38.0 0.0 copy-start.13
  38.0 0.0 copy-start.14
  38.0 3.6 %all-to-all-start = ((bf16[4,48,768]{2,1,0:T(8,128)(2,1)}), bf16[4,48,768]{2,1,0:T(8,128)(2,1)S(1)}, u32[]{:S(2)}, u32[]{:S(2)}) async-start(bf16[4,48,768]{2,1,0:T(8,128)(2,1)} %facet_terms_0.1), calls=%async_computation | async-start | bytes 589824 | tf_op jit(solution)/shard_map/all_to_all | solution.py:318
  41.6 0.0 copy-done.12
  41.7 0.9 slice_add_fusion.1
  42.6 4.7 %all-to-all-done = bf16[4,48,768]{2,1,0:T(8,128)(2,1)S(1)} async-done(((bf16[4,48,768]{2,1,0:T(8,128)(2,1)}), bf16[4,48,768]{2,1,0:T(8,128)(2,1)S(1)}, u32[]{:S(2)}, u32[]{:S(2)}) %all-to-all-start) | async-done | bytes 294944 | tf_op jit(solution)/shard_map/all_to_all | solution.py:318
  47.4 0.0 slice-done
  47.4 5.4 %collective-permute-start.1 = (bf16[8,768]{1,0:T(8,128)(2,1)S(1)}, bf16[8,768]{1,0:T(8,128)(2,1)S(1)}, u32[]{:S(2)}, u32[]{:S(2)}) collective-permute-start(bf16[8,768]{1,0:T(8,128)(2,1)S(1)} %slice.808), channel_id=1, source_target_pairs={{0,4},{4,8},{8,12},{12,16},{16,20},{20,24},{24,28},{28,32},{32,36}... | collective-permute-start | bytes 36872 | tf_op jit(solution)/shard_map/ppermute | solution.py:314
  52.9 1.9 %collective-permute-start.2 = (bf16[48,768]{1,0:T(8,128)(2,1)S(1)}, bf16[48,768]{1,0:T(8,128)(2,1)S(1)}, u32[]{:S(2)}, u32[]{:S(2)}) collective-permute-start(bf16[48,768]{1,0:T(8,128)(2,1)S(1)} %get-tuple-element.5), channel_id=1, source_target_pairs={{4,0},{8,4},{12,8},{16,12},{20,16},{24,20},{28,24},{32,28},{36,32}... | collective-permute-start | bytes 221192 | tf_op jit(solution)/shard_map/ppermute | solution.py:314
  54.8 0.0 collective-permute-done.1
  54.8 7.6 %collective-permute-done.2 = bf16[48,768]{1,0:T(8,128)(2,1)S(1)} collective-permute-done((bf16[48,768]{1,0:T(8,128)(2,1)S(1)}, bf16[48,768]{1,0:T(8,128)(2,1)S(1)}, u32[]{:S(2)}, u32[]{:S(2)}) %collective-permute-start.2) | collective-permute-done | bytes 73760 | tf_op jit(solution)/shard_map/ppermute | solution.py:314
  62.5 0.0 copy-done.13
  62.5 0.0 copy-done.14
  62.5 0.1 fusion.37
  62.6 0.2 multiply_add_fusion.1
  62.8 0.3 add_bitcast_fusion.3
  63.1 0.3 add_bitcast_fusion.1
  63.4 0.1 multiply_convert_fusion.1
  63.5 20.6 %all-gather = bf16[16,48,640]{2,1,0:T(8,128)(2,1)S(1)} all-gather(bf16[4,48,640]{2,1,0:T(8,128)(2,1)S(1)} %multiply_convert_fusion.1), channel_id=2, replica_groups=mesh['cube'=4,'facet'=32,'dp'=4] {'cube'}, dimensions={0}, use_global_device_ids=true | all-gather | bytes 1228800 | tf_op jit(solution)/shard_map/all_gather | solution.py:387
  84.2 0.1 convert_reduce_fusion
  84.3 0.2 multiply_convert_fusion
  84.6 0.1 broadcast_in_dim.10
  84.7 17.7 %all_to_all.15 = bf16[4,5,48,640]{3,2,1,0:T(8,128)(2,1)S(1)} all-to-all(bf16[4,5,48,640]{3,2,1,0:T(8,128)(2,1)S(1)} %broadcast_in_dim.10), channel_id=1, replica_groups=mesh['cube'=4,'facet'=32,'dp'=4] {'dp'}, dimensions={0} | all-to-all | bytes 2457600 | tf_op jit(solution)/shard_map/all_to_all | solution.py:391
  102.4 0.1 slice_bitcast_fusion.3
  102.5 0.9 subtract_maximum_fusion
  103.3 1.0 fusion
  (13 shorter events, 0.2 us)
Async XLA Ops:
  1.7 31.7 %collective-permute-start = (bf16[48,2560]{1,0:T(8,128)(2,1)S(1)}, bf16[48,2560]{1,0:T(8,128)(2,1)S(1)}, u32[]{:S(2)}, u32[]{:S(2)}) collective-permute-start(bf16[48,2560]{1,0:T(8,128)(2,1)S(1)} %bitcast_convert_fusion.pixels_ref), channel_id=1, source_target_pairs={{0,4},{4,8},{8,12},{12,16},{16,20},{20,24},{24,28},{28,32},{32,36}... | collective-permute-start | bytes 737288 | tf_op jit(solution)/shard_map/ppermute | solution.py:314
  13.5 1.0 copy-start
  14.5 0.7 copy-start.2
  15.2 0.7 copy-start.4
  15.8 0.7 copy-start.6
  16.5 1.3 %copy-start.8 = (bf16[20,128,256]{2,1,0:T(8,128)(2,1)S(1)}, bf16[20,128,256]{2,1,0:T(8,128)(2,1)}, u32[]{:S(2)}) copy-start(bf16[20,128,256]{2,1,0:T(8,128)(2,1)} %constant.53.clone.table_hbm) | copy-start | bytes 3932164
  17.8 9.2 %copy-start.11 = (bf16[4,1,48,2560]{3,2,1,0:T(8,128)(2,1)S(1)}, bf16[4,1,48,2560]{3,2,1,0:T(8,128)(2,1)}, u32[]{:S(2)}) copy-start(bf16[4,1,48,2560]{3,2,1,0:T(8,128)(2,1)} %param.9) | copy-start | bytes 2949124
  22.6 10.0 %all-to-all-start.1 = ((bf16[4,48,768]{2,1,0:T(8,128)(2,1)}), bf16[4,48,768]{2,1,0:T(8,128)(2,1)S(1)}, u32[]{:S(2)}, u32[]{:S(2)}) async-start(bf16[4,48,768]{2,1,0:T(8,128)(2,1)} %facet_terms_3.1), calls=%async_computation.1 | async-start | bytes 589824 | tf_op jit(solution)/shard_map/all_to_all | solution.py:318
  27.7 2.2 %copy-start.10 = (f32[1,48,2560]{2,1,0:T(8,128)S(1)}, f32[1,48,2560]{2,1,0:T(8,128)}, u32[]{:S(2)}) copy-start(f32[1,48,2560]{2,1,0:T(8,128)} %param.8) | copy-start | bytes 1474564
  28.3 5.1 %copy-start.1 = (bf16[1,64,16,128]{3,2,1,0:T(8,128)(2,1)S(1)}, bf16[1,64,16,128]{3,2,1,0:T(8,128)(2,1)}, u32[]{:S(2)}) copy-start(bf16[1,64,16,128]{3,2,1,0:T(8,128)(2,1)} %param.10) | copy-start | bytes 786436
  28.3 5.0 %copy-start.3 = (bf16[1,64,16]{1,2,0:T(8,128)(2,1)S(1)}, bf16[1,64,16]{1,2,0:T(8,128)(2,1)}, u32[]{:S(2)}) copy-start(bf16[1,64,16]{1,2,0:T(8,128)(2,1)} %param.11) | copy-start | bytes 6148
  28.3 5.0 %copy-start.5 = (s32[1,64]{1,0:T(1,128)S(1)}, s32[1,64]{1,0:T(1,128)}, u32[]{:S(2)}) copy-start(s32[1,64]{1,0:T(1,128)} %starts_hbm.3) | copy-start | bytes 772
  28.4 5.0 %copy-start.7 = (s32[1,64]{1,0:T(1,128)S(1)}, s32[1,64]{1,0:T(1,128)}, u32[]{:S(2)}) copy-start(s32[1,64]{1,0:T(1,128)} %slots_hbm.3) | copy-start | bytes 772
  28.4 5.0 %copy-start.9 = (bf16[20,128,256]{2,1,0:T(8,128)(2,1)S(1)}, bf16[20,128,256]{2,1,0:T(8,128)(2,1)}, u32[]{:S(2)}) copy-start(bf16[20,128,256]{2,1,0:T(8,128)(2,1)} %constant.53.clone.table_hbm) | copy-start | bytes 3932164
  33.4 8.3 %copy-start.12 = (f32[56,768]{1,0:T(8,128)S(1)}, f32[56,768]{1,0:T(8,128)}, u32[]{:S(2)}) copy-start(f32[56,768]{1,0:T(8,128)} %fusion.17) | copy-start | bytes 516100
  38.0 9.3 %slice-start = ((f32[56,768]{1,0:T(8,128)}), f32[8,768]{1,0:T(8,128)S(1)}, s32[]{:S(2)}) async-start(f32[56,768]{1,0:T(8,128)} %fusion.17), calls=%async_computation.3 | async-start | bytes 49152 | tf_op jit(solution)/shard_map/slice | solution.py:367
  38.0 24.5 %copy-start.13 = (f32[48,768]{1,0:T(8,128)S(1)}, f32[48,768]{1,0:T(8,128)}, u32[]{:S(2)}) copy-start(f32[48,768]{1,0:T(8,128)} %pad_dynamic-slice_fusion.1) | copy-start | bytes 442372
  38.0 24.5 %copy-start.14 = (pred[56]{0:T(512)(128)(4,1)S(1)}, pred[56]{0:T(512)(128)(4,1)}, u32[]{:S(2)}) copy-start(pred[56]{0:T(512)(128)(4,1)} %compare_or_fusion) | copy-start | bytes 172
  38.0 9.3 %all-to-all-start = ((bf16[4,48,768]{2,1,0:T(8,128)(2,1)}), bf16[4,48,768]{2,1,0:T(8,128)(2,1)S(1)}, u32[]{:S(2)}, u32[]{:S(2)}) async-start(bf16[4,48,768]{2,1,0:T(8,128)(2,1)} %facet_terms_0.1), calls=%async_computation | async-start | bytes 589824 | tf_op jit(solution)/shard_map/all_to_all | solution.py:318
  47.4 7.4 %collective-permute-start.1 = (bf16[8,768]{1,0:T(8,128)(2,1)S(1)}, bf16[8,768]{1,0:T(8,128)(2,1)S(1)}, u32[]{:S(2)}, u32[]{:S(2)}) collective-permute-start(bf16[8,768]{1,0:T(8,128)(2,1)S(1)} %slice.808), channel_id=1, source_target_pairs={{0,4},{4,8},{8,12},{12,16},{16,20},{20,24},{24,28},{28,32},{32,36}... | collective-permute-start | bytes 36872 | tf_op jit(solution)/shard_map/ppermute | solution.py:314
  52.9 9.6 %collective-permute-start.2 = (bf16[48,768]{1,0:T(8,128)(2,1)S(1)}, bf16[48,768]{1,0:T(8,128)(2,1)S(1)}, u32[]{:S(2)}, u32[]{:S(2)}) collective-permute-start(bf16[48,768]{1,0:T(8,128)(2,1)S(1)} %get-tuple-element.5), channel_id=1, source_target_pairs={{4,0},{8,4},{12,8},{16,12},{20,16},{24,20},{28,24},{32,28},{36,32}... | collective-permute-start | bytes 221192 | tf_op jit(solution)/shard_map/ppermute | solution.py:314

commit v3 on v2

--- a/solution.py
+++ b/solution.py
@@ -46,6 +46,7 @@
 SPAN = PART + HALO
 CHUNKS = W // 64
 UNROLL = 4
+VMEM_LIMIT = 62 * 1024 * 1024
 NORM = 1.0 / math.sqrt(W)
 C1, C2 = math.cos(2 * math.pi / 5), math.cos(4 * math.pi / 5)
 S1, S2 = math.sin(2 * math.pi / 5), math.sin(4 * math.pi / 5)
@@ -115,21 +116,26 @@
     payload_hbm,
     table_hbm,
     pixels_ref,
-    out_ref,
-    starts_ref,
-    slots_ref,
-    live_ref,
-    list_ref,
-    weight_ref,
-    payload_ref,
-    table_ref,
-    order_ref,
-    re_ref,
-    im_ref,
-    spec_ref,
-    grad_ref,
-    sems,
+    *refs,
 ):
+    if base == 0:
+        below_ref, refs = refs[0], refs[1:]
+    (
+        out_ref,
+        starts_ref,
+        slots_ref,
+        live_ref,
+        list_ref,
+        weight_ref,
+        payload_ref,
+        table_ref,
+        order_ref,
+        re_ref,
+        im_ref,
+        spec_ref,
+        grad_ref,
+        sems,
+    ) = refs
     pairs = [
         (table_hbm, table_ref),
         (starts_hbm, starts_ref),
@@ -269,21 +275,23 @@
     natural = lax.dot_general(
         mixed, order_ref[...], (((1,), (1,)), ((), ())), preferred_element_type=jnp.float32
     ).astype(jnp.bfloat16)
-    out_ref[0, :, :HALO] = jnp.zeros((FR, HALO), jnp.bfloat16)
+    out_ref[0, :FR, :HALO] = jnp.zeros((FR, HALO), jnp.bfloat16)
     for g in range(4):
         rows = natural[FR * g : FR * (g + 1)]
-        out_ref[g, :, HALO:] = rows
+        out_ref[g, :FR, HALO:] = rows
         if g < 3:
-            out_ref[g + 1, :, :HALO] = rows[:, PART - HALO :]
-
-
-def facet_terms(base, pixels, starts, slots, live, weights, payload, table):
+            out_ref[g + 1, :FR, :HALO] = rows[:, PART - HALO :]
+        if base == 0:
+            out_ref[g, FR:, :] = below_ref[g]
+
+
+def facet_terms(base, pixels, starts, slots, live, weights, payload, table, *below):
     hbm = pl.BlockSpec(memory_space=pltpu.HBM)
     vmem = pl.BlockSpec(memory_space=pltpu.VMEM)
     return pl.pallas_call(
         functools.partial(facet_pass, base),
-        out_shape=jax.ShapeDtypeStruct((DP, FR, SPAN), jnp.bfloat16),
-        in_specs=[hbm] * 6 + [vmem],
+        out_shape=jax.ShapeDtypeStruct((DP, FR * (1 + len(below)), SPAN), jnp.bfloat16),
+        in_specs=[hbm] * 6 + [vmem] * (1 + len(below)),
         out_specs=vmem,
         scratch_shapes=[
             pltpu.SMEM((1, BLK), jnp.int32),
@@ -300,12 +308,12 @@
             pltpu.VMEM((CHUNKS + 1, FR, 128), jnp.float32),
             pltpu.SemaphoreType.DMA((6,)),
         ],
-        compiler_params=pltpu.CompilerParams(vmem_limit_bytes=32 * 1024 * 1024),
+        compiler_params=pltpu.CompilerParams(vmem_limit_bytes=VMEM_LIMIT),
         cost_estimate=pl.CostEstimate(
             flops=2 * 10**9, bytes_accessed=4 * 10**6, transcendentals=0
         ),
         name=f"facet_terms_{base}",
-    )(starts, slots, live, weights, payload, table, pixels)
+    )(starts, slots, live, weights, payload, table, pixels, *below)
 
 
 def hop(block, distance):
@@ -362,9 +370,10 @@
     synth = synthesize(own_dual)
 
     own_terms = facet_terms(PER, pixels, *blocks)
-    own_sum = gathered_sum(own_terms) + synth[8:]
-    upper_terms = facet_terms(0, rows_above, *blocks)
-    upper_sum = gathered_sum(upper_terms) + jnp.pad(synth[:8], ((FR - 8, 0), (0, 0)))
+    terms = facet_terms(0, rows_above, *blocks, own_terms)
+    sums = gathered_sum(terms)
+    upper_sum = sums[:FR] + jnp.pad(synth[:8], ((FR - 8, 0), (0, 0)))
+    own_sum = sums[FR:] + synth[8:]
     sent_up, sent_down = lax.optimization_barrier(
         (upper_sum.astype(jnp.bfloat16), own_sum[FR - 8 :].astype(jnp.bfloat16))
     )

time: 105 us -> 100 us (0.952)
  the two profiles are of different devices: /device:TPU:17 before, /device:TPU:49 now
where the time goes in v3:
time: 100 us; the launch traced here: 99.6 us
  blocking collectives  38.6 us (39%)
  starting transfers between devices  23.6 us (24%)
  waiting for transfers between devices  14.5 us (14%)
  Pallas kernels  13.4 us (13%)
  other arithmetic  7.01 us (7%)
  between operations  1.55 us (2%)
    all_gather x1, blocking collectives, on_device(): squares = lax.all_gather((shifted * shifted).astype(jnp.bfloat16), 'cube')  19.8 us
    all_to_all x1, blocking collectives, on_device(): lax.all_to_all(jnp.broadcast_to(own_part, (DP,) + own_part.shape), 'dp',...  18.8 us
    ppermute x3, starting transfers between devices, hop(): return lax.ppermute(block, 'facet', route)  17 us
    pallas_call x2, Pallas kernels, facet_terms(): pl.pallas_call(functools.partial(facet_pass, base), out_shape=jax.ShapeDt...  13.4 us
    ppermute x3, waiting for transfers between devices, hop(): return lax.ppermute(block, 'facet', route)  7.63 us
    all_to_all x1, waiting for transfers between devices, gathered_sum(): mixed = lax.all_to_all(parts, 'dp', 0, 0)  6.87 us
    all_to_all x1, starting transfers between devices, gathered_sum(): mixed = lax.all_to_all(parts, 'dp', 0, 0)  6.61 us
  transfers between devices with their start and end apart: 4, of which 2 were waited for; matrix products, arithmetic and copies ran while one was open for 3% of the time, Pallas kernels for 7%

profile of v3, /device:TPU:49, one launch (start us, length us, event | category | flops | bytes accessed | tf_op | source)
XLA Modules:
  0.0 99.6 jit_solution(12614778520238434994)
XLA Ops:
  0.6 1.1 %bitcast_convert_fusion.pixels_ref = bf16[48,2560]{1,0:T(8,128)(2,1)S(1)} fusion(f32[1,48,2560]{2,1,0:T(8,128)} %param.8), kind=kLoop, calls=%fused_computation.156 | loop fusion | flops 122880 | bytes 737280 | tf_op jit(solution)/shard_map/convert_element_type | solution.py:359
  1.7 0.0 copy-start.1
  1.7 11.2 %collective-permute-start = (bf16[48,2560]{1,0:T(8,128)(2,1)S(1)}, bf16[48,2560]{1,0:T(8,128)(2,1)S(1)}, u32[]{:S(2)}, u32[]{:S(2)}) collective-permute-start(bf16[48,2560]{1,0:T(8,128)(2,1)S(1)} %bitcast_convert_fusion.pixels_ref), channel_id=1, source_target_pairs={{0,4},{4,8},{8,12},{12,16},{16,20},{20,24},{24,28},{28,32},{32,36}... | collective-permute-start | bytes 737288 | tf_op jit(solution)/shard_map/ppermute | solution.py:322
  13.6 1.0 %fusion.1 = f32[4,48,896]{2,1,0:T(8,128)S(1)} fusion(s32[]{:T(128)S(6)} %select_n.11, bf16[4,48,2560]{2,1,0:T(8,128)(2,1)} %bitcast.39), kind=kLoop, calls=%fused_computation.13 | loop fusion | flops 172032 | bytes 1671172 | tf_op jit(solution)/shard_map/convert_element_type | solution.py:366
  14.6 0.0 copy-done.1
  14.6 0.6 fusion.38
  15.3 6.7 %facet_terms_3.1.refs_0_ = bf16[4,48,768]{2,1,0:T(8,128)(2,1)} custom-call(s32[1,64]{1,0:T(1,128)} %starts_hbm.3, s32[1,64]{1,0:T(1,128)} %slots_hbm.3, s32[1,1]{1,0:T(1,128)S(6)} %copy.10.live_hbm, bf16[16,64]{1,0:T(8,128)(2,1)} %bitcast.42, bf16[64,16,128]{2,1,0:T(8,128)(2,1)} %bitcast.40, bf16[20,128,256]{2,1,0:T(8,128)(2,1)} %constant.53.clone.table_hbm, ...), custom_call_target="tpu_custom_call" | custom-call | flops 2000000000 | bytes 4000000 | tf_op jit(solution)/shard_map/facet_terms_3/pallas_call | solution.py:291
  21.9 0.6 fusion.53
  22.5 0.0 collective-permute-done.pixels_ref
  22.6 0.0 copy-start.2
  22.6 0.7 copy-done.2
  23.2 6.7 %facet_terms_0.1 = bf16[4,96,768]{2,1,0:T(8,128)(2,1)} custom-call(s32[1,64]{1,0:T(1,128)} %starts_hbm.3, s32[1,64]{1,0:T(1,128)} %slots_hbm.3, s32[1,1]{1,0:T(1,128)S(6)} %copy.10.live_hbm, bf16[16,64]{1,0:T(8,128)(2,1)} %bitcast.43, bf16[64,16,128]{2,1,0:T(8,128)(2,1)} %bitcast.41, bf16[20,128,256]{2,1,0:T(8,128)(2,1)} %constant.53.clone.table_hbm, ...), custom_call_target="tpu_custom_call" | custom-call | flops 2000000000 | bytes 4000000 | tf_op jit(solution)/shard_map/facet_terms_0/pallas_call | solution.py:291
  30.0 0.0 copy-start
  30.0 6.6 %all-to-all-start = ((bf16[4,96,768]{2,1,0:T(8,128)(2,1)}), bf16[4,96,768]{2,1,0:T(8,128)(2,1)S(1)}, u32[]{:S(2)}, u32[]{:S(2)}) async-start(bf16[4,96,768]{2,1,0:T(8,128)(2,1)} %facet_terms_0.1), calls=%async_computation | async-start | bytes 1179648 | tf_op jit(solution)/shard_map/all_to_all | solution.py:326
  36.6 0.3 fusion.17
  36.9 0.0 slice-start
  37.0 0.0 copy-done
  37.0 6.9 %all-to-all-done = bf16[4,96,768]{2,1,0:T(8,128)(2,1)S(1)} async-done(((bf16[4,96,768]{2,1,0:T(8,128)(2,1)}), bf16[4,96,768]{2,1,0:T(8,128)(2,1)S(1)}, u32[]{:S(2)}, u32[]{:S(2)}) %all-to-all-start) | async-done | bytes 589856 | tf_op jit(solution)/shard_map/all_to_all | solution.py:326
  43.9 0.1 convert_reduce_fusion.1
  44.0 3.9 %collective-permute-start.1 = (bf16[8,768]{1,0:T(8,128)(2,1)S(1)}, bf16[8,768]{1,0:T(8,128)(2,1)S(1)}, u32[]{:S(2)}, u32[]{:S(2)}) collective-permute-start(bf16[8,768]{1,0:T(8,128)(2,1)S(1)} %slice.820), channel_id=1, source_target_pairs={{0,4},{4,8},{8,12},{12,16},{16,20},{20,24},{24,28},{28,32},{32,36}... | collective-permute-start | bytes 36872 | tf_op jit(solution)/shard_map/ppermute | solution.py:322
  47.9 0.0 slice-done
  47.9 1.9 %collective-permute-start.2 = (bf16[48,768]{1,0:T(8,128)(2,1)S(1)}, bf16[48,768]{1,0:T(8,128)(2,1)S(1)}, u32[]{:S(2)}, u32[]{:S(2)}) collective-permute-start(bf16[48,768]{1,0:T(8,128)(2,1)S(1)} %get-tuple-element.5), channel_id=1, source_target_pairs={{4,0},{8,4},{12,8},{16,12},{20,16},{24,20},{28,24},{32,28},{36,32}... | collective-permute-start | bytes 221192 | tf_op jit(solution)/shard_map/ppermute | solution.py:322
  49.9 0.0 collective-permute-done.1
  49.9 7.6 %collective-permute-done.2 = bf16[48,768]{1,0:T(8,128)(2,1)S(1)} collective-permute-done((bf16[48,768]{1,0:T(8,128)(2,1)S(1)}, bf16[48,768]{1,0:T(8,128)(2,1)S(1)}, u32[]{:S(2)}, u32[]{:S(2)}) %collective-permute-start.2) | collective-permute-done | bytes 73760 | tf_op jit(solution)/shard_map/ppermute | solution.py:322
  57.5 0.1 fusion.37
  57.6 0.2 multiply_add_fusion.1
  57.9 0.3 add_bitcast_fusion.3
  58.2 0.3 add_bitcast_fusion.1
  58.5 0.1 multiply_convert_fusion.1
  58.5 19.8 %all-gather = bf16[16,48,640]{2,1,0:T(8,128)(2,1)S(1)} all-gather(bf16[4,48,640]{2,1,0:T(8,128)(2,1)S(1)} %multiply_convert_fusion.1), channel_id=2, replica_groups=mesh['cube'=4,'facet'=32,'dp'=4] {'cube'}, dimensions={0}, use_global_device_ids=true | all-gather | bytes 1228800 | tf_op jit(solution)/shard_map/all_gather | solution.py:396
  78.3 0.1 convert_reduce_fusion
  78.5 0.2 multiply_convert_fusion
  78.8 0.1 broadcast_in_dim.10
  78.9 18.8 %all_to_all.10 = bf16[4,5,48,640]{3,2,1,0:T(8,128)(2,1)S(1)} all-to-all(bf16[4,5,48,640]{3,2,1,0:T(8,128)(2,1)S(1)} %broadcast_in_dim.10), channel_id=1, replica_groups=mesh['cube'=4,'facet'=32,'dp'=4] {'dp'}, dimensions={0} | all-to-all | bytes 2457600 | tf_op jit(solution)/shard_map/all_to_all | solution.py:400
  97.7 0.1 slice_bitcast_fusion.3
  97.8 0.8 subtract_maximum_fusion
  98.6 1.0 %fusion = bf16[4,1,48,2560]{3,2,1,0:T(8,128)(2,1)} fusion(bf16[5,48,640]{2,1,0:T(8,128)(2,1)S(1)} %get-tuple-element.9, bf16[5,48,640]{2,1,0:T(8,128)(2,1)S(1)} %get-tuple-element.10, bf16[5,48,640]{2,1,0:T(8,128)(2,1)S(1)} %get-tuple-element.11, bf16[5,48,640]{2,1,0:T(8,128)(2,1)S(1)} %get-tuple-element.8), kind=kLoop, calls=%fused_computation.4 | loop fusion | flops 3932160 | bytes 2211840 | tf_op jit(solution)/shard_map/broadcast_in_dim | solution.py:404
  (12 shorter events, 0.2 us)
Async XLA Ops:
  1.7 12.9 %copy-start.1 = (bf16[48,2560]{1,0:T(8,128)(2,1)}, bf16[48,2560]{1,0:T(8,128)(2,1)S(1)}, u32[]{:S(2)}) copy-start(bf16[48,2560]{1,0:T(8,128)(2,1)S(1)} %bitcast_convert_fusion.pixels_ref) | copy-start | bytes 737284
  1.7 20.8 %collective-permute-start = (bf16[48,2560]{1,0:T(8,128)(2,1)S(1)}, bf16[48,2560]{1,0:T(8,128)(2,1)S(1)}, u32[]{:S(2)}, u32[]{:S(2)}) collective-permute-start(bf16[48,2560]{1,0:T(8,128)(2,1)S(1)} %bitcast_convert_fusion.pixels_ref), channel_id=1, source_target_pairs={{0,4},{4,8},{8,12},{12,16},{16,20},{20,24},{24,28},{28,32},{32,36}... | collective-permute-start | bytes 737288 | tf_op jit(solution)/shard_map/ppermute | solution.py:322
  22.6 0.7 copy-start.2
  30.0 7.0 %copy-start = (f32[1,48,2560]{2,1,0:T(8,128)S(1)}, f32[1,48,2560]{2,1,0:T(8,128)}, u32[]{:S(2)}) copy-start(f32[1,48,2560]{2,1,0:T(8,128)} %param.8) | copy-start | bytes 1474564
  30.0 13.9 %all-to-all-start = ((bf16[4,96,768]{2,1,0:T(8,128)(2,1)}), bf16[4,96,768]{2,1,0:T(8,128)(2,1)S(1)}, u32[]{:S(2)}, u32[]{:S(2)}) async-start(bf16[4,96,768]{2,1,0:T(8,128)(2,1)} %facet_terms_0.1), calls=%async_computation | async-start | bytes 1179648 | tf_op jit(solution)/shard_map/all_to_all | solution.py:326
  36.9 11.0 %slice-start = ((bf16[48,2560]{1,0:T(8,128)(2,1)}), bf16[8,2560]{1,0:T(8,128)(2,1)S(1)}, s32[]{:S(2)}) async-start(bf16[48,2560]{1,0:T(8,128)(2,1)} %copy-done.2), calls=%async_computation.2 | async-start | bytes 81920 | tf_op jit(solution)/shard_map/slice | solution.py:386
  44.0 5.9 %collective-permute-start.1 = (bf16[8,768]{1,0:T(8,128)(2,1)S(1)}, bf16[8,768]{1,0:T(8,128)(2,1)S(1)}, u32[]{:S(2)}, u32[]{:S(2)}) collective-permute-start(bf16[8,768]{1,0:T(8,128)(2,1)S(1)} %slice.820), channel_id=1, source_target_pairs={{0,4},{4,8},{8,12},{12,16},{16,20},{20,24},{24,28},{28,32},{32,36}... | collective-permute-start | bytes 36872 | tf_op jit(solution)/shard_map/ppermute | solution.py:322
  47.9 9.6 %collective-permute-start.2 = (bf16[48,768]{1,0:T(8,128)(2,1)S(1)}, bf16[48,768]{1,0:T(8,128)(2,1)S(1)}, u32[]{:S(2)}, u32[]{:S(2)}) collective-permute-start(bf16[48,768]{1,0:T(8,128)(2,1)S(1)} %get-tuple-element.5), channel_id=1, source_target_pairs={{4,0},{8,4},{12,8},{16,12},{20,16},{24,20},{28,24},{32,28},{36,32}... | collective-permute-start | bytes 221192 | tf_op jit(solution)/shard_map/ppermute | solution.py:322

commit v4 on v1

--- a/solution.py
+++ b/solution.py
@@ -46,6 +46,7 @@
 SPAN = PART + HALO
 CHUNKS = W // 64
 UNROLL = 4
+VMEM_LIMIT = 24 * 1024 * 1024
 NORM = 1.0 / math.sqrt(W)
 C1, C2 = math.cos(2 * math.pi / 5), math.cos(4 * math.pi / 5)
 S1, S2 = math.sin(2 * math.pi / 5), math.sin(4 * math.pi / 5)
@@ -55,10 +56,7 @@
     x = np.arange(W).reshape(R, Q).T
     angles = (x[:, :, None] * np.arange(R)[None, None, :] % W) * (2.0 * math.pi / W)
     table = np.concatenate([np.cos(angles), -np.sin(angles)], -1).astype(jnp.bfloat16)
-    y = np.arange(PART)
-    order = np.zeros((PART, PART), np.float32)
-    order[y, (y % Q) * 32 + y // Q] = 1.0
-    return table, order.astype(jnp.bfloat16)
+    return table
 
 
 def times_i(value, sign):
@@ -100,37 +98,83 @@
     return out
 
 
-def facet_pass(
-    base,
-    starts_ref,
-    slots_ref,
-    live_ref,
+def residue_order():
+    y = lax.broadcasted_iota(jnp.int32, (PART, 128), 0)
+    group = ((y.astype(jnp.float32) + 0.5) * (1.0 / Q)).astype(jnp.int32)
+    target = (y - Q * group) * 32 + group
+    lane = lax.broadcasted_iota(jnp.int32, (PART, 128), 1)
+    tiles = [jnp.where(target == lane + 128 * j, 1.0, 0.0) for j in range(PART // 128)]
+    return jnp.concatenate(tiles, 1).astype(jnp.bfloat16)
+
+
+def add_blocks(base, numbers_ref, weight_ref, payload_ref, spec_ref, grad_ref, list_ref):
+    lane = lax.broadcasted_iota(jnp.int32, (1, 128), 1)
+    half = lane & 63
+
+    def collect(b, count):
+        slot = numbers_ref[1, b] - base
+        list_ref[count] = b
+        return count + jnp.where((slot >= 0) & (slot < PER), 1, 0)
+
+    count = lax.fori_loop(0, numbers_ref[2, 0], collect, 0)
+    for u in range(UNROLL):
+        list_ref[count + u] = list_ref[0]
+    weights = weight_ref[...]
+    slot_lane = lax.broadcasted_iota(jnp.int32, (1, BLK), 1)
+    ones = jnp.ones((BLK, 128), jnp.bfloat16)
+
+    def blocks(step, carry):
+        places = [step * UNROLL + u for u in range(UNROLL)]
+        numbers = [list_ref[place] for place in places]
+        picked = [
+            jnp.where(slot_lane == jnp.where(place < count, b, -1), weights, 0.0)
+            for place, b in zip(places, numbers)
+        ]
+        factors = jnp.dot(
+            jnp.concatenate(picked, 0).astype(jnp.bfloat16), ones, preferred_element_type=jnp.float32
+        )
+        found = []
+        for u, b in enumerate(numbers):
+            start = numbers_ref[0, b]
+            slot = jnp.clip(numbers_ref[1, b] - base, 0, PER - 1)
+            chunk = start >> 6
+            offset = start & 63
+            rows = pl.ds(pl.multiple_of(slot * TILE, TILE), TILE)
+            first = pltpu.roll(spec_ref[chunk, rows, :], (128 - offset) & 127, 1)
+            second = pltpu.roll(spec_ref[chunk + 1, rows, :], 64 - offset, 1)
+            model = jnp.where(half < 64 - offset, first, second)
+            misfit = factors[TILE * u : TILE * (u + 1)] * (
+                model - payload_ref[b].astype(jnp.float32)
+            )
+            lower = jnp.where(half >= offset, pltpu.roll(misfit, offset, 1), 0.0)
+            upper = jnp.where(half < offset, pltpu.roll(misfit, 64 + offset, 1), 0.0)
+            found.append((chunk, rows, lower, upper))
+        for chunk, rows, lower, upper in found:
+            grad_ref[chunk, rows, :] += lower
+            grad_ref[chunk + 1, rows, :] += upper
+        return carry
+
+    lax.fori_loop(0, (count + UNROLL - 1) // UNROLL, blocks, 0)
+
+
+def own_pass(
+    numbers_ref,
+    weight_ref,
+    payload_ref,
+    table_ref,
     pixels_ref,
-    payload_ref,
-    weight_ref,
-    table_ref,
+    spec_ref,
+    grad_ref,
     order_ref,
-    out_ref,
+    list_ref,
     re_ref,
     im_ref,
-    spec_ref,
-    grad_ref,
-    list_ref,
 ):
     lane = lax.broadcasted_iota(jnp.int32, (1, 128), 1)
     low = lane < 64
-    half = lane % 64
-    quarter = lane // 32
-
-    def collect(b, count):
-        slot = slots_ref[b] - base
-        list_ref[count] = b
-        return count + jnp.where((slot >= 0) & (slot < PER), 1, 0)
-
-    count = lax.fori_loop(0, live_ref[0], collect, 0)
-    for u in range(UNROLL):
-        list_ref[count + u] = list_ref[0]
-
+    quarter = lane >> 5
+
+    order_ref[...] = residue_order()
     stacked = jnp.concatenate(
         [pixels_ref[:, PART * g : PART * (g + 1)] for g in range(4)], 0
     )
@@ -164,31 +208,29 @@
     lax.fori_loop(0, FR // 8, forward, 0)
     spec_ref[CHUNKS] = spec_ref[0]
     grad_ref[...] = jnp.zeros_like(grad_ref)
-
-    def blocks(step, carry):
-        found = []
-        for u in range(UNROLL):
-            place = step * UNROLL + u
-            b = list_ref[place]
-            start = starts_ref[b]
-            slot = jnp.clip(slots_ref[b] - base, 0, PER - 1)
-            chunk = start // 64
-            offset = start % 64
-            rows = pl.ds(pl.multiple_of(slot * TILE, TILE), TILE)
-            first = pltpu.roll(spec_ref[chunk, rows, :], (128 - offset) % 128, 1)
-            second = pltpu.roll(spec_ref[chunk + 1, rows, :], 64 - offset, 1)
-            model = jnp.where(half < 64 - offset, first, second)
-            factor = weight_ref[b].astype(jnp.float32) * jnp.where(place < count, 1.0, 0.0)
-            misfit = factor * (model - payload_ref[b].astype(jnp.float32))
-            lower = jnp.where(half >= offset, pltpu.roll(misfit, offset, 1), 0.0)
-            upper = jnp.where(half < offset, pltpu.roll(misfit, 64 + offset, 1), 0.0)
-            found.append((chunk, rows, lower, upper))
-        for chunk, rows, lower, upper in found:
-            grad_ref[chunk, rows, :] += lower
-            grad_ref[chunk + 1, rows, :] += upper
-        return carry
-
-    lax.fori_loop(0, (count + UNROLL - 1) // UNROLL, blocks, 0)
+    add_blocks(PER, numbers_ref, weight_ref, payload_ref, spec_ref, grad_ref, list_ref)
+
+
+def below_pass(
+    numbers_ref,
+    weight_ref,
+    payload_ref,
+    spec_ref,
+    own_ref,
+    table_ref,
+    order_ref,
+    out_ref,
+    list_ref,
+    re_ref,
+    im_ref,
+    grad_ref,
+    tile_ref,
+):
+    lane = lax.broadcasted_iota(jnp.int32, (1, 128), 1)
+    low = lane < 64
+    quarter = lane >> 5
+    grad_ref[...] = own_ref[...]
+    add_blocks(0, numbers_ref, weight_ref, payload_ref, spec_ref, grad_ref, list_ref)
     grad_ref[0] += grad_ref[CHUNKS]
 
     def backward(i, carry):
@@ -222,9 +264,9 @@
             tile = places[g][3]
             for p in range(3):
                 tile = jnp.where(quarter == p, places[g][p], tile)
-            spec_ref[5 * g + j] = tile
+            tile_ref[5 * g + j] = tile
     mixed = jnp.concatenate(
-        [jnp.concatenate([spec_ref[5 * g + j] for j in range(5)], 1) for g in range(4)], 0
+        [jnp.concatenate([tile_ref[5 * g + j] for j in range(5)], 1) for g in range(4)], 0
     ).astype(jnp.bfloat16)
     natural = lax.dot_general(
         mixed, order_ref[...], (((1,), (1,)), ((), ())), preferred_element_type=jnp.float32
@@ -237,27 +279,49 @@
             out_ref[g + 1, :, :HALO] = rows[:, PART - HALO :]
 
 
-def facet_terms(base, pixels, payload, weights, starts, slots, live, table, order):
-    smem = pl.BlockSpec(memory_space=pltpu.SMEM)
-    vmem = pl.BlockSpec(memory_space=pltpu.VMEM)
+SMEM_SPEC = pl.BlockSpec(memory_space=pltpu.SMEM)
+VMEM_SPEC = pl.BlockSpec(memory_space=pltpu.VMEM)
+SPECTRA = jax.ShapeDtypeStruct((CHUNKS + 1, FR, 128), jnp.float32)
+
+
+def own_spectra(numbers, weights, payload, table, pixels):
     return pl.pallas_call(
-        functools.partial(facet_pass, base),
+        own_pass,
+        out_shape=(SPECTRA, SPECTRA, jax.ShapeDtypeStruct((PART, PART), jnp.bfloat16)),
+        in_specs=[SMEM_SPEC] + [VMEM_SPEC] * 4,
+        out_specs=(VMEM_SPEC,) * 3,
+        scratch_shapes=[
+            pltpu.SMEM((BLK + UNROLL,), jnp.int32),
+            pltpu.VMEM((Q, FR, R), jnp.float32),
+            pltpu.VMEM((Q, FR, R), jnp.float32),
+        ],
+        compiler_params=pltpu.CompilerParams(vmem_limit_bytes=VMEM_LIMIT),
+        cost_estimate=pl.CostEstimate(
+            flops=2 * 10**9, bytes_accessed=4 * 10**6, transcendentals=0
+        ),
+        name="own_spectra",
+    )(numbers, weights, payload, table, pixels)
+
+
+def gradient_parts(numbers, weights, payload, spectra, own, table, order):
+    return pl.pallas_call(
+        below_pass,
         out_shape=jax.ShapeDtypeStruct((DP, FR, SPAN), jnp.bfloat16),
-        in_specs=[smem] * 3 + [vmem] * 5,
-        out_specs=vmem,
+        in_specs=[SMEM_SPEC] + [VMEM_SPEC] * 6,
+        out_specs=VMEM_SPEC,
         scratch_shapes=[
+            pltpu.SMEM((BLK + UNROLL,), jnp.int32),
             pltpu.VMEM((Q, FR, R), jnp.float32),
             pltpu.VMEM((Q, FR, R), jnp.float32),
             pltpu.VMEM((CHUNKS + 1, FR, 128), jnp.float32),
-            pltpu.VMEM((CHUNKS + 1, FR, 128), jnp.float32),
-            pltpu.SMEM((BLK + UNROLL,), jnp.int32),
+            pltpu.VMEM((Q, FR, R), jnp.float32),
         ],
-        compiler_params=pltpu.CompilerParams(vmem_limit_bytes=32 * 1024 * 1024),
+        compiler_params=pltpu.CompilerParams(vmem_limit_bytes=VMEM_LIMIT),
         cost_estimate=pl.CostEstimate(
             flops=2 * 10**9, bytes_accessed=4 * 10**6, transcendentals=0
         ),
-        name=f"facet_terms_{base}",
-    )(starts, slots, live, pixels, payload, weights, table, order)
+        name="gradient_parts",
+    )(numbers, weights, payload, spectra, own, table, order)
 
 
 def hop(block, distance):
@@ -296,51 +360,61 @@
 
 
 def on_device(image, dual, payload, vis_weight, freq_start, tile_slot, live):
-    table, order = tables()
-    table, order = jnp.asarray(table), jnp.asarray(order)
+    table = jnp.asarray(tables())
     position = lax.axis_index("dp")
-    facet = lax.axis_index("facet")
     own_rows = image[0]
-    pixels = own_rows.astype(jnp.bfloat16)
-    rows_above = hop(pixels, 1)
-    weights = jnp.broadcast_to(vis_weight[0][:, :, None], payload.shape[1:])
-    blocks = (payload[0], weights, freq_start[0], tile_slot[0], live[0], table, order)
+    payload_below = hop(payload[0], -1)
+    meta = jnp.concatenate(
+        [
+            vis_weight[0].T.astype(jnp.float32),
+            freq_start.astype(jnp.float32),
+            tile_slot.astype(jnp.float32),
+            jnp.broadcast_to(live, (1, BLK)).astype(jnp.float32),
+        ],
+        0,
+    )
+    meta_below = hop(meta, -1)
+    numbers = jnp.concatenate([freq_start, tile_slot, jnp.broadcast_to(live, (1, BLK))], 0)
 
     left = position * PART
     own_dual = lax.dynamic_slice_in_dim(
         jnp.pad(dual[:, 0], ((0, 0), (0, 0), (HALO, 128))), left, SPAN + 128, 2
     ).astype(jnp.float32)
-    own_image = lax.dynamic_slice_in_dim(
+    old = lax.dynamic_slice_in_dim(
         jnp.pad(own_rows, ((0, 0), (HALO, 0))), left, SPAN, 1
     )
     synth = synthesize(own_dual)
-
-    own_terms = facet_terms(PER, pixels, *blocks)
-    own_sum = gathered_sum(own_terms) + synth[8:]
-    last_rows = hop(own_sum[FR - 8 :].astype(jnp.bfloat16), 1)
-    upper_terms = facet_terms(0, rows_above, *blocks)
-    upper_sum = gathered_sum(upper_terms) + jnp.pad(synth[:8], ((FR - 8, 0), (0, 0)))
-    from_below = hop(upper_sum.astype(jnp.bfloat16), -1)
-
-    total = own_sum + from_below.astype(jnp.float32)
-    above = last_rows.astype(jnp.float32) + upper_sum[FR - 8 :]
-    image_above = lax.dynamic_slice_in_dim(
-        jnp.pad(rows_above[FR - 8 :], ((0, 0), (HALO, 0))), left, SPAN, 1
-    ).astype(jnp.float32)
-    old = jnp.concatenate([image_above, own_image], 0)
-    new = jnp.maximum(old - TAU_STEP * jnp.concatenate([above, total], 0), 0.0)
+    synth_below = hop(synth[:8], -1)
+
+    spectra, own, order = own_spectra(
+        numbers, meta[:TILE], payload[0], table, own_rows.astype(jnp.bfloat16)
+    )
+    terms = gradient_parts(
+        meta_below[TILE:].astype(jnp.int32),
+        meta_below[:TILE],
+        payload_below,
+        spectra,
+        own,
+        table,
+        order,
+    )
+    synth = synth[8:] + jnp.pad(synth_below, ((FR - 8, 0), (0, 0)))
+    total = gathered_sum(terms) + synth
+    new = jnp.maximum(old - TAU_STEP * total, 0.0)
     column = lax.broadcasted_iota(jnp.int32, old.shape, 1) + left
-    row = lax.broadcasted_iota(jnp.int32, old.shape, 0)
-    inside = (column >= HALO) & ((row >= 8) | (facet > 0))
-    extra = jnp.where(inside, 2.0 * new - old, 0.0)
+    extra = jnp.where(column >= HALO, 2.0 * new - old, 0.0)
+    extra_above = hop(extra[FR - 8 :].astype(jnp.bfloat16), 1).astype(jnp.float32)
+    extra = jnp.concatenate([extra_above, extra], 0)
 
     shifted = own_dual[:, :, HALO : HALO + PART] + SIGMA_STEP * analyze(extra)
     squares = lax.all_gather((shifted * shifted).astype(jnp.bfloat16), "cube")
     norms = jnp.sqrt(jnp.sum(squares.astype(jnp.float32), 0))
     dual_part = (shifted * (RADIUS / jnp.maximum(norms, RADIUS))).astype(jnp.bfloat16)
-    dual_next = lax.all_gather(dual_part, "dp", axis=2, tiled=True)
-    descent = lax.all_gather(total[:, HALO:].astype(jnp.bfloat16), "dp", axis=1, tiled=True)
-    updated = jnp.maximum(own_rows - TAU_STEP * descent.astype(jnp.float32), 0.0)
+    own_part = jnp.concatenate([dual_part, total[None, :, HALO:].astype(jnp.bfloat16)], 0)
+    parts = lax.all_to_all(jnp.broadcast_to(own_part, (DP,) + own_part.shape), "dp", 0, 0)
+    whole = jnp.concatenate([parts[d] for d in range(DP)], -1)
+    dual_next = whole[:4]
+    updated = jnp.maximum(own_rows - TAU_STEP * whole[4].astype(jnp.float32), 0.0)
     return (updated[None], dual_next[:, None])
 
 

time: 112 us -> 92.2 us (0.82)
  blocking collectives: 48.5 us -> 32.6 us
  local copies, waits for them, and re-layouts: 8.18 us -> 1.21 us
  other arithmetic: 6.02 us -> 9.74 us
  Pallas kernels: 9.71 us -> 6.51 us
  waiting for transfers between devices: 7.7 us -> 10.6 us
    all_gather x2 -> x0, blocking collectives: 27.8 us -> none  [the longest x1 15.6 us: on_device(): dual_next = lax.all_gather(dual_part, 'dp', axis=2, tiled=True)]
    all_to_all x0 -> x1, blocking collectives: none -> 16.2 us  [on_device(): lax.all_to_all(jnp.broadcast_to(own_part, (DP,) + own_part.shape), 'dp',...]
    ppermute x3 -> x4, waiting for transfers between devices: 1.94 us -> 10.6 us  [hop(): return lax.ppermute(block, 'facet', route)]
    unnamed x35 -> x6, local copies, waits for them, and re-layouts: 7.12 us -> 0.8 us
    all_to_all x2 -> x1, waiting for transfers between devices: 5.76 us -> 0.01 us  [gathered_sum(): mixed = lax.all_to_all(parts, 'dp', 0, 0)]
    all_gather x1, blocking collectives: 20.6 us -> 16.5 us  [on_device(): squares = lax.all_gather((shifted * shifted).astype(jnp.bfloat16), 'cube')]
    pallas_call x2, Pallas kernels: 9.71 us -> 6.51 us  [the longest x1 3.46 us: gradient_parts(): pl.pallas_call(below_pass, out_shape=jax.ShapeDtypeStruct((DP, FR, SPAN),...]
    all_to_all x2 -> x1, starting transfers between devices: 9.25 us -> 6.05 us  [gathered_sum(): mixed = lax.all_to_all(parts, 'dp', 0, 0)]
  transfers between devices with their start and end apart: 5 -> 5, of which waited for: 2 -> 2; matrix products, arithmetic and copies ran while one was open for 4% -> 5% of each run, Pallas kernels for 9% -> 3%
where the time goes in v4:
time: 92.2 us; the launch traced here: 91.7 us
  blocking collectives  32.6 us (35%)
  starting transfers between devices  29.5 us (32%)
  waiting for transfers between devices  10.6 us (11%)
  other arithmetic  9.74 us (11%)
  Pallas kernels  6.51 us (7%)
  between operations  1.5 us (2%)
  local copies, waits for them, and re-layouts  1.21 us (1%)
    ppermute x4, starting transfers between devices, hop(): return lax.ppermute(block, 'facet', route)  23.4 us
    all_gather x1, blocking collectives, on_device(): squares = lax.all_gather((shifted * shifted).astype(jnp.bfloat16), 'cube')  16.5 us
    all_to_all x1, blocking collectives, on_device(): lax.all_to_all(jnp.broadcast_to(own_part, (DP,) + own_part.shape), 'dp',...  16.2 us
    ppermute x4, waiting for transfers between devices, hop(): return lax.ppermute(block, 'facet', route)  10.6 us
    all_to_all x1, starting transfers between devices, gathered_sum(): mixed = lax.all_to_all(parts, 'dp', 0, 0)  6.05 us
    pallas_call x1, Pallas kernels, gradient_parts(): pl.pallas_call(below_pass, out_shape=jax.ShapeDtypeStruct((DP, FR, SPAN),...  3.46 us
    pallas_call x1, Pallas kernels, own_spectra(): pl.pallas_call(own_pass, out_shape=(SPECTRA, SPECTRA, jax.ShapeDtypeStruc...  3.05 us
  transfers between devices with their start and end apart: 5, of which 2 were waited for; matrix products, arithmetic and copies ran while one was open for 5% of the time, Pallas kernels for 3%

profile of v4, /device:TPU:32, one launch (start us, length us, event | category | flops | bytes accessed | tf_op | source)
XLA Modules:
  0.0 91.7 jit_solution(14261789838271201616)
XLA Ops:
  0.6 0.7 convert_element_type.67
  1.3 0.7 convert_element_type.66
  1.9 0.7 convert_bitcast_fusion.weight_ref
  3.3 0.1 pad.42.clone
  3.4 0.1 maximum_maximum_fusion
  3.4 10.2 %collective-permute-start = (f32[19,64]{1,0:T(8,128)S(1)}, f32[19,64]{1,0:T(8,128)S(1)}, u32[]{:S(2)}, u32[]{:S(2)}) collective-permute-start(f32[19,64]{1,0:T(8,128)S(1)} %maximum_maximum_fusion), channel_id=1, source_target_pairs={{4,0},{8,4},{12,8},{16,12},{20,16},{24,20},{28,24},{32,28},{36,32}... | collective-permute-start | bytes 14600 | tf_op jit(solution)/shard_map/ppermute | solution.py:330
  13.7 2.6 %collective-permute-start.1 = (bf16[64,16,128]{2,1,0:T(8,128)(2,1)}, bf16[64,16,128]{2,1,0:T(8,128)(2,1)S(1)}, u32[]{:S(2)}, u32[]{:S(2)}) collective-permute-start(bf16[64,16,128]{2,1,0:T(8,128)(2,1)} %bitcast.46), channel_id=1, source_target_pairs={{4,0},{8,4},{12,8},{16,12},{20,16},{24,20},{28,24},{32,28},{36,32}... | collective-permute-start | bytes 786440 | tf_op jit(solution)/shard_map/ppermute | solution.py:330
  16.3 0.1 pad.38.clone
  16.4 0.7 add_add_fusion.numbers_ref
  17.1 1.1 %bitcast_convert_fusion.pixels_ref = bf16[48,2560]{1,0:T(8,128)(2,1)S(1)} fusion(f32[1,48,2560]{2,1,0:T(8,128)} %param.8), kind=kLoop, calls=%fused_computation.168 | loop fusion | flops 122880 | bytes 737280 | tf_op jit(solution)/shard_map/convert_element_type | solution.py:390
  18.2 1.0 %fusion.1 = f32[4,48,896]{2,1,0:T(8,128)S(1)} fusion(s32[]{:T(128)S(6)} %select_n.10, bf16[4,48,2560]{2,1,0:T(8,128)(2,1)} %bitcast.50), kind=kLoop, calls=%fused_computation.19 | loop fusion | flops 172032 | bytes 1671172 | tf_op jit(solution)/shard_map/convert_element_type | solution.py:382
  19.2 0.6 fusion.55
  19.8 0.0 copy-start
  19.8 0.0 copy-start.1
  19.9 0.6 fusion.40
  20.5 0.3 copy-done
  20.8 0.5 copy-done.1
  21.2 3.0 %own_spectra.1 = (f32[41,48,128]{2,1,0:T(8,128)S(1)}, f32[41,48,128]{2,1,0:T(8,128)S(1)}, bf16[640,640]{1,0:T(8,128)(2,1)S(1)}) custom-call(s32[3,64]{1,0:T(4,128)S(1)} %add_add_fusion.numbers_ref, f32[16,64]{1,0:T(8,128)S(1)} %convert_bitcast_fusion.weight_ref, bf16[64,16,128]{2,1,0:T(8,128)(2,1)S(1)} %bitcast.47, bf16[20,128,256]{2,1,0:T(8,128)(2,1)S(1)} %copy-done.1, ...), custom_call_target="tpu_custom_call" | custom-call | flops 2000000000 | bytes 4000000 | tf_op jit(solution)/shard_map/own_spectra/pallas_call | solution.py:288
  24.3 0.0 collective-permute-done
  24.3 0.0 collective-permute-done.1.payload_ref
  24.3 3.5 %gradient_parts.1 = bf16[4,48,768]{2,1,0:T(8,128)(2,1)} custom-call(s32[3,64]{1,0:T(4,128)S(1)} %slice_convert_fusion.2.numbers_ref, f32[16,64]{1,0:T(8,128)S(1)} %slice.407.weight_ref, bf16[64,16,128]{2,1,0:T(8,128)(2,1)S(1)} %collective-permute-done.1.payload_ref, f32[41,48,128]{2,1,0:T(8,128)S(1)} %get-tuple-element.5.spec_ref, ...), custom_call_target="tpu_custom_call" | custom-call | flops 2000000000 | bytes 4000000 | tf_op jit(solution)/shard_map/gradient_parts/pallas_call | solution.py:307
  27.8 0.0 copy-start.2
  27.8 6.1 %all-to-all-start = ((bf16[4,48,768]{2,1,0:T(8,128)(2,1)}), bf16[4,48,768]{2,1,0:T(8,128)(2,1)S(1)}, u32[]{:S(2)}, u32[]{:S(2)}) async-start(bf16[4,48,768]{2,1,0:T(8,128)(2,1)} %gradient_parts.1), calls=%async_computation | async-start | bytes 589824 | tf_op jit(solution)/shard_map/all_to_all | solution.py:334
  33.9 0.3 fusion.17
  34.2 8.7 %collective-permute-start.2 = (f32[8,768]{1,0:T(8,128)S(1)}, f32[8,768]{1,0:T(8,128)S(1)}, u32[]{:S(2)}, u32[]{:S(2)}) collective-permute-start(f32[8,768]{1,0:T(8,128)S(1)} %slice.445), channel_id=1, source_target_pairs={{4,0},{8,4},{12,8},{16,12},{20,16},{24,20},{28,24},{32,28},{36,32}... | collective-permute-start | bytes 73736 | tf_op jit(solution)/shard_map/ppermute | solution.py:330
  42.9 0.0 all-to-all-done
  43.0 1.4 %collective-permute-done.2 = f32[8,768]{1,0:T(8,128)S(1)} collective-permute-done((f32[8,768]{1,0:T(8,128)S(1)}, f32[8,768]{1,0:T(8,128)S(1)}, u32[]{:S(2)}, u32[]{:S(2)}) %collective-permute-start.2) | collective-permute-done | bytes 24608 | tf_op jit(solution)/shard_map/ppermute | solution.py:330
  44.4 0.0 copy-done.2
  44.4 0.1 subtract_select_fusion
  44.5 1.9 %collective-permute-start.3 = (bf16[8,768]{1,0:T(8,128)(2,1)S(1)}, bf16[8,768]{1,0:T(8,128)(2,1)S(1)}, u32[]{:S(2)}, u32[]{:S(2)}) collective-permute-start(bf16[8,768]{1,0:T(8,128)(2,1)S(1)} %slice.877), channel_id=1, source_target_pairs={{0,4},{4,8},{8,12},{12,16},{16,20},{20,24},{24,28},{28,32},{32,36}... | collective-permute-start | bytes 36872 | tf_op jit(solution)/shard_map/ppermute | solution.py:330
  46.4 9.2 %collective-permute-done.3 = bf16[8,768]{1,0:T(8,128)(2,1)S(1)} collective-permute-done((bf16[8,768]{1,0:T(8,128)(2,1)S(1)}, bf16[8,768]{1,0:T(8,128)(2,1)S(1)}, u32[]{:S(2)}, u32[]{:S(2)}) %collective-permute-start.3) | collective-permute-done | bytes 12320 | tf_op jit(solution)/shard_map/ppermute | solution.py:330
  55.6 0.2 multiply_add_fusion.1
  55.9 0.3 add_bitcast_fusion.1
  56.2 0.3 add_bitcast_fusion.3
  56.5 0.1 multiply_convert_fusion.1
  56.5 16.5 %all-gather = bf16[16,48,640]{2,1,0:T(8,128)(2,1)S(1)} all-gather(bf16[4,48,640]{2,1,0:T(8,128)(2,1)S(1)} %multiply_convert_fusion.1), channel_id=2, replica_groups=mesh['cube'=4,'facet'=32,'dp'=4] {'cube'}, dimensions={0}, use_global_device_ids=true | all-gather | bytes 1228800 | tf_op jit(solution)/shard_map/all_gather | solution.py:410
  73.0 0.1 convert_reduce_fusion
  73.1 0.3 multiply_convert_fusion
  73.4 0.1 broadcast_in_dim.25
  73.5 16.2 %all_to_all.10 = bf16[4,5,48,640]{3,2,1,0:T(8,128)(2,1)S(1)} all-to-all(bf16[4,5,48,640]{3,2,1,0:T(8,128)(2,1)S(1)} %broadcast_in_dim.25), channel_id=1, replica_groups=mesh['cube'=4,'facet'=32,'dp'=4] {'dp'}, dimensions={0} | all-to-all | bytes 2457600 | tf_op jit(solution)/shard_map/all_to_all | solution.py:414
  89.7 0.1 slice_bitcast_fusion.3
  89.8 0.9 subtract_maximum_fusion
  90.7 1.0 %fusion = bf16[4,1,48,2560]{3,2,1,0:T(8,128)(2,1)} fusion(bf16[5,48,640]{2,1,0:T(8,128)(2,1)S(1)} %get-tuple-element.11, bf16[5,48,640]{2,1,0:T(8,128)(2,1)S(1)} %get-tuple-element.12, bf16[5,48,640]{2,1,0:T(8,128)(2,1)S(1)} %get-tuple-element.13, bf16[5,48,640]{2,1,0:T(8,128)(2,1)S(1)} %get-tuple-element.10), kind=kLoop, calls=%fused_computation.3 | loop fusion | flops 3932160 | bytes 2211840 | tf_op jit(solution)/shard_map/broadcast_in_dim | solution.py:418
  (10 shorter events, 0.2 us)
Async XLA Ops:
  3.4 20.9 %collective-permute-start = (f32[19,64]{1,0:T(8,128)S(1)}, f32[19,64]{1,0:T(8,128)S(1)}, u32[]{:S(2)}, u32[]{:S(2)}) collective-permute-start(f32[19,64]{1,0:T(8,128)S(1)} %maximum_maximum_fusion), channel_id=1, source_target_pairs={{4,0},{8,4},{12,8},{16,12},{20,16},{24,20},{28,24},{32,28},{36,32}... | collective-permute-start | bytes 14600 | tf_op jit(solution)/shard_map/ppermute | solution.py:330
  13.7 10.7 %collective-permute-start.1 = (bf16[64,16,128]{2,1,0:T(8,128)(2,1)}, bf16[64,16,128]{2,1,0:T(8,128)(2,1)S(1)}, u32[]{:S(2)}, u32[]{:S(2)}) collective-permute-start(bf16[64,16,128]{2,1,0:T(8,128)(2,1)} %bitcast.46), channel_id=1, source_target_pairs={{4,0},{8,4},{12,8},{16,12},{20,16},{24,20},{28,24},{32,28},{36,32}... | collective-permute-start | bytes 786440 | tf_op jit(solution)/shard_map/ppermute | solution.py:330
  19.8 1.0 %copy-start = (bf16[1,64,16,128]{3,2,1,0:T(8,128)(2,1)S(1)}, bf16[1,64,16,128]{3,2,1,0:T(8,128)(2,1)}, u32[]{:S(2)}) copy-start(bf16[1,64,16,128]{3,2,1,0:T(8,128)(2,1)} %param.10) | copy-start | bytes 786436
  19.8 1.4 %copy-start.1 = (bf16[20,128,256]{2,1,0:T(8,128)(2,1)S(1)}, bf16[20,128,256]{2,1,0:T(8,128)(2,1)}, u32[]{:S(2)}) copy-start(bf16[20,128,256]{2,1,0:T(8,128)(2,1)} %constant.47.clone.table_ref) | copy-start | bytes 3932164
  27.8 16.6 %copy-start.2 = (f32[1,48,2560]{2,1,0:T(8,128)S(1)}, f32[1,48,2560]{2,1,0:T(8,128)}, u32[]{:S(2)}) copy-start(f32[1,48,2560]{2,1,0:T(8,128)} %param.8) | copy-start | bytes 1474564
  27.8 15.1 %all-to-all-start = ((bf16[4,48,768]{2,1,0:T(8,128)(2,1)}), bf16[4,48,768]{2,1,0:T(8,128)(2,1)S(1)}, u32[]{:S(2)}, u32[]{:S(2)}) async-start(bf16[4,48,768]{2,1,0:T(8,128)(2,1)} %gradient_parts.1), calls=%async_computation | async-start | bytes 589824 | tf_op jit(solution)/shard_map/all_to_all | solution.py:334
  34.2 10.2 %collective-permute-start.2 = (f32[8,768]{1,0:T(8,128)S(1)}, f32[8,768]{1,0:T(8,128)S(1)}, u32[]{:S(2)}, u32[]{:S(2)}) collective-permute-start(f32[8,768]{1,0:T(8,128)S(1)} %slice.445), channel_id=1, source_target_pairs={{4,0},{8,4},{12,8},{16,12},{20,16},{24,20},{28,24},{32,28},{36,32}... | collective-permute-start | bytes 73736 | tf_op jit(solution)/shard_map/ppermute | solution.py:330
  44.5 11.1 %collective-permute-start.3 = (bf16[8,768]{1,0:T(8,128)(2,1)S(1)}, bf16[8,768]{1,0:T(8,128)(2,1)S(1)}, u32[]{:S(2)}, u32[]{:S(2)}) collective-permute-start(bf16[8,768]{1,0:T(8,128)(2,1)S(1)} %slice.877), channel_id=1, source_target_pairs={{0,4},{4,8},{8,12},{12,16},{16,20},{20,24},{24,28},{28,32},{32,36}... | collective-permute-start | bytes 36872 | tf_op jit(solution)/shard_map/ppermute | solution.py:330

commit v5 on v4

--- a/solution.py
+++ b/solution.py
@@ -57,6 +57,17 @@
     angles = (x[:, :, None] * np.arange(R)[None, None, :] % W) * (2.0 * math.pi / W)
     table = np.concatenate([np.cos(angles), -np.sin(angles)], -1).astype(jnp.bfloat16)
     return table
+
+
+def column_filters():
+    band = np.zeros((2 * HALO, 2 * HALO), np.float32)
+    for b, taps in enumerate((LOWPASS, HIGHPASS)):
+        for k in range(8):
+            j = np.arange(HALO)
+            band[HALO + j - k, HALO * b + j] = taps[k]
+    leading = band.astype(jnp.bfloat16)
+    rest = (band - leading.astype(np.float32)).astype(jnp.bfloat16)
+    return np.stack([leading, rest])
 
 
 def times_i(value, sign):
@@ -176,7 +187,7 @@
 
     order_ref[...] = residue_order()
     stacked = jnp.concatenate(
-        [pixels_ref[:, PART * g : PART * (g + 1)] for g in range(4)], 0
+        [pixels_ref[:, PART * g : PART * (g + 1)].astype(jnp.bfloat16) for g in range(4)], 0
     )
     sorted_rows = jnp.dot(stacked, order_ref[...], preferred_element_type=jnp.float32)
     for j in range(5):
@@ -324,15 +335,114 @@
     )(numbers, weights, payload, spectra, own, table, order)
 
 
-def hop(block, distance):
-    devices = range(lax.axis_size("facet"))
-    route = [(i - distance, i) for i in devices if i - distance in devices]
-    return lax.ppermute(block, "facet", route)
-
-
-def gathered_sum(parts):
-    mixed = lax.all_to_all(parts, "dp", 0, 0)
-    return jnp.sum(mixed.astype(jnp.float32), 0)
+def update(left_ref, parts_ref, synth_ref, old_ref, copies_ref, last_ref, total_ref):
+    total = synth_ref[...]
+    for d in range(DP):
+        total = total + parts_ref[d].astype(jnp.float32)
+    old = old_ref[...]
+    new = jnp.maximum(old - TAU_STEP * total, 0.0)
+    column = lax.broadcasted_iota(jnp.int32, old.shape, 1) + left_ref[0]
+    extra = jnp.where(column >= HALO, 2.0 * new - old, 0.0).astype(jnp.bfloat16)
+    for c in range(4):
+        copies_ref[c] = extra
+    last_ref[...] = extra[FR - TILE :]
+    total_ref[...] = total[:, HALO:].astype(jnp.bfloat16)
+
+
+def updated_columns(left, parts, synth, old):
+    return pl.pallas_call(
+        update,
+        out_shape=(
+            jax.ShapeDtypeStruct((4, FR, SPAN), jnp.bfloat16),
+            jax.ShapeDtypeStruct((TILE, SPAN), jnp.bfloat16),
+            jax.ShapeDtypeStruct((FR, PART), jnp.bfloat16),
+        ),
+        in_specs=[SMEM_SPEC] + [VMEM_SPEC] * 3,
+        out_specs=(VMEM_SPEC,) * 3,
+        compiler_params=pltpu.CompilerParams(vmem_limit_bytes=VMEM_LIMIT),
+        name="updated_columns",
+    )(left, parts, synth, old)
+
+
+def shrink(
+    channel_ref,
+    extra_ref,
+    above0_ref,
+    above1_ref,
+    above2_ref,
+    above3_ref,
+    dual_ref,
+    total_ref,
+    filters_ref,
+    out_ref,
+    rows_ref,
+    own_ref,
+    norm_ref,
+):
+    above = (above0_ref, above1_ref, above2_ref, above3_ref)
+    for k in range(4):
+        channel = (channel_ref[0] + 4 - k) & 3
+        for j in range(PART // HALO):
+            window = pl.ds(HALO * j, 2 * HALO)
+            block = jnp.concatenate([above[k][:, window], extra_ref[channel, :, window]], 0)
+            rows_ref[...] = jnp.dot(
+                block, filters_ref[0], preferred_element_type=jnp.float32
+            ) + jnp.dot(block, filters_ref[1], preferred_element_type=jnp.float32)
+            tile = pl.ds(HALO * j, HALO)
+            for b in range(2):
+                across = [rows_ref[TILE - i : TILE - i + FR, HALO * b : HALO * (b + 1)] for i in range(8)]
+                for a, taps in enumerate((LOWPASS, HIGHPASS)):
+                    value = taps[0] * across[0]
+                    for i in range(1, 8):
+                        value = value + taps[i] * across[i]
+                    s = 2 * a + b
+                    moved = (
+                        dual_ref[channel, s, :, tile].astype(jnp.float32) + SIGMA_STEP * value
+                    )
+                    if k == 0:
+                        own_ref[s, :, tile] = moved
+                        norm_ref[s, :, tile] = moved * moved
+                    elif k < 3:
+                        norm_ref[s, :, tile] += moved * moved
+                    else:
+                        norm = norm_ref[s, :, tile] + moved * moved
+                        scale = jnp.minimum(RADIUS * lax.rsqrt(norm), 1.0)
+                        result = (own_ref[s, :, tile] * scale).astype(jnp.bfloat16)
+                        for d in range(DP):
+                            out_ref[d, s, :, tile] = result
+    for d in range(DP):
+        out_ref[d, 4] = total_ref[...]
+
+
+def dual_columns(channel, extra, above, dual, total, filters):
+    return pl.pallas_call(
+        shrink,
+        out_shape=jax.ShapeDtypeStruct((DP, 5, FR, PART), jnp.bfloat16),
+        in_specs=[SMEM_SPEC] + [VMEM_SPEC] * 8,
+        out_specs=VMEM_SPEC,
+        scratch_shapes=[
+            pltpu.VMEM((FR + TILE, 2 * HALO), jnp.float32),
+            pltpu.VMEM((4, FR, PART), jnp.float32),
+            pltpu.VMEM((4, FR, PART), jnp.float32),
+        ],
+        compiler_params=pltpu.CompilerParams(vmem_limit_bytes=VMEM_LIMIT),
+        name="dual_columns",
+    )(channel, extra, *above, dual, total, filters)
+
+
+def copies(block, axis):
+    return lax.all_to_all(block, axis, 0, 0)
+
+
+def hop(block, distance, turn=0):
+    channels, facets = lax.axis_size("cube"), lax.axis_size("facet")
+    route = [
+        (c * facets + f - distance, (c + turn) % channels * facets + f)
+        for c in range(channels)
+        for f in range(facets)
+        if 0 <= f - distance < facets
+    ]
+    return lax.ppermute(block, ("cube", "facet"), route)
 
 
 def synthesize(dual):
@@ -348,47 +458,30 @@
     return summed
 
 
-def analyze(extra):
-    subbands = []
-    for row_taps in (LOWPASS, HIGHPASS):
-        filtered = sum(row_taps[k] * extra[8 - k : 8 - k + FR] for k in range(8))
-        for col_taps in (LOWPASS, HIGHPASS):
-            subbands.append(
-                sum(col_taps[k] * filtered[:, HALO - k : HALO - k + PART] for k in range(8))
-            )
-    return jnp.stack(subbands)
-
-
 def on_device(image, dual, payload, vis_weight, freq_start, tile_slot, live):
     table = jnp.asarray(tables())
+    filters = jnp.asarray(column_filters())
     position = lax.axis_index("dp")
     own_rows = image[0]
     payload_below = hop(payload[0], -1)
-    meta = jnp.concatenate(
-        [
-            vis_weight[0].T.astype(jnp.float32),
-            freq_start.astype(jnp.float32),
-            tile_slot.astype(jnp.float32),
-            jnp.broadcast_to(live, (1, BLK)).astype(jnp.float32),
-        ],
-        0,
+    left = position * PART
+    dual_slice = lax.dynamic_slice_in_dim(
+        jnp.pad(dual[:, 0], ((0, 0), (0, 0), (0, 128))), left, SPAN, 2
     )
+    duals = lax.all_gather(dual_slice, "cube")
+
+    numbers = jnp.concatenate([freq_start, tile_slot, jnp.broadcast_to(live, (1, BLK))], 0)
+    meta = jnp.concatenate([vis_weight[0].T.astype(jnp.float32), numbers.astype(jnp.float32)], 0)
     meta_below = hop(meta, -1)
-    numbers = jnp.concatenate([freq_start, tile_slot, jnp.broadcast_to(live, (1, BLK))], 0)
-
-    left = position * PART
+
     own_dual = lax.dynamic_slice_in_dim(
         jnp.pad(dual[:, 0], ((0, 0), (0, 0), (HALO, 128))), left, SPAN + 128, 2
     ).astype(jnp.float32)
-    old = lax.dynamic_slice_in_dim(
-        jnp.pad(own_rows, ((0, 0), (HALO, 0))), left, SPAN, 1
-    )
+    old = lax.dynamic_slice_in_dim(jnp.pad(own_rows, ((0, 0), (HALO, 0))), left, SPAN, 1)
     synth = synthesize(own_dual)
     synth_below = hop(synth[:8], -1)
 
-    spectra, own, order = own_spectra(
-        numbers, meta[:TILE], payload[0], table, own_rows.astype(jnp.bfloat16)
-    )
+    spectra, own, order = own_spectra(numbers, meta[:TILE], payload[0], table, own_rows)
     terms = gradient_parts(
         meta_below[TILE:].astype(jnp.int32),
         meta_below[:TILE],
@@ -399,20 +492,13 @@
         order,
     )
     synth = synth[8:] + jnp.pad(synth_below, ((FR - 8, 0), (0, 0)))
-    total = gathered_sum(terms) + synth
-    new = jnp.maximum(old - TAU_STEP * total, 0.0)
-    column = lax.broadcasted_iota(jnp.int32, old.shape, 1) + left
-    extra = jnp.where(column >= HALO, 2.0 * new - old, 0.0)
-    extra_above = hop(extra[FR - 8 :].astype(jnp.bfloat16), 1).astype(jnp.float32)
-    extra = jnp.concatenate([extra_above, extra], 0)
-
-    shifted = own_dual[:, :, HALO : HALO + PART] + SIGMA_STEP * analyze(extra)
-    squares = lax.all_gather((shifted * shifted).astype(jnp.bfloat16), "cube")
-    norms = jnp.sqrt(jnp.sum(squares.astype(jnp.float32), 0))
-    dual_part = (shifted * (RADIUS / jnp.maximum(norms, RADIUS))).astype(jnp.bfloat16)
-    own_part = jnp.concatenate([dual_part, total[None, :, HALO:].astype(jnp.bfloat16)], 0)
-    parts = lax.all_to_all(jnp.broadcast_to(own_part, (DP,) + own_part.shape), "dp", 0, 0)
-    whole = jnp.concatenate([parts[d] for d in range(DP)], -1)
+    parts = copies(terms, "dp")
+    extra_copies, last_rows, total = updated_columns(left[None], parts, synth, old)
+    extra = copies(extra_copies, "cube")
+    above = [hop(last_rows, 1, k) for k in range(4)]
+    channel = lax.axis_index("cube")
+    result = dual_columns(channel[None], extra, above, duals, total, filters)
+    whole = jnp.concatenate([part for part in copies(result, "dp")], -1)
     dual_next = whole[:4]
     updated = jnp.maximum(own_rows - TAU_STEP * whole[4].astype(jnp.float32), 0.0)
     return (updated[None], dual_next[:, None])

time: 92.2 us -> 107 us (1.16)
  the two profiles are of different devices: /device:TPU:32 before, /device:TPU:1 now
where the time goes in v5:
time: 107 us
  starting transfers between devices  42.6 us (40%)
  blocking collectives  19.7 us (18%)
  between operations  15 us (14%)
  waiting for transfers between devices  10.8 us (10%)
  Pallas kernels  10.6 us (10%)
  other arithmetic  4.93 us (5%)
  local copies, waits for them, and re-layouts  3.26 us (3%)
    ppermute x7, starting transfers between devices, hop(): return lax.ppermute(block, ('cube', 'facet'), route)  33.7 us
    all_to_all x1, blocking collectives, copies(): return lax.all_to_all(block, axis, 0, 0)  19.7 us
    all_to_all x2, starting transfers between devices, copies(): return lax.all_to_all(block, axis, 0, 0)  8.89 us
    all_to_all x2, waiting for transfers between devices, copies(): return lax.all_to_all(block, axis, 0, 0)  5.64 us
    ppermute x7, waiting for transfers between devices, hop(): return lax.ppermute(block, ('cube', 'facet'), route)  5.18 us
    pallas_call x1, Pallas kernels, gradient_parts(): pl.pallas_call(below_pass, out_shape=jax.ShapeDtypeStruct((DP, FR, SPAN),...  4.46 us
    pallas_call x1, Pallas kernels, dual_columns(): pl.pallas_call(shrink, out_shape=jax.ShapeDtypeStruct((DP, 5, FR, PART),...  2.74 us
    pallas_call x1, Pallas kernels, own_spectra(): pl.pallas_call(own_pass, out_shape=(SPECTRA, SPECTRA, jax.ShapeDtypeStruc...  2.58 us
  transfers between devices with their start and end apart: 10, of which 3 were waited for; matrix products, arithmetic and copies ran while one was open for 3% of the time, Pallas kernels for 7%

profile of v5, /device:TPU:1, one launch (start us, length us, event | category | flops | bytes accessed | tf_op | source)
XLA Modules:
  0.0 106.9 jit_solution(11382777054267647220)
XLA Ops:
  7.2 0.0 copy-start.5
  7.2 0.0 all-gather.3.cloned.1.call-start
  7.9 0.7 convert_bitcast_fusion.weight_ref
  8.6 0.1 pad.37.clone
  8.7 0.7 add_add_fusion
  9.5 8.8 %collective-permute-start = (f32[19,64]{1,0:T(8,128)S(1)}, f32[19,64]{1,0:T(8,128)S(1)}, u32[]{:S(2)}, u32[]{:S(2)}) collective-permute-start(f32[19,64]{1,0:T(8,128)S(1)} %pad_maximum_fusion.3), channel_id=1, source_target_pairs={{4,0},{8,4},{12,8},{16,12},{20,16},{24,20},{28,24},{32,28},{36,32}... | collective-permute-start | bytes 14600 | tf_op jit(solution)/shard_map/ppermute | solution.py:445
  18.2 1.9 %collective-permute-start.1 = (bf16[64,16,128]{2,1,0:T(8,128)(2,1)}, bf16[64,16,128]{2,1,0:T(8,128)(2,1)S(1)}, u32[]{:S(2)}, u32[]{:S(2)}) collective-permute-start(bf16[64,16,128]{2,1,0:T(8,128)(2,1)} %bitcast.38), channel_id=1, source_target_pairs={{4,0},{8,4},{12,8},{16,12},{20,16},{24,20},{28,24},{32,28},{36,32}... | collective-permute-start | bytes 786440 | tf_op jit(solution)/shard_map/ppermute | solution.py:445
  20.2 1.7 %pad_dynamic-slice_fusion.1 = bf16[4,48,768]{2,1,0:T(8,128)(2,1)} fusion(s32[]{:T(128)S(6)} %select_n.8, bf16[4,48,2560]{2,1,0:T(8,128)(2,1)} %bitcast.40), kind=kLoop, calls=%fused_computation.1 | loop fusion | bytes 1277956 | tf_op jit(solution)/shard_map/dynamic_slice | solution.py:468
  21.9 0.0 all-gather.3.cloned.1.call-update
  21.9 0.0 copy-done.5
  21.9 0.1 fusion.1
  22.0 0.6 fusion.48
  22.6 0.0 copy-start
  22.7 0.0 copy-start.3
  22.7 0.0 copy-start.4
  22.7 0.6 fusion.33
  23.3 0.3 fusion.17
  23.6 1.9 %collective-permute-start.2 = (f32[8,768]{1,0:T(8,128)S(1)}, f32[8,768]{1,0:T(8,128)S(1)}, u32[]{:S(2)}, u32[]{:S(2)}) collective-permute-start(f32[8,768]{1,0:T(8,128)S(1)} %slice.299), channel_id=1, source_target_pairs={{4,0},{8,4},{12,8},{16,12},{20,16},{24,20},{28,24},{32,28},{36,32}... | collective-permute-start | bytes 73736 | tf_op jit(solution)/shard_map/ppermute | solution.py:445
  25.6 0.0 copy-done
  25.6 0.0 copy-done.3
  25.6 0.0 copy-done.4
  25.6 2.6 %own_spectra.1 = (f32[41,48,128]{2,1,0:T(8,128)S(1)}, f32[41,48,128]{2,1,0:T(8,128)S(1)}, bf16[640,640]{1,0:T(8,128)(2,1)S(1)}) custom-call(s32[3,64]{1,0:T(4,128)S(1)} %get-tuple-element.26.numbers_ref, f32[16,64]{1,0:T(8,128)S(1)} %convert_bitcast_fusion.weight_ref, bf16[64,16,128]{2,1,0:T(8,128)(2,1)S(1)} %bitcast.39, ...), custom_call_target="tpu_custom_call" | custom-call | flops 2000000000 | bytes 4000000 | tf_op jit(solution)/shard_map/own_spectra/pallas_call | solution.py:299
  28.2 0.0 collective-permute-done
  28.2 2.0 %collective-permute-done.1.payload_ref = bf16[64,16,128]{2,1,0:T(8,128)(2,1)S(1)} collective-permute-done((bf16[64,16,128]{2,1,0:T(8,128)(2,1)}, bf16[64,16,128]{2,1,0:T(8,128)(2,1)S(1)}, u32[]{:S(2)}, u32[]{:S(2)}) %collective-permute-start.1) | collective-permute-done | bytes 262176 | tf_op jit(solution)/shard_map/ppermute | solution.py:445
  30.2 4.5 %gradient_parts.1 = bf16[4,48,768]{2,1,0:T(8,128)(2,1)} custom-call(s32[3,64]{1,0:T(4,128)S(1)} %slice_convert_fusion.numbers_ref, f32[16,64]{1,0:T(8,128)S(1)} %slice.261.weight_ref, bf16[64,16,128]{2,1,0:T(8,128)(2,1)S(1)} %collective-permute-done.1.payload_ref, f32[41,48,128]{2,1,0:T(8,128)S(1)} %get-tuple-element.8.spec_ref, ...), custom_call_target="tpu_custom_call" | custom-call | flops 2000000000 | bytes 4000000 | tf_op jit(solution)/shard_map/gradient_parts/pallas_call | solution.py:318
  34.7 0.0 copy-start.2
  34.7 3.6 %all-to-all-start = ((bf16[4,48,768]{2,1,0:T(8,128)(2,1)}), bf16[4,48,768]{2,1,0:T(8,128)(2,1)S(1)}, u32[]{:S(2)}, u32[]{:S(2)}) async-start(bf16[4,48,768]{2,1,0:T(8,128)(2,1)} %gradient_parts.1), calls=%async_computation | async-start | bytes 589824 | tf_op jit(solution)/shard_map/all_to_all | solution.py:434
  38.3 0.0 collective-permute-done.2
  38.3 5.6 %all-to-all-done.parts_ref = bf16[4,48,768]{2,1,0:T(8,128)(2,1)S(1)} async-done(((bf16[4,48,768]{2,1,0:T(8,128)(2,1)}), bf16[4,48,768]{2,1,0:T(8,128)(2,1)S(1)}, u32[]{:S(2)}, u32[]{:S(2)}) %all-to-all-start) | async-done | bytes 294944 | tf_op jit(solution)/shard_map/all_to_all | solution.py:434
  44.0 0.8 updated_columns.1
  44.7 5.3 %all-to-all-start.1 = ((bf16[4,48,768]{2,1,0:T(8,128)(2,1)}), bf16[4,48,768]{2,1,0:T(8,128)(2,1)S(1)}, u32[]{:S(2)}, u32[]{:S(2)}) async-start(bf16[4,48,768]{2,1,0:T(8,128)(2,1)} %get-tuple-element.11), calls=%async_computation.1 | async-start | bytes 589824 | tf_op jit(solution)/shard_map/all_to_all | solution.py:434
  50.1 5.9 %collective-permute-start.3 = (bf16[16,768]{1,0:T(8,128)(2,1)S(1)}, bf16[16,768]{1,0:T(8,128)(2,1)S(1)}, u32[]{:S(2)}, u32[]{:S(2)}) collective-permute-start(bf16[16,768]{1,0:T(8,128)(2,1)S(1)} %get-tuple-element.12), channel_id=1, source_target_pairs={{0,4},{4,8},{8,12},{12,16},{16,20},{20,24},{24,28},{28,32},{32,36}... | collective-permute-start | bytes 73736 | tf_op jit(solution)/shard_map/ppermute | solution.py:445
  56.0 4.0 %collective-permute-start.4 = (bf16[16,768]{1,0:T(8,128)(2,1)S(1)}, bf16[16,768]{1,0:T(8,128)(2,1)S(1)}, u32[]{:S(2)}, u32[]{:S(2)}) collective-permute-start(bf16[16,768]{1,0:T(8,128)(2,1)S(1)} %get-tuple-element.12), channel_id=1, source_target_pairs={{0,132},{4,136},{8,140},{12,144},{16,148},{20,152},{24,156},{28,16... | collective-permute-start | bytes 73736 | tf_op jit(solution)/shard_map/ppermute | solution.py:445
  59.9 9.3 %collective-permute-start.5 = (bf16[16,768]{1,0:T(8,128)(2,1)S(1)}, bf16[16,768]{1,0:T(8,128)(2,1)S(1)}, u32[]{:S(2)}, u32[]{:S(2)}) collective-permute-start(bf16[16,768]{1,0:T(8,128)(2,1)S(1)} %get-tuple-element.12), channel_id=1, source_target_pairs={{0,260},{4,264},{8,268},{12,272},{16,276},{20,280},{24,284},{28,28... | collective-permute-start | bytes 73736 | tf_op jit(solution)/shard_map/ppermute | solution.py:445
  69.2 1.9 %collective-permute-start.6 = (bf16[16,768]{1,0:T(8,128)(2,1)S(1)}, bf16[16,768]{1,0:T(8,128)(2,1)S(1)}, u32[]{:S(2)}, u32[]{:S(2)}) collective-permute-start(bf16[16,768]{1,0:T(8,128)(2,1)S(1)} %get-tuple-element.12), channel_id=1, source_target_pairs={{0,388},{4,392},{8,396},{12,400},{16,404},{20,408},{24,412},{28,41... | collective-permute-start | bytes 73736 | tf_op jit(solution)/shard_map/ppermute | solution.py:445
  71.1 0.0 collective-permute-done.3.above0_ref
  71.2 0.0 collective-permute-done.4.above1_ref
  71.2 0.0 collective-permute-done.5.above2_ref
  71.2 3.2 %collective-permute-done.6.above3_ref = bf16[16,768]{1,0:T(8,128)(2,1)S(1)} collective-permute-done((bf16[16,768]{1,0:T(8,128)(2,1)S(1)}, bf16[16,768]{1,0:T(8,128)(2,1)S(1)}, u32[]{:S(2)}, u32[]{:S(2)}) %collective-permute-start.6) | collective-permute-done | bytes 24608 | tf_op jit(solution)/shard_map/ppermute | solution.py:445
  74.4 0.0 all-to-all-done.1.extra_ref
  74.4 0.0 all-gather.3.cloned.1.call-done
  74.4 0.0 copy-done.2
  74.4 0.0 copy-start.1
  74.4 1.3 %copy-done.1 = bf16[16,48,768]{2,1,0:T(8,128)(2,1)S(1)} copy-done((bf16[16,48,768]{2,1,0:T(8,128)(2,1)S(1)}, bf16[16,48,768]{2,1,0:T(8,128)(2,1)}, u32[]{:S(2)}) %copy-start.1) | copy-done | bytes 1179672
  75.6 2.7 %dual_columns.1 = bf16[4,5,48,640]{3,2,1,0:T(8,128)(2,1)S(1)} custom-call(s32[1]{0:T(128)} %bitcast.channel_ref, bf16[4,48,768]{2,1,0:T(8,128)(2,1)S(1)} %all-to-all-done.1.extra_ref, bf16[16,768]{1,0:T(8,128)(2,1)S(1)} %collective-permute-done.3.above0_ref, bf16[16,768]{1,0:T(8,128)(2,1)S(1)} %collective-permute-done.4.above1_ref, ...), custom_call_target="tpu_custom_call" | custom-call | tf_op jit(solution)/shard_map/dual_columns/pallas_call | solution.py:418
  78.4 19.7 %all_to_all.15 = bf16[4,5,48,640]{3,2,1,0:T(8,128)(2,1)S(1)} all-to-all(bf16[4,5,48,640]{3,2,1,0:T(8,128)(2,1)S(1)} %dual_columns.1), channel_id=1, replica_groups=mesh['cube'=4,'facet'=32,'dp'=4] {'dp'}, dimensions={0} | all-to-all | bytes 2457600 | tf_op jit(solution)/shard_map/all_to_all | solution.py:434
  98.1 0.1 slice_bitcast_fusion.3
  98.2 0.9 subtract_maximum_fusion
  99.0 1.0 fusion
  (7 shorter events, 0.1 us)
Async XLA Ops:
  7.2 14.8 %copy-start.5 = (bf16[4,1,48,2560]{3,2,1,0:T(8,128)(2,1)S(1)}, bf16[4,1,48,2560]{3,2,1,0:T(8,128)(2,1)}, u32[]{:S(2)}) copy-start(bf16[4,1,48,2560]{3,2,1,0:T(8,128)(2,1)} %param.10) | copy-start | bytes 2949124
  7.2 67.2 %all-gather.3.cloned.1.call-start = ((), (), s32[]{:S(2)}) async-start(), calls=%async_computation.3 | async-start | bytes 1474560 | tf_op jit(solution)/shard_map/all_gather | solution.py:471
  9.5 18.8 %collective-permute-start = (f32[19,64]{1,0:T(8,128)S(1)}, f32[19,64]{1,0:T(8,128)S(1)}, u32[]{:S(2)}, u32[]{:S(2)}) collective-permute-start(f32[19,64]{1,0:T(8,128)S(1)} %pad_maximum_fusion.3), channel_id=1, source_target_pairs={{4,0},{8,4},{12,8},{16,12},{20,16},{24,20},{28,24},{32,28},{36,32}... | collective-permute-start | bytes 14600 | tf_op jit(solution)/shard_map/ppermute | solution.py:445
  18.2 12.0 %collective-permute-start.1 = (bf16[64,16,128]{2,1,0:T(8,128)(2,1)}, bf16[64,16,128]{2,1,0:T(8,128)(2,1)S(1)}, u32[]{:S(2)}, u32[]{:S(2)}) collective-permute-start(bf16[64,16,128]{2,1,0:T(8,128)(2,1)} %bitcast.38), channel_id=1, source_target_pairs={{4,0},{8,4},{12,8},{16,12},{20,16},{24,20},{28,24},{32,28},{36,32}... | collective-permute-start | bytes 786440 | tf_op jit(solution)/shard_map/ppermute | solution.py:445
  22.6 2.9 %copy-start = (f32[1,48,2560]{2,1,0:T(8,128)S(1)}, f32[1,48,2560]{2,1,0:T(8,128)}, u32[]{:S(2)}) copy-start(f32[1,48,2560]{2,1,0:T(8,128)} %param.9) | copy-start | bytes 1474564
  22.7 2.9 %copy-start.3 = (bf16[1,64,16,128]{3,2,1,0:T(8,128)(2,1)S(1)}, bf16[1,64,16,128]{3,2,1,0:T(8,128)(2,1)}, u32[]{:S(2)}) copy-start(bf16[1,64,16,128]{3,2,1,0:T(8,128)(2,1)} %param.11) | copy-start | bytes 786436
  22.7 2.9 %copy-start.4 = (bf16[20,128,256]{2,1,0:T(8,128)(2,1)S(1)}, bf16[20,128,256]{2,1,0:T(8,128)(2,1)}, u32[]{:S(2)}) copy-start(bf16[20,128,256]{2,1,0:T(8,128)(2,1)} %constant.16.clone.table_ref) | copy-start | bytes 3932164
  23.6 14.7 %collective-permute-start.2 = (f32[8,768]{1,0:T(8,128)S(1)}, f32[8,768]{1,0:T(8,128)S(1)}, u32[]{:S(2)}, u32[]{:S(2)}) collective-permute-start(f32[8,768]{1,0:T(8,128)S(1)} %slice.299), channel_id=1, source_target_pairs={{4,0},{8,4},{12,8},{16,12},{20,16},{24,20},{28,24},{32,28},{36,32}... | collective-permute-start | bytes 73736 | tf_op jit(solution)/shard_map/ppermute | solution.py:445
  34.7 39.7 %copy-start.2 = (bf16[2,256,256]{2,1,0:T(8,128)(2,1)S(1)}, bf16[2,256,256]{2,1,0:T(8,128)(2,1)}, u32[]{:S(2)}) copy-start(bf16[2,256,256]{2,1,0:T(8,128)(2,1)} %constant.17.clone.filters_ref) | copy-start | bytes 786436
  34.7 9.3 %all-to-all-start = ((bf16[4,48,768]{2,1,0:T(8,128)(2,1)}), bf16[4,48,768]{2,1,0:T(8,128)(2,1)S(1)}, u32[]{:S(2)}, u32[]{:S(2)}) async-start(bf16[4,48,768]{2,1,0:T(8,128)(2,1)} %gradient_parts.1), calls=%async_computation | async-start | bytes 589824 | tf_op jit(solution)/shard_map/all_to_all | solution.py:434
  44.7 29.6 %all-to-all-start.1 = ((bf16[4,48,768]{2,1,0:T(8,128)(2,1)}), bf16[4,48,768]{2,1,0:T(8,128)(2,1)S(1)}, u32[]{:S(2)}, u32[]{:S(2)}) async-start(bf16[4,48,768]{2,1,0:T(8,128)(2,1)} %get-tuple-element.11), calls=%async_computation.1 | async-start | bytes 589824 | tf_op jit(solution)/shard_map/all_to_all | solution.py:434
  50.1 21.1 %collective-permute-start.3 = (bf16[16,768]{1,0:T(8,128)(2,1)S(1)}, bf16[16,768]{1,0:T(8,128)(2,1)S(1)}, u32[]{:S(2)}, u32[]{:S(2)}) collective-permute-start(bf16[16,768]{1,0:T(8,128)(2,1)S(1)} %get-tuple-element.12), channel_id=1, source_target_pairs={{0,4},{4,8},{8,12},{12,16},{16,20},{20,24},{24,28},{28,32},{32,36}... | collective-permute-start | bytes 73736 | tf_op jit(solution)/shard_map/ppermute | solution.py:445
  56.0 15.2 %collective-permute-start.4 = (bf16[16,768]{1,0:T(8,128)(2,1)S(1)}, bf16[16,768]{1,0:T(8,128)(2,1)S(1)}, u32[]{:S(2)}, u32[]{:S(2)}) collective-permute-start(bf16[16,768]{1,0:T(8,128)(2,1)S(1)} %get-tuple-element.12), channel_id=1, source_target_pairs={{0,132},{4,136},{8,140},{12,144},{16,148},{20,152},{24,156},{28,16... | collective-permute-start | bytes 73736 | tf_op jit(solution)/shard_map/ppermute | solution.py:445
  59.9 11.2 %collective-permute-start.5 = (bf16[16,768]{1,0:T(8,128)(2,1)S(1)}, bf16[16,768]{1,0:T(8,128)(2,1)S(1)}, u32[]{:S(2)}, u32[]{:S(2)}) collective-permute-start(bf16[16,768]{1,0:T(8,128)(2,1)S(1)} %get-tuple-element.12), channel_id=1, source_target_pairs={{0,260},{4,264},{8,268},{12,272},{16,276},{20,280},{24,284},{28,28... | collective-permute-start | bytes 73736 | tf_op jit(solution)/shard_map/ppermute | solution.py:445
  69.2 5.1 %collective-permute-start.6 = (bf16[16,768]{1,0:T(8,128)(2,1)S(1)}, bf16[16,768]{1,0:T(8,128)(2,1)S(1)}, u32[]{:S(2)}, u32[]{:S(2)}) collective-permute-start(bf16[16,768]{1,0:T(8,128)(2,1)S(1)} %get-tuple-element.12), channel_id=1, source_target_pairs={{0,388},{4,392},{8,396},{12,400},{16,404},{20,408},{24,412},{28,41... | collective-permute-start | bytes 73736 | tf_op jit(solution)/shard_map/ppermute | solution.py:445
  74.4 1.3 %copy-start.1 = (bf16[16,48,768]{2,1,0:T(8,128)(2,1)S(1)}, bf16[16,48,768]{2,1,0:T(8,128)(2,1)}, u32[]{:S(2)}) copy-start(bf16[16,48,768]{2,1,0:T(8,128)(2,1)} %all-gather.3.cloned.1.call-done) | copy-start | bytes 3538948
Sparse Core Ops, SparseCore 0:
  22.0 45.8 all-gather.2

commit v6 on v5

--- a/solution.py
+++ b/solution.py
@@ -367,10 +367,7 @@
 def shrink(
     channel_ref,
     extra_ref,
-    above0_ref,
-    above1_ref,
-    above2_ref,
-    above3_ref,
+    above_ref,
     dual_ref,
     total_ref,
     filters_ref,
@@ -379,12 +376,13 @@
     own_ref,
     norm_ref,
 ):
-    above = (above0_ref, above1_ref, above2_ref, above3_ref)
     for k in range(4):
         channel = (channel_ref[0] + 4 - k) & 3
         for j in range(PART // HALO):
             window = pl.ds(HALO * j, 2 * HALO)
-            block = jnp.concatenate([above[k][:, window], extra_ref[channel, :, window]], 0)
+            block = jnp.concatenate(
+                [above_ref[channel, :, window], extra_ref[channel, :, window]], 0
+            )
             rows_ref[...] = jnp.dot(
                 block, filters_ref[0], preferred_element_type=jnp.float32
             ) + jnp.dot(block, filters_ref[1], preferred_element_type=jnp.float32)
@@ -418,7 +416,7 @@
     return pl.pallas_call(
         shrink,
         out_shape=jax.ShapeDtypeStruct((DP, 5, FR, PART), jnp.bfloat16),
-        in_specs=[SMEM_SPEC] + [VMEM_SPEC] * 8,
+        in_specs=[SMEM_SPEC] + [VMEM_SPEC] * 5,
         out_specs=VMEM_SPEC,
         scratch_shapes=[
             pltpu.VMEM((FR + TILE, 2 * HALO), jnp.float32),
@@ -427,22 +425,21 @@
         ],
         compiler_params=pltpu.CompilerParams(vmem_limit_bytes=VMEM_LIMIT),
         name="dual_columns",
-    )(channel, extra, *above, dual, total, filters)
-
-
-def copies(block, axis):
-    return lax.all_to_all(block, axis, 0, 0)
-
-
-def hop(block, distance, turn=0):
-    channels, facets = lax.axis_size("cube"), lax.axis_size("facet")
-    route = [
-        (c * facets + f - distance, (c + turn) % channels * facets + f)
-        for c in range(channels)
-        for f in range(facets)
-        if 0 <= f - distance < facets
-    ]
-    return lax.ppermute(block, ("cube", "facet"), route)
+    )(channel, extra, above, dual, total, filters)
+
+
+def exchange(parts, axis):
+    return lax.all_to_all(parts, axis, 0, 0)
+
+
+def gather(block, axis):
+    return exchange(jnp.broadcast_to(block, (lax.axis_size(axis),) + block.shape), axis)
+
+
+def hop(block, distance):
+    devices = range(lax.axis_size("facet"))
+    route = [(i - distance, i) for i in devices if i - distance in devices]
+    return lax.ppermute(block, "facet", route)
 
 
 def synthesize(dual):
@@ -465,23 +462,13 @@
     own_rows = image[0]
     payload_below = hop(payload[0], -1)
     left = position * PART
-    dual_slice = lax.dynamic_slice_in_dim(
-        jnp.pad(dual[:, 0], ((0, 0), (0, 0), (0, 128))), left, SPAN, 2
-    )
-    duals = lax.all_gather(dual_slice, "cube")
-
     numbers = jnp.concatenate([freq_start, tile_slot, jnp.broadcast_to(live, (1, BLK))], 0)
     meta = jnp.concatenate([vis_weight[0].T.astype(jnp.float32), numbers.astype(jnp.float32)], 0)
     meta_below = hop(meta, -1)
 
-    own_dual = lax.dynamic_slice_in_dim(
-        jnp.pad(dual[:, 0], ((0, 0), (0, 0), (HALO, 128))), left, SPAN + 128, 2
-    ).astype(jnp.float32)
-    old = lax.dynamic_slice_in_dim(jnp.pad(own_rows, ((0, 0), (HALO, 0))), left, SPAN, 1)
-    synth = synthesize(own_dual)
-    synth_below = hop(synth[:8], -1)
-
     spectra, own, order = own_spectra(numbers, meta[:TILE], payload[0], table, own_rows)
+    own_dual, order = lax.optimization_barrier((dual[:, 0], order))
+    duals = gather(lax.dynamic_slice_in_dim(own_dual, left, PART, 2), "cube")
     terms = gradient_parts(
         meta_below[TILE:].astype(jnp.int32),
         meta_below[:TILE],
@@ -491,14 +478,22 @@
         table,
         order,
     )
+    own_dual, own_rows, terms = lax.optimization_barrier((own_dual, own_rows, terms))
+    parts = exchange(terms, "dp")
+    dual_slice = lax.dynamic_slice_in_dim(
+        jnp.pad(own_dual, ((0, 0), (0, 0), (HALO, 128))), left, SPAN + 128, 2
+    ).astype(jnp.float32)
+    old = lax.dynamic_slice_in_dim(jnp.pad(own_rows, ((0, 0), (HALO, 0))), left, SPAN, 1)
+    synth = synthesize(dual_slice)
+    synth_below = hop(synth[:8], -1)
     synth = synth[8:] + jnp.pad(synth_below, ((FR - 8, 0), (0, 0)))
-    parts = copies(terms, "dp")
     extra_copies, last_rows, total = updated_columns(left[None], parts, synth, old)
-    extra = copies(extra_copies, "cube")
-    above = [hop(last_rows, 1, k) for k in range(4)]
+    above = hop(last_rows, 1)
+    extra = exchange(extra_copies, "cube")
+    above = gather(above, "cube")
     channel = lax.axis_index("cube")
     result = dual_columns(channel[None], extra, above, duals, total, filters)
-    whole = jnp.concatenate([part for part in copies(result, "dp")], -1)
+    whole = jnp.concatenate([part for part in exchange(result, "dp")], -1)
     dual_next = whole[:4]
     updated = jnp.maximum(own_rows - TAU_STEP * whole[4].astype(jnp.float32), 0.0)
     return (updated[None], dual_next[:, None])

time: 107 us -> 124 us (1.16); the launches traced: 107 us -> 122 us
  waiting for transfers between devices: 10.8 us -> 40.1 us
  starting transfers between devices: 42.6 us -> 27 us
  between operations: 15 us -> 1.45 us
  blocking collectives: 19.7 us -> 28.8 us
  local copies, waits for them, and re-layouts: 3.26 us -> 7.75 us
    all_to_all x2 -> x3, waiting for transfers between devices: 5.64 us -> 28.8 us  [exchange(): return lax.all_to_all(parts, axis, 0, 0)]
    ppermute x7 -> x4, starting transfers between devices: 33.7 us -> 14.8 us  [hop(): return lax.ppermute(block, 'facet', route)]
    all_to_all x1 -> x2, blocking collectives: 19.7 us -> 28.8 us  [exchange(): return lax.all_to_all(parts, axis, 0, 0)]
    ppermute x7 -> x4, waiting for transfers between devices: 5.18 us -> 11.2 us  [hop(): return lax.ppermute(block, 'facet', route)]
    unnamed x12 -> x16, local copies, waits for them, and re-layouts: 1.29 us -> 5.5 us
    all_to_all x2 -> x3, starting transfers between devices: 8.89 us -> 12.3 us  [exchange(): return lax.all_to_all(parts, axis, 0, 0)]
    convert_element_type x1 -> x2, other arithmetic: 0.06 us -> 1.76 us  [the longest x1 1.02 us: on_device(): dual_slice = lax.dynamic_slice_in_dim(jnp.pad(own_dual, ((0, 0), (0, 0),...]
  transfers between devices with their start and end apart: 10 -> 7, of which waited for: 3 -> 5; matrix products, arithmetic and copies ran while one was open for 3% -> 3% of each run, Pallas kernels for 7% -> 2%
where the time goes in v6:
time: 124 us; the launch traced here: 122 us
  waiting for transfers between devices  40.1 us (32%)
  blocking collectives  28.8 us (23%)
  starting transfers between devices  27 us (22%)
  Pallas kernels  10.7 us (9%)
  local copies, waits for them, and re-layouts  7.75 us (6%)
  other arithmetic  5.89 us (5%)
  between operations  1.45 us (1%)
    all_to_all x3, waiting for transfers between devices, exchange(): return lax.all_to_all(parts, axis, 0, 0)  28.8 us
    all_to_all x2, blocking collectives, exchange(): return lax.all_to_all(parts, axis, 0, 0)  28.8 us
    ppermute x4, starting transfers between devices, hop(): return lax.ppermute(block, 'facet', route)  14.8 us
    all_to_all x3, starting transfers between devices, exchange(): return lax.all_to_all(parts, axis, 0, 0)  12.3 us
    ppermute x4, waiting for transfers between devices, hop(): return lax.ppermute(block, 'facet', route)  11.2 us
    unnamed x16, local copies, waits for them, and re-layouts  5.5 us
    pallas_call x1, Pallas kernels, gradient_parts(): pl.pallas_call(below_pass, out_shape=jax.ShapeDtypeStruct((DP, FR, SPAN),...  4.56 us
    pallas_call x1, Pallas kernels, dual_columns(): pl.pallas_call(shrink, out_shape=jax.ShapeDtypeStruct((DP, 5, FR, PART),...  2.79 us
  transfers between devices with their start and end apart: 7, of which 5 were waited for; matrix products, arithmetic and copies ran while one was open for 3% of the time, Pallas kernels for 2%

profile of v6, /device:TPU:1, one launch (start us, length us, event | category | flops | bytes accessed | tf_op | source)
XLA Modules:
  0.0 121.7 jit_solution(3689813763946217711)
XLA Ops:
  1.3 0.7 convert_bitcast_fusion.weight_ref
  2.0 0.1 pad.32.clone
  2.0 0.7 fusion.65
  2.8 8.8 %collective-permute-start = (f32[19,64]{1,0:T(8,128)S(1)}, f32[19,64]{1,0:T(8,128)S(1)}, u32[]{:S(2)}, u32[]{:S(2)}) collective-permute-start(f32[19,64]{1,0:T(8,128)S(1)} %pad_maximum_fusion.3), channel_id=1, source_target_pairs={{4,0},{8,4},{12,8},{16,12},{20,16},{24,20},{28,24},{32,28},{36,32}... | collective-permute-start | bytes 14600 | tf_op jit(solution)/shard_map/ppermute | solution.py:442
  11.6 1.9 %collective-permute-start.1 = (bf16[64,16,128]{2,1,0:T(8,128)(2,1)}, bf16[64,16,128]{2,1,0:T(8,128)(2,1)S(1)}, u32[]{:S(2)}, u32[]{:S(2)}) collective-permute-start(bf16[64,16,128]{2,1,0:T(8,128)(2,1)} %bitcast.45), channel_id=1, source_target_pairs={{4,0},{8,4},{12,8},{16,12},{20,16},{24,20},{28,24},{32,28},{36,32}... | collective-permute-start | bytes 786440 | tf_op jit(solution)/shard_map/ppermute | solution.py:442
  13.5 0.0 copy-start
  13.5 1.0 copy-done
  14.5 0.0 copy-start.3
  14.5 0.9 copy-done.3
  15.5 0.0 copy-start.4
  15.5 1.3 %copy-done.4 = bf16[20,128,256]{2,1,0:T(8,128)(2,1)S(1)} copy-done((bf16[20,128,256]{2,1,0:T(8,128)(2,1)S(1)}, bf16[20,128,256]{2,1,0:T(8,128)(2,1)}, u32[]{:S(2)}) %copy-start.4) | copy-done | bytes 1310744
  16.8 0.0 copy-start.5
  16.8 2.5 %own_spectra.1 = (f32[41,48,128]{2,1,0:T(8,128)S(1)}, f32[41,48,128]{2,1,0:T(8,128)S(1)}, bf16[640,640]{1,0:T(8,128)(2,1)S(1)}) custom-call(s32[3,64]{1,0:T(4,128)S(1)} %get-tuple-element.35.numbers_ref, f32[16,64]{1,0:T(8,128)S(1)} %convert_bitcast_fusion.weight_ref, bf16[64,16,128]{2,1,0:T(8,128)(2,1)S(1)} %bitcast.46, ...), custom_call_target="tpu_custom_call" | custom-call | flops 2000000000 | bytes 4000000 | tf_op jit(solution)/shard_map/own_spectra/pallas_call | solution.py:299
  19.3 0.0 copy-start.6
  19.4 1.0 copy-done.6
  20.3 0.0 collective-permute-done
  20.3 3.2 %collective-permute-done.1.payload_ref = bf16[64,16,128]{2,1,0:T(8,128)(2,1)S(1)} collective-permute-done((bf16[64,16,128]{2,1,0:T(8,128)(2,1)}, bf16[64,16,128]{2,1,0:T(8,128)(2,1)S(1)}, u32[]{:S(2)}, u32[]{:S(2)}) %collective-permute-start.1) | collective-permute-done | bytes 262176 | tf_op jit(solution)/shard_map/ppermute | solution.py:442
  23.6 0.0 copy-done.5
  23.6 0.0 copy-start.7
  23.6 1.2 copy-done.7
  24.8 4.6 %gradient_parts.1 = bf16[4,48,768]{2,1,0:T(8,128)(2,1)} custom-call(s32[3,64]{1,0:T(4,128)S(1)} %slice_convert_fusion.numbers_ref, f32[16,64]{1,0:T(8,128)S(1)} %slice.261.weight_ref, bf16[64,16,128]{2,1,0:T(8,128)(2,1)S(1)} %collective-permute-done.1.payload_ref, f32[41,48,128]{2,1,0:T(8,128)S(1)} %get-tuple-element.15.spec_ref, ...), custom_call_target="tpu_custom_call" | custom-call | flops 2000000000 | bytes 4000000 | tf_op jit(solution)/shard_map/gradient_parts/pallas_call | solution.py:318
  29.3 3.5 %all-to-all-start = ((bf16[4,48,768]{2,1,0:T(8,128)(2,1)}), bf16[4,48,768]{2,1,0:T(8,128)(2,1)S(1)}, u32[]{:S(2)}, u32[]{:S(2)}) async-start(bf16[4,48,768]{2,1,0:T(8,128)(2,1)} %gradient_parts.1), calls=%async_computation | async-start | bytes 589824 | tf_op jit(solution)/shard_map/all_to_all | solution.py:432
  32.8 1.0 fusion.3
  33.9 0.6 fusion.50
  34.5 0.0 copy-start.1
  34.5 0.6 fusion.35
  35.1 0.3 fusion.19
  35.4 1.9 %collective-permute-start.2 = (f32[8,768]{1,0:T(8,128)S(1)}, f32[8,768]{1,0:T(8,128)S(1)}, u32[]{:S(2)}, u32[]{:S(2)}) collective-permute-start(f32[8,768]{1,0:T(8,128)S(1)} %slice.299), channel_id=1, source_target_pairs={{4,0},{8,4},{12,8},{16,12},{20,16},{24,20},{28,24},{32,28},{36,32}... | collective-permute-start | bytes 73736 | tf_op jit(solution)/shard_map/ppermute | solution.py:442
  37.4 0.0 copy-done.1
  37.4 7.1 %collective-permute-done.2 = f32[8,768]{1,0:T(8,128)S(1)} collective-permute-done((f32[8,768]{1,0:T(8,128)S(1)}, f32[8,768]{1,0:T(8,128)S(1)}, u32[]{:S(2)}, u32[]{:S(2)}) %collective-permute-start.2) | collective-permute-done | bytes 24608 | tf_op jit(solution)/shard_map/ppermute | solution.py:442
  44.5 0.0 all-to-all-done.parts_ref
  44.5 0.8 updated_columns.1
  45.3 2.1 %collective-permute-start.3 = (bf16[16,768]{1,0:T(8,128)(2,1)S(1)}, bf16[16,768]{1,0:T(8,128)(2,1)S(1)}, u32[]{:S(2)}, u32[]{:S(2)}) collective-permute-start(bf16[16,768]{1,0:T(8,128)(2,1)S(1)} %get-tuple-element.22), channel_id=1, source_target_pairs={{0,4},{4,8},{8,12},{12,16},{16,20},{20,24},{24,28},{28,32},{32,36}... | collective-permute-start | bytes 73736 | tf_op jit(solution)/shard_map/ppermute | solution.py:442
  47.5 0.9 collective-permute-done.3
  48.4 9.6 %all_to_all.25.above_ref = bf16[4,16,768]{2,1,0:T(8,128)(2,1)S(1)} all-to-all(bf16[4,16,768]{2,1,0:T(8,128)(2,1)S(1)} %broadcast_in_dim.29), channel_id=1, replica_groups=mesh['cube'=4,'facet'=32,'dp'=4] {'cube'}, dimensions={0} | all-to-all | bytes 196608 | tf_op jit(solution)/shard_map/all_to_all | solution.py:432
  58.0 3.5 %all-to-all-start.1 = ((bf16[4,48,768]{2,1,0:T(8,128)(2,1)}), bf16[4,48,768]{2,1,0:T(8,128)(2,1)S(1)}, u32[]{:S(2)}, u32[]{:S(2)}) async-start(bf16[4,48,768]{2,1,0:T(8,128)(2,1)} %get-tuple-element.21), calls=%async_computation.1 | async-start | bytes 589824 | tf_op jit(solution)/shard_map/all_to_all | solution.py:432
  61.5 1.0 constant_dynamic-slice_fusion
  62.5 0.0 copy-start.2
  62.5 5.0 %all-to-all-done.1.extra_ref = bf16[4,48,768]{2,1,0:T(8,128)(2,1)S(1)} async-done(((bf16[4,48,768]{2,1,0:T(8,128)(2,1)}), bf16[4,48,768]{2,1,0:T(8,128)(2,1)S(1)}, u32[]{:S(2)}, u32[]{:S(2)}) %all-to-all-start.1) | async-done | bytes 294944 | tf_op jit(solution)/shard_map/all_to_all | solution.py:432
  67.5 1.0 broadcast_in_dim.30
  68.5 5.4 %all-to-all-start.3 = ((bf16[4,4,48,640]{3,2,1,0:T(8,128)(2,1)}), bf16[4,4,48,640]{3,2,1,0:T(8,128)(2,1)S(1)}, u32[]{:S(2)}, u32[]{:S(2)}) async-start(bf16[4,4,48,640]{3,2,1,0:T(8,128)(2,1)} %broadcast_in_dim.30), calls=%async_computation.3 | async-start | bytes 1966080 | tf_op jit(solution)/shard_map/all_to_all | solution.py:432
  73.9 23.8 %all-to-all-done.3.dual_ref = bf16[4,4,48,640]{3,2,1,0:T(8,128)(2,1)S(1)} async-done(((bf16[4,4,48,640]{3,2,1,0:T(8,128)(2,1)}), bf16[4,4,48,640]{3,2,1,0:T(8,128)(2,1)S(1)}, u32[]{:S(2)}, u32[]{:S(2)}) %all-to-all-start.3) | async-done | bytes 983072 | tf_op jit(solution)/shard_map/all_to_all | solution.py:432
  97.7 0.0 copy-done.2
  97.7 2.8 %dual_columns.1 = bf16[4,5,48,640]{3,2,1,0:T(8,128)(2,1)S(1)} custom-call(s32[1]{0:T(128)} %bitcast.7.channel_ref, bf16[4,48,768]{2,1,0:T(8,128)(2,1)S(1)} %all-to-all-done.1.extra_ref, bf16[4,16,768]{2,1,0:T(8,128)(2,1)S(1)} %all_to_all.25.above_ref, bf16[4,4,48,640]{3,2,1,0:T(8,128)(2,1)S(1)} %all-to-all-done.3.dual_ref, ...), custom_call_target="tpu_custom_call" | custom-call | tf_op jit(solution)/shard_map/dual_columns/pallas_call | solution.py:416
  100.5 19.2 %all_to_all.26 = bf16[4,5,48,640]{3,2,1,0:T(8,128)(2,1)S(1)} all-to-all(bf16[4,5,48,640]{3,2,1,0:T(8,128)(2,1)S(1)} %dual_columns.1), channel_id=1, replica_groups=mesh['cube'=4,'facet'=32,'dp'=4] {'dp'}, dimensions={0} | all-to-all | bytes 2457600 | tf_op jit(solution)/shard_map/all_to_all | solution.py:432
  119.7 0.1 slice_bitcast_fusion.3
  119.8 0.9 fusion.2
  120.6 1.0 fusion
  (8 shorter events, 0.1 us)
Async XLA Ops:
  2.8 17.5 %collective-permute-start = (f32[19,64]{1,0:T(8,128)S(1)}, f32[19,64]{1,0:T(8,128)S(1)}, u32[]{:S(2)}, u32[]{:S(2)}) collective-permute-start(f32[19,64]{1,0:T(8,128)S(1)} %pad_maximum_fusion.3), channel_id=1, source_target_pairs={{4,0},{8,4},{12,8},{16,12},{20,16},{24,20},{28,24},{32,28},{36,32}... | collective-permute-start | bytes 14600 | tf_op jit(solution)/shard_map/ppermute | solution.py:442
  11.6 12.0 %collective-permute-start.1 = (bf16[64,16,128]{2,1,0:T(8,128)(2,1)}, bf16[64,16,128]{2,1,0:T(8,128)(2,1)S(1)}, u32[]{:S(2)}, u32[]{:S(2)}) collective-permute-start(bf16[64,16,128]{2,1,0:T(8,128)(2,1)} %bitcast.45), channel_id=1, source_target_pairs={{4,0},{8,4},{12,8},{16,12},{20,16},{24,20},{28,24},{32,28},{36,32}... | collective-permute-start | bytes 786440 | tf_op jit(solution)/shard_map/ppermute | solution.py:442
  13.5 1.0 copy-start
  14.5 0.9 copy-start.3
  15.5 1.3 %copy-start.4 = (bf16[20,128,256]{2,1,0:T(8,128)(2,1)S(1)}, bf16[20,128,256]{2,1,0:T(8,128)(2,1)}, u32[]{:S(2)}) copy-start(bf16[20,128,256]{2,1,0:T(8,128)(2,1)} %constant.17.clone.table_ref) | copy-start | bytes 3932164
  16.8 6.8 %copy-start.5 = (bf16[20,128,256]{2,1,0:T(8,128)(2,1)S(1)}, bf16[20,128,256]{2,1,0:T(8,128)(2,1)}, u32[]{:S(2)}) copy-start(bf16[20,128,256]{2,1,0:T(8,128)(2,1)} %constant.17.clone.table_ref) | copy-start | bytes 3932164
  19.3 1.0 copy-start.6
  23.6 1.2 copy-start.7
  29.3 15.2 %all-to-all-start = ((bf16[4,48,768]{2,1,0:T(8,128)(2,1)}), bf16[4,48,768]{2,1,0:T(8,128)(2,1)S(1)}, u32[]{:S(2)}, u32[]{:S(2)}) async-start(bf16[4,48,768]{2,1,0:T(8,128)(2,1)} %gradient_parts.1), calls=%async_computation | async-start | bytes 589824 | tf_op jit(solution)/shard_map/all_to_all | solution.py:432
  34.5 2.9 %copy-start.1 = (f32[1,48,2560]{2,1,0:T(8,128)S(1)}, f32[1,48,2560]{2,1,0:T(8,128)}, u32[]{:S(2)}) copy-start(f32[1,48,2560]{2,1,0:T(8,128)} %param.9) | copy-start | bytes 1474564
  35.4 9.1 %collective-permute-start.2 = (f32[8,768]{1,0:T(8,128)S(1)}, f32[8,768]{1,0:T(8,128)S(1)}, u32[]{:S(2)}, u32[]{:S(2)}) collective-permute-start(f32[8,768]{1,0:T(8,128)S(1)} %slice.299), channel_id=1, source_target_pairs={{4,0},{8,4},{12,8},{16,12},{20,16},{24,20},{28,24},{32,28},{36,32}... | collective-permute-start | bytes 73736 | tf_op jit(solution)/shard_map/ppermute | solution.py:442
  45.3 3.1 %collective-permute-start.3 = (bf16[16,768]{1,0:T(8,128)(2,1)S(1)}, bf16[16,768]{1,0:T(8,128)(2,1)S(1)}, u32[]{:S(2)}, u32[]{:S(2)}) collective-permute-start(bf16[16,768]{1,0:T(8,128)(2,1)S(1)} %get-tuple-element.22), channel_id=1, source_target_pairs={{0,4},{4,8},{8,12},{12,16},{16,20},{20,24},{24,28},{28,32},{32,36}... | collective-permute-start | bytes 73736 | tf_op jit(solution)/shard_map/ppermute | solution.py:442
  58.0 9.5 %all-to-all-start.1 = ((bf16[4,48,768]{2,1,0:T(8,128)(2,1)}), bf16[4,48,768]{2,1,0:T(8,128)(2,1)S(1)}, u32[]{:S(2)}, u32[]{:S(2)}) async-start(bf16[4,48,768]{2,1,0:T(8,128)(2,1)} %get-tuple-element.21), calls=%async_computation.1 | async-start | bytes 589824 | tf_op jit(solution)/shard_map/all_to_all | solution.py:432
  62.5 35.2 %copy-start.2 = (bf16[2,256,256]{2,1,0:T(8,128)(2,1)S(1)}, bf16[2,256,256]{2,1,0:T(8,128)(2,1)}, u32[]{:S(2)}) copy-start(bf16[2,256,256]{2,1,0:T(8,128)(2,1)} %constant.18.clone.filters_ref) | copy-start | bytes 786436
  68.5 29.2 %all-to-all-start.3 = ((bf16[4,4,48,640]{3,2,1,0:T(8,128)(2,1)}), bf16[4,4,48,640]{3,2,1,0:T(8,128)(2,1)S(1)}, u32[]{:S(2)}, u32[]{:S(2)}) async-start(bf16[4,4,48,640]{3,2,1,0:T(8,128)(2,1)} %broadcast_in_dim.30), calls=%async_computation.3 | async-start | bytes 1966080 | tf_op jit(solution)/shard_map/all_to_all | solution.py:432

commit v7 on v4

--- a/solution.py
+++ b/solution.py
@@ -46,6 +46,7 @@
 SPAN = PART + HALO
 CHUNKS = W // 64
 UNROLL = 4
+NUMBERS = SPAN + 2 * HALO
 VMEM_LIMIT = 24 * 1024 * 1024
 NORM = 1.0 / math.sqrt(W)
 C1, C2 = math.cos(2 * math.pi / 5), math.cos(4 * math.pi / 5)
@@ -57,6 +58,17 @@
     angles = (x[:, :, None] * np.arange(R)[None, None, :] % W) * (2.0 * math.pi / W)
     table = np.concatenate([np.cos(angles), -np.sin(angles)], -1).astype(jnp.bfloat16)
     return table
+
+
+def column_filters():
+    band = np.zeros((2 * HALO, 2 * HALO), np.float32)
+    for b, taps in enumerate((LOWPASS, HIGHPASS)):
+        for k in range(8):
+            j = np.arange(HALO)
+            band[HALO + j - k, HALO * b + j] = taps[k]
+    leading = band.astype(jnp.bfloat16)
+    rest = (band - leading.astype(np.float32)).astype(jnp.bfloat16)
+    return np.stack([leading, rest])
 
 
 def times_i(value, sign):
@@ -107,7 +119,7 @@
     return jnp.concatenate(tiles, 1).astype(jnp.bfloat16)
 
 
-def add_blocks(base, numbers_ref, weight_ref, payload_ref, spec_ref, grad_ref, list_ref):
+def add_blocks(base, numbers_ref, weights, payload_ref, spec_ref, grad_ref, list_ref):
     lane = lax.broadcasted_iota(jnp.int32, (1, 128), 1)
     half = lane & 63
 
@@ -119,9 +131,8 @@
     count = lax.fori_loop(0, numbers_ref[2, 0], collect, 0)
     for u in range(UNROLL):
         list_ref[count + u] = list_ref[0]
-    weights = weight_ref[...]
-    slot_lane = lax.broadcasted_iota(jnp.int32, (1, BLK), 1)
-    ones = jnp.ones((BLK, 128), jnp.bfloat16)
+    slot_lane = lax.broadcasted_iota(jnp.int32, (1, 128), 1)
+    ones = jnp.ones((128, 128), jnp.bfloat16)
 
     def blocks(step, carry):
         places = [step * UNROLL + u for u in range(UNROLL)]
@@ -176,7 +187,7 @@
 
     order_ref[...] = residue_order()
     stacked = jnp.concatenate(
-        [pixels_ref[:, PART * g : PART * (g + 1)] for g in range(4)], 0
+        [pixels_ref[:, PART * g : PART * (g + 1)].astype(jnp.bfloat16) for g in range(4)], 0
     )
     sorted_rows = jnp.dot(stacked, order_ref[...], preferred_element_type=jnp.float32)
     for j in range(5):
@@ -208,12 +219,14 @@
     lax.fori_loop(0, FR // 8, forward, 0)
     spec_ref[CHUNKS] = spec_ref[0]
     grad_ref[...] = jnp.zeros_like(grad_ref)
-    add_blocks(PER, numbers_ref, weight_ref, payload_ref, spec_ref, grad_ref, list_ref)
+    blank = jnp.zeros((TILE, 128 - BLK), jnp.float32)
+    weights = jnp.concatenate([weight_ref[...].astype(jnp.float32), blank], 1)
+    add_blocks(PER, numbers_ref, weights, payload_ref, spec_ref, grad_ref, list_ref)
 
 
 def below_pass(
     numbers_ref,
-    weight_ref,
+    mail_ref,
     payload_ref,
     spec_ref,
     own_ref,
@@ -230,7 +243,10 @@
     low = lane < 64
     quarter = lane >> 5
     grad_ref[...] = own_ref[...]
-    add_blocks(0, numbers_ref, weight_ref, payload_ref, spec_ref, grad_ref, list_ref)
+    weights = jnp.concatenate(
+        [mail_ref[:, SPAN : SPAN + HALO], mail_ref[:, SPAN + HALO : NUMBERS]], 0
+    )
+    add_blocks(0, numbers_ref, weights, payload_ref, spec_ref, grad_ref, list_ref)
     grad_ref[0] += grad_ref[CHUNKS]
 
     def backward(i, carry):
@@ -303,7 +319,7 @@
     )(numbers, weights, payload, table, pixels)
 
 
-def gradient_parts(numbers, weights, payload, spectra, own, table, order):
+def gradient_parts(numbers, mail, payload, spectra, own, table, order):
     return pl.pallas_call(
         below_pass,
         out_shape=jax.ShapeDtypeStruct((DP, FR, SPAN), jnp.bfloat16),
@@ -321,7 +337,65 @@
             flops=2 * 10**9, bytes_accessed=4 * 10**6, transcendentals=0
         ),
         name="gradient_parts",
-    )(numbers, weights, payload, spectra, own, table, order)
+    )(numbers, mail, payload, spectra, own, table, order)
+
+
+def prepare(
+    part_ref, numbers_ref, weight_ref, dual_ref, filters_ref, mail_ref, synth_ref, rows_ref
+):
+    part = part_ref[0]
+    for a, taps in enumerate((LOWPASS, HIGHPASS)):
+        rows_ref[a, :8] = jnp.zeros((8, SPAN), jnp.float32)
+        rows_ref[a, 8 + FR :] = jnp.zeros((8, SPAN), jnp.float32)
+        for j in range(SPAN // HALO + 1):
+            place = (PART // HALO) * part - 1 + j
+            inside = (place >= 0) & (place < W // HALO)
+            columns = pl.ds(pl.multiple_of(jnp.clip(place, 0, W // HALO - 1) * HALO, HALO), HALO)
+            pair = jnp.concatenate([dual_ref[2 * a + b, :, columns] for b in range(2)], 1)
+            across = sum(
+                lax.dot_general(
+                    pair,
+                    filters_ref[i],
+                    (((1,), (1,)), ((), ())),
+                    preferred_element_type=jnp.float32,
+                )
+                for i in range(2)
+            )
+            across = jnp.where(inside, across, 0.0)
+            if j > 0:
+                rows_ref[a, 8 : 8 + FR, HALO * (j - 1) : HALO * j] += across[:, :HALO]
+            if j < SPAN // HALO:
+                rows_ref[a, 8 : 8 + FR, HALO * j : HALO * (j + 1)] = across[:, HALO:]
+    for j in range(SPAN // HALO):
+        tile = pl.ds(HALO * j, HALO)
+        value = 0.0
+        for a, taps in enumerate((LOWPASS, HIGHPASS)):
+            for k in range(8):
+                value = value + taps[k] * rows_ref[a, k : k + FR + 8, tile]
+        mail_ref[:, tile] = value[:8]
+        synth_ref[:, tile] = value[8:]
+    blank = jnp.zeros((8, 128 - BLK), jnp.float32)
+    weights = weight_ref[...].astype(jnp.float32)
+    for i in range(2):
+        tile = pl.ds(SPAN + HALO * i, HALO)
+        mail_ref[:, tile] = jnp.concatenate([weights[8 * i : 8 * i + 8], blank], 1)
+    mail_ref[:, NUMBERS:] = jnp.zeros((8, HALO), jnp.float32)
+    mail_ref[:3, NUMBERS : NUMBERS + BLK] = numbers_ref[...].astype(jnp.float32)
+
+
+def prepared(part, numbers, weights, dual, filters):
+    return pl.pallas_call(
+        prepare,
+        out_shape=(
+            jax.ShapeDtypeStruct((8, NUMBERS + HALO), jnp.float32),
+            jax.ShapeDtypeStruct((FR, SPAN), jnp.float32),
+        ),
+        in_specs=[SMEM_SPEC] + [VMEM_SPEC] * 4,
+        out_specs=(VMEM_SPEC,) * 2,
+        scratch_shapes=[pltpu.VMEM((2, FR + 16, SPAN), jnp.float32)],
+        compiler_params=pltpu.CompilerParams(vmem_limit_bytes=VMEM_LIMIT),
+        name="prepared",
+    )(part, numbers, weights, dual, filters)
 
 
 def hop(block, distance):
@@ -333,19 +407,6 @@
 def gathered_sum(parts):
     mixed = lax.all_to_all(parts, "dp", 0, 0)
     return jnp.sum(mixed.astype(jnp.float32), 0)
-
-
-def synthesize(dual):
-    summed = jnp.zeros((FR + 8, SPAN), jnp.float32)
-    for a, row_taps in enumerate((LOWPASS, HIGHPASS)):
-        across = jnp.zeros((FR, SPAN), jnp.float32)
-        for b, col_taps in enumerate((LOWPASS, HIGHPASS)):
-            for k in range(8):
-                across = across + col_taps[k] * dual[2 * a + b][:, k : k + SPAN]
-        padded = jnp.pad(across, ((8, 7), (0, 0)))
-        for k in range(8):
-            summed = summed + row_taps[k] * padded[k : k + FR + 8]
-    return summed
 
 
 def analyze(extra):
@@ -363,42 +424,25 @@
     table = jnp.asarray(tables())
     position = lax.axis_index("dp")
     own_rows = image[0]
+    filters = jnp.asarray(column_filters())
     payload_below = hop(payload[0], -1)
-    meta = jnp.concatenate(
-        [
-            vis_weight[0].T.astype(jnp.float32),
-            freq_start.astype(jnp.float32),
-            tile_slot.astype(jnp.float32),
-            jnp.broadcast_to(live, (1, BLK)).astype(jnp.float32),
-        ],
-        0,
-    )
-    meta_below = hop(meta, -1)
     numbers = jnp.concatenate([freq_start, tile_slot, jnp.broadcast_to(live, (1, BLK))], 0)
-
     left = position * PART
-    own_dual = lax.dynamic_slice_in_dim(
-        jnp.pad(dual[:, 0], ((0, 0), (0, 0), (HALO, 128))), left, SPAN + 128, 2
-    ).astype(jnp.float32)
+    own_dual = lax.dynamic_slice_in_dim(dual[:, 0], left, PART, 2).astype(jnp.float32)
     old = lax.dynamic_slice_in_dim(
         jnp.pad(own_rows, ((0, 0), (HALO, 0))), left, SPAN, 1
     )
-    synth = synthesize(own_dual)
-    synth_below = hop(synth[:8], -1)
-
-    spectra, own, order = own_spectra(
-        numbers, meta[:TILE], payload[0], table, own_rows.astype(jnp.bfloat16)
+
+    weights = vis_weight[0].T
+    spectra, own, order = own_spectra(numbers, weights, payload[0], table, own_rows)
+    weights, order = lax.optimization_barrier((weights, order))
+    mail, synth = prepared(position[None], numbers, weights, dual[:, 0], filters)
+    mail_below = hop(mail, -1)
+    numbers_below = mail_below[:3, NUMBERS : NUMBERS + BLK].astype(jnp.int32)
+    terms = gradient_parts(
+        numbers_below, mail_below, payload_below, spectra, own, table, order
     )
-    terms = gradient_parts(
-        meta_below[TILE:].astype(jnp.int32),
-        meta_below[:TILE],
-        payload_below,
-        spectra,
-        own,
-        table,
-        order,
-    )
-    synth = synth[8:] + jnp.pad(synth_below, ((FR - 8, 0), (0, 0)))
+    synth = synth + jnp.pad(mail_below[:, :SPAN], ((FR - 8, 0), (0, 0)))
     total = gathered_sum(terms) + synth
     new = jnp.maximum(old - TAU_STEP * total, 0.0)
     column = lax.broadcasted_iota(jnp.int32, old.shape, 1) + left
@@ -406,7 +450,7 @@
     extra_above = hop(extra[FR - 8 :].astype(jnp.bfloat16), 1).astype(jnp.float32)
     extra = jnp.concatenate([extra_above, extra], 0)
 
-    shifted = own_dual[:, :, HALO : HALO + PART] + SIGMA_STEP * analyze(extra)
+    shifted = own_dual + SIGMA_STEP * analyze(extra)
     squares = lax.all_gather((shifted * shifted).astype(jnp.bfloat16), "cube")
     norms = jnp.sqrt(jnp.sum(squares.astype(jnp.float32), 0))
     dual_part = (shifted * (RADIUS / jnp.maximum(norms, RADIUS))).astype(jnp.bfloat16)

time: 92.2 us -> 95.5 us (1.036)
  the two profiles are of different devices: /device:TPU:32 before, /device:TPU:16 now
where the time goes in v7:
time: 95.5 us; the launch traced here: 95 us
  blocking collectives  32.1 us (34%)
  starting transfers between devices  22.7 us (24%)
  waiting for transfers between devices  16.3 us (17%)
  local copies, waits for them, and re-layouts  10.7 us (11%)
  Pallas kernels  7.62 us (8%)
  other arithmetic  4.04 us (4%)
  between operations  1.43 us (1%)
    all_gather x1, blocking collectives, on_device(): squares = lax.all_gather((shifted * shifted).astype(jnp.bfloat16), 'cube')  17.9 us
    ppermute x3, starting transfers between devices, hop(): return lax.ppermute(block, 'facet', route)  14.8 us
    all_to_all x1, blocking collectives, on_device(): lax.all_to_all(jnp.broadcast_to(own_part, (DP,) + own_part.shape), 'dp',...  14.3 us
    unnamed x30, local copies, waits for them, and re-layouts  10.4 us
    ppermute x3, waiting for transfers between devices, hop(): return lax.ppermute(block, 'facet', route)  9.49 us
    all_to_all x1, starting transfers between devices, gathered_sum(): mixed = lax.all_to_all(parts, 'dp', 0, 0)  7.97 us
    all_to_all x1, waiting for transfers between devices, gathered_sum(): mixed = lax.all_to_all(parts, 'dp', 0, 0)  6.84 us
    pallas_call x1, Pallas kernels, gradient_parts(): pl.pallas_call(below_pass, out_shape=jax.ShapeDtypeStruct((DP, FR, SPAN),...  3.84 us
  transfers between devices with their start and end apart: 4, of which 3 were waited for; matrix products, arithmetic and copies ran while one was open for 1% of the time, Pallas kernels for 4%

profile of v7, /device:TPU:16, one launch (start us, length us, event | category | flops | bytes accessed | tf_op | source)
XLA Modules:
  0.0 95.0 jit_solution(7848960666586887064)
XLA Ops:
  0.6 10.2 %collective-permute-start.1 = (bf16[64,16,128]{2,1,0:T(8,128)(2,1)}, bf16[64,16,128]{2,1,0:T(8,128)(2,1)S(1)}, u32[]{:S(2)}, u32[]{:S(2)}) collective-permute-start(bf16[64,16,128]{2,1,0:T(8,128)(2,1)} %bitcast.55), channel_id=1, source_target_pairs={{4,0},{8,4},{12,8},{16,12},{20,16},{24,20},{28,24},{32,28},{36,32}... | collective-permute-start | bytes 786440 | tf_op jit(solution)/shard_map/ppermute | solution.py:404
  11.5 0.1 pad.28.clone
  11.6 0.7 add_add_fusion.1.numbers_ref
  12.3 0.0 copy-start.1
  12.3 1.0 %copy-done.1 = f32[1,48,2560]{2,1,0:T(8,128)S(1)} copy-done((f32[1,48,2560]{2,1,0:T(8,128)S(1)}, f32[1,48,2560]{2,1,0:T(8,128)}, u32[]{:S(2)}) %copy-start.1) | copy-done | bytes 491544
  13.4 0.0 copy-start.4
  13.4 0.7 copy-done.4
  14.1 0.0 copy-start.6
  14.1 0.9 copy-done.6
  15.0 0.0 copy-start.7
  15.0 1.3 %copy-done.7 = bf16[20,128,256]{2,1,0:T(8,128)(2,1)S(1)} copy-done((bf16[20,128,256]{2,1,0:T(8,128)(2,1)S(1)}, bf16[20,128,256]{2,1,0:T(8,128)(2,1)}, u32[]{:S(2)}) %copy-start.7) | copy-done | bytes 1310744
  16.3 0.0 copy-start
  16.3 0.0 copy-start.3
  16.3 0.0 copy-start.5
  16.3 0.0 copy-start.8
  16.3 2.5 %own_spectra.1 = (f32[41,48,128]{2,1,0:T(8,128)S(1)}, f32[41,48,128]{2,1,0:T(8,128)S(1)}, bf16[640,640]{1,0:T(8,128)(2,1)S(1)}) custom-call(s32[3,64]{1,0:T(4,128)S(1)} %add_add_fusion.1.numbers_ref, bf16[16,64]{1,0:T(8,128)(2,1)S(1)} %bitcast.53, bf16[64,16,128]{2,1,0:T(8,128)(2,1)S(1)} %bitcast.56, bf16[20,128,256]{2,1,0:T(8,128)(2,1)S(1)} %copy-done.7, ...), custom_call_target="tpu_custom_call" | custom-call | flops 2000000000 | bytes 4000000 | tf_op jit(solution)/shard_map/own_spectra/pallas_call | solution.py:304
  18.9 0.0 copy-start.9
  18.9 1.0 %copy-done.9 = f32[41,48,128]{2,1,0:T(8,128)} copy-done((f32[41,48,128]{2,1,0:T(8,128)}, f32[41,48,128]{2,1,0:T(8,128)S(1)}, u32[]{:S(2)}) %copy-start.9) | copy-done | bytes 1007640
  19.9 0.0 copy-start.11
  19.9 1.0 %copy-done.11 = f32[41,48,128]{2,1,0:T(8,128)} copy-done((f32[41,48,128]{2,1,0:T(8,128)}, f32[41,48,128]{2,1,0:T(8,128)S(1)}, u32[]{:S(2)}) %copy-start.11) | copy-done | bytes 1007640
  20.8 0.0 copy-start.13
  20.8 0.9 copy-done.13
  21.7 0.0 copy-done
  21.7 0.0 copy-done.3
  21.7 0.0 copy-done.5
  21.7 1.2 %prepared.1 = (f32[8,1152]{1,0:T(8,128)S(1)}, f32[48,768]{1,0:T(8,128)S(1)}) custom-call(s32[1]{0:T(128)} %bitcast.3.part_ref, s32[3,64]{1,0:T(4,128)S(1)} %add_add_fusion.1.numbers_ref, bf16[16,64]{1,0:T(8,128)(2,1)S(1)} %bitcast.54, bf16[4,48,2560]{2,1,0:T(8,128)(2,1)S(1)} %bitcast.48, bf16[2,256,256]{2,1,0:T(8,128)(2,1)S(1)} %copy-done.3), custom_call_target="tpu_custom_call" | custom-call | tf_op jit(solution)/shard_map/prepared/pallas_call | solution.py:387
  23.0 2.6 %collective-permute-start = (f32[8,1152]{1,0:T(8,128)S(1)}, f32[8,1152]{1,0:T(8,128)S(1)}, u32[]{:S(2)}, u32[]{:S(2)}) collective-permute-start(f32[8,1152]{1,0:T(8,128)S(1)} %get-tuple-element.11), channel_id=1, source_target_pairs={{4,0},{8,4},{12,8},{16,12},{20,16},{24,20},{28,24},{32,28},{36,32}... | collective-permute-start | bytes 110600 | tf_op jit(solution)/shard_map/ppermute | solution.py:404
  25.6 1.6 %collective-permute-done.mail_ref = f32[8,1152]{1,0:T(8,128)S(1)} collective-permute-done((f32[8,1152]{1,0:T(8,128)S(1)}, f32[8,1152]{1,0:T(8,128)S(1)}, u32[]{:S(2)}, u32[]{:S(2)}) %collective-permute-start) | collective-permute-done | bytes 36896 | tf_op jit(solution)/shard_map/ppermute | solution.py:404
  27.2 0.0 collective-permute-done.1.payload_ref
  27.2 0.0 copy-done.8
  27.2 0.0 copy-start.10
  27.2 1.2 %copy-done.10 = f32[41,48,128]{2,1,0:T(8,128)S(1)} copy-done((f32[41,48,128]{2,1,0:T(8,128)S(1)}, f32[41,48,128]{2,1,0:T(8,128)}, u32[]{:S(2)}) %copy-start.10) | copy-done | bytes 1007640
  28.4 0.0 copy-start.12
  28.4 1.2 %copy-done.12 = f32[41,48,128]{2,1,0:T(8,128)S(1)} copy-done((f32[41,48,128]{2,1,0:T(8,128)S(1)}, f32[41,48,128]{2,1,0:T(8,128)}, u32[]{:S(2)}) %copy-start.12) | copy-done | bytes 1007640
  29.6 0.0 copy-start.14
  29.6 1.1 %copy-done.14 = bf16[640,640]{1,0:T(8,128)(2,1)S(1)} copy-done((bf16[640,640]{1,0:T(8,128)(2,1)S(1)}, bf16[640,640]{1,0:T(8,128)(2,1)}, u32[]{:S(2)}) %copy-start.14) | copy-done | bytes 819224
  30.8 3.8 %gradient_parts.1 = bf16[4,48,768]{2,1,0:T(8,128)(2,1)} custom-call(s32[3,64]{1,0:T(4,128)S(1)} %slice_convert_fusion.2.numbers_ref, f32[8,1152]{1,0:T(8,128)S(1)} %collective-permute-done.mail_ref, bf16[64,16,128]{2,1,0:T(8,128)(2,1)S(1)} %collective-permute-done.1.payload_ref, f32[41,48,128]{2,1,0:T(8,128)S(1)} %copy-done.10, ...), custom_call_target="tpu_custom_call" | custom-call | flops 2000000000 | bytes 4000000 | tf_op jit(solution)/shard_map/gradient_parts/pallas_call | solution.py:323
  34.6 0.0 copy-start.2
  34.6 8.0 %all-to-all-start = ((bf16[4,48,768]{2,1,0:T(8,128)(2,1)}), bf16[4,48,768]{2,1,0:T(8,128)(2,1)S(1)}, u32[]{:S(2)}, u32[]{:S(2)}) async-start(bf16[4,48,768]{2,1,0:T(8,128)(2,1)} %gradient_parts.1), calls=%async_computation | async-start | bytes 589824 | tf_op jit(solution)/shard_map/all_to_all | solution.py:408
  42.6 6.8 %all-to-all-done = bf16[4,48,768]{2,1,0:T(8,128)(2,1)S(1)} async-done(((bf16[4,48,768]{2,1,0:T(8,128)(2,1)}), bf16[4,48,768]{2,1,0:T(8,128)(2,1)S(1)}, u32[]{:S(2)}, u32[]{:S(2)}) %all-to-all-start) | async-done | bytes 294944 | tf_op jit(solution)/shard_map/all_to_all | solution.py:408
  49.5 0.0 copy-done.2
  49.5 0.1 subtract_select_fusion
  49.6 1.9 %collective-permute-start.2 = (bf16[8,768]{1,0:T(8,128)(2,1)S(1)}, bf16[8,768]{1,0:T(8,128)(2,1)S(1)}, u32[]{:S(2)}, u32[]{:S(2)}) collective-permute-start(bf16[8,768]{1,0:T(8,128)(2,1)S(1)} %slice.318), channel_id=1, source_target_pairs={{0,4},{4,8},{8,12},{12,16},{16,20},{20,24},{24,28},{28,32},{32,36}... | collective-permute-start | bytes 36872 | tf_op jit(solution)/shard_map/ppermute | solution.py:404
  51.5 7.9 %collective-permute-done.2 = bf16[8,768]{1,0:T(8,128)(2,1)S(1)} collective-permute-done((bf16[8,768]{1,0:T(8,128)(2,1)S(1)}, bf16[8,768]{1,0:T(8,128)(2,1)S(1)}, u32[]{:S(2)}, u32[]{:S(2)}) %collective-permute-start.2) | collective-permute-done | bytes 12320 | tf_op jit(solution)/shard_map/ppermute | solution.py:404
  59.4 0.2 multiply_add_fusion.1
  59.6 0.3 multiply_add_fusion.5
  59.9 0.3 multiply_add_fusion.3
  60.2 0.1 fusion.6
  60.3 17.9 %all_gather.4 = bf16[4,4,48,640]{3,2,1,0:T(8,128)(2,1)S(1)} all-gather(bf16[1,4,48,640]{3,2,1,0:T(8,128)(2,1)S(1)} %fusion.6), channel_id=1, replica_groups=mesh['cube'=4,'facet'=32,'dp'=4] {'cube'}, dimensions={0}, use_global_device_ids=true | all-gather | bytes 1228800 | tf_op jit(solution)/shard_map/all_gather | solution.py:454
  78.2 0.1 convert_reduce_fusion
  78.3 0.2 fusion.3
  78.6 0.1 broadcast_in_dim.23
  78.7 14.3 %all_to_all.10 = bf16[4,5,48,640]{3,2,1,0:T(8,128)(2,1)S(1)} all-to-all(bf16[4,5,48,640]{3,2,1,0:T(8,128)(2,1)S(1)} %broadcast_in_dim.23), channel_id=1, replica_groups=mesh['cube'=4,'facet'=32,'dp'=4] {'dp'}, dimensions={0} | all-to-all | bytes 2457600 | tf_op jit(solution)/shard_map/all_to_all | solution.py:458
  93.0 0.1 slice_bitcast_fusion.3
  93.1 1.0 %fusion = bf16[4,1,48,2560]{3,2,1,0:T(8,128)(2,1)} fusion(bf16[5,48,640]{2,1,0:T(8,128)(2,1)S(1)} %get-tuple-element.19, bf16[5,48,640]{2,1,0:T(8,128)(2,1)S(1)} %get-tuple-element.20, bf16[5,48,640]{2,1,0:T(8,128)(2,1)S(1)} %get-tuple-element.21, bf16[5,48,640]{2,1,0:T(8,128)(2,1)S(1)} %get-tuple-element.18), kind=kLoop, calls=%fused_computation.2 | loop fusion | flops 3932160 | bytes 2211840 | tf_op jit(solution)/shard_map/broadcast_in_dim | solution.py:462
  94.1 0.8 subtract_maximum_fusion
  (8 shorter events, 0.1 us)
Async XLA Ops:
  0.6 26.6 %collective-permute-start.1 = (bf16[64,16,128]{2,1,0:T(8,128)(2,1)}, bf16[64,16,128]{2,1,0:T(8,128)(2,1)S(1)}, u32[]{:S(2)}, u32[]{:S(2)}) collective-permute-start(bf16[64,16,128]{2,1,0:T(8,128)(2,1)} %bitcast.55), channel_id=1, source_target_pairs={{4,0},{8,4},{12,8},{16,12},{20,16},{24,20},{28,24},{32,28},{36,32}... | collective-permute-start | bytes 786440 | tf_op jit(solution)/shard_map/ppermute | solution.py:404
  12.3 1.0 %copy-start.1 = (f32[1,48,2560]{2,1,0:T(8,128)S(1)}, f32[1,48,2560]{2,1,0:T(8,128)}, u32[]{:S(2)}) copy-start(f32[1,48,2560]{2,1,0:T(8,128)} %param.9) | copy-start | bytes 1474564
  13.4 0.7 copy-start.4
  14.1 0.9 %copy-start.6 = (bf16[1,64,16,128]{3,2,1,0:T(8,128)(2,1)S(1)}, bf16[1,64,16,128]{3,2,1,0:T(8,128)(2,1)}, u32[]{:S(2)}) copy-start(bf16[1,64,16,128]{3,2,1,0:T(8,128)(2,1)} %param.11) | copy-start | bytes 786436
  15.0 1.3 %copy-start.7 = (bf16[20,128,256]{2,1,0:T(8,128)(2,1)S(1)}, bf16[20,128,256]{2,1,0:T(8,128)(2,1)}, u32[]{:S(2)}) copy-start(bf16[20,128,256]{2,1,0:T(8,128)(2,1)} %constant.10.clone.table_ref) | copy-start | bytes 3932164
  16.3 5.4 %copy-start = (bf16[4,1,48,2560]{3,2,1,0:T(8,128)(2,1)S(1)}, bf16[4,1,48,2560]{3,2,1,0:T(8,128)(2,1)}, u32[]{:S(2)}) copy-start(bf16[4,1,48,2560]{3,2,1,0:T(8,128)(2,1)} %param.10) | copy-start | bytes 2949124
  16.3 5.4 %copy-start.3 = (bf16[2,256,256]{2,1,0:T(8,128)(2,1)S(1)}, bf16[2,256,256]{2,1,0:T(8,128)(2,1)}, u32[]{:S(2)}) copy-start(bf16[2,256,256]{2,1,0:T(8,128)(2,1)} %constant.11.clone.filters_ref) | copy-start | bytes 786436
  16.3 5.4 %copy-start.5 = (bf16[1,64,16]{1,2,0:T(8,128)(2,1)S(1)}, bf16[1,64,16]{1,2,0:T(8,128)(2,1)}, u32[]{:S(2)}) copy-start(bf16[1,64,16]{1,2,0:T(8,128)(2,1)} %param.12) | copy-start | bytes 6148
  16.3 10.9 %copy-start.8 = (bf16[20,128,256]{2,1,0:T(8,128)(2,1)S(1)}, bf16[20,128,256]{2,1,0:T(8,128)(2,1)}, u32[]{:S(2)}) copy-start(bf16[20,128,256]{2,1,0:T(8,128)(2,1)} %constant.10.clone.table_ref) | copy-start | bytes 3932164
  18.9 1.0 %copy-start.9 = (f32[41,48,128]{2,1,0:T(8,128)}, f32[41,48,128]{2,1,0:T(8,128)S(1)}, u32[]{:S(2)}) copy-start(f32[41,48,128]{2,1,0:T(8,128)S(1)} %get-tuple-element.12.spec_ref) | copy-start | bytes 3022852
  19.9 1.0 %copy-start.11 = (f32[41,48,128]{2,1,0:T(8,128)}, f32[41,48,128]{2,1,0:T(8,128)S(1)}, u32[]{:S(2)}) copy-start(f32[41,48,128]{2,1,0:T(8,128)S(1)} %get-tuple-element.13.own_ref) | copy-start | bytes 3022852
  20.8 0.9 copy-start.13
  23.0 4.2 %collective-permute-start = (f32[8,1152]{1,0:T(8,128)S(1)}, f32[8,1152]{1,0:T(8,128)S(1)}, u32[]{:S(2)}, u32[]{:S(2)}) collective-permute-start(f32[8,1152]{1,0:T(8,128)S(1)} %get-tuple-element.11), channel_id=1, source_target_pairs={{4,0},{8,4},{12,8},{16,12},{20,16},{24,20},{28,24},{32,28},{36,32}... | collective-permute-start | bytes 110600 | tf_op jit(solution)/shard_map/ppermute | solution.py:404
  27.2 1.2 %copy-start.10 = (f32[41,48,128]{2,1,0:T(8,128)S(1)}, f32[41,48,128]{2,1,0:T(8,128)}, u32[]{:S(2)}) copy-start(f32[41,48,128]{2,1,0:T(8,128)} %copy-done.9) | copy-start | bytes 3022852
  28.4 1.2 %copy-start.12 = (f32[41,48,128]{2,1,0:T(8,128)S(1)}, f32[41,48,128]{2,1,0:T(8,128)}, u32[]{:S(2)}) copy-start(f32[41,48,128]{2,1,0:T(8,128)} %copy-done.11) | copy-start | bytes 3022852
  29.6 1.1 %copy-start.14 = (bf16[640,640]{1,0:T(8,128)(2,1)S(1)}, bf16[640,640]{1,0:T(8,128)(2,1)}, u32[]{:S(2)}) copy-start(bf16[640,640]{1,0:T(8,128)(2,1)} %copy-done.13) | copy-start | bytes 2457604
  34.6 14.9 %copy-start.2 = (f32[1,48,2560]{2,1,0:T(8,128)S(1)}, f32[1,48,2560]{2,1,0:T(8,128)}, u32[]{:S(2)}) copy-start(f32[1,48,2560]{2,1,0:T(8,128)} %param.9) | copy-start | bytes 1474564
  34.6 14.8 %all-to-all-start = ((bf16[4,48,768]{2,1,0:T(8,128)(2,1)}), bf16[4,48,768]{2,1,0:T(8,128)(2,1)S(1)}, u32[]{:S(2)}, u32[]{:S(2)}) async-start(bf16[4,48,768]{2,1,0:T(8,128)(2,1)} %gradient_parts.1), calls=%async_computation | async-start | bytes 589824 | tf_op jit(solution)/shard_map/all_to_all | solution.py:408
  49.6 9.8 %collective-permute-start.2 = (bf16[8,768]{1,0:T(8,128)(2,1)S(1)}, bf16[8,768]{1,0:T(8,128)(2,1)S(1)}, u32[]{:S(2)}, u32[]{:S(2)}) collective-permute-start(bf16[8,768]{1,0:T(8,128)(2,1)S(1)} %slice.318), channel_id=1, source_target_pairs={{0,4},{4,8},{8,12},{12,16},{16,20},{20,24},{24,28},{28,32},{32,36}... | collective-permute-start | bytes 36872 | tf_op jit(solution)/shard_map/ppermute | solution.py:404

commit v8 on v4

--- a/solution.py
+++ b/solution.py
@@ -46,7 +46,7 @@
 SPAN = PART + HALO
 CHUNKS = W // 64
 UNROLL = 4
-VMEM_LIMIT = 24 * 1024 * 1024
+VMEM_LIMIT = 60 * 1024 * 1024
 NORM = 1.0 / math.sqrt(W)
 C1, C2 = math.cos(2 * math.pi / 5), math.cos(4 * math.pi / 5)
 S1, S2 = math.sin(2 * math.pi / 5), math.sin(4 * math.pi / 5)
@@ -57,6 +57,21 @@
     angles = (x[:, :, None] * np.arange(R)[None, None, :] % W) * (2.0 * math.pi / W)
     table = np.concatenate([np.cos(angles), -np.sin(angles)], -1).astype(jnp.bfloat16)
     return table
+
+
+def constants():
+    return np.concatenate([tables().reshape(Q * R, 2 * R), column_filters().reshape(-1, 2 * HALO)])
+
+
+def column_filters():
+    band = np.zeros((2 * HALO, 2 * HALO), np.float32)
+    for b, taps in enumerate((LOWPASS, HIGHPASS)):
+        for k in range(8):
+            j = np.arange(HALO)
+            band[HALO + j - k, HALO * b + j] = taps[k]
+    leading = band.astype(jnp.bfloat16)
+    rest = (band - leading.astype(np.float32)).astype(jnp.bfloat16)
+    return np.stack([leading, rest])
 
 
 def times_i(value, sign):
@@ -107,21 +122,20 @@
     return jnp.concatenate(tiles, 1).astype(jnp.bfloat16)
 
 
-def add_blocks(base, numbers_ref, weight_ref, payload_ref, spec_ref, grad_ref, list_ref):
+def add_blocks(base, start, slot, live, weights, payload_ref, spec_ref, grad_ref, list_ref):
     lane = lax.broadcasted_iota(jnp.int32, (1, 128), 1)
     half = lane & 63
 
     def collect(b, count):
-        slot = numbers_ref[1, b] - base
+        place = slot(b) - base
         list_ref[count] = b
-        return count + jnp.where((slot >= 0) & (slot < PER), 1, 0)
-
-    count = lax.fori_loop(0, numbers_ref[2, 0], collect, 0)
+        return count + jnp.where((place >= 0) & (place < PER), 1, 0)
+
+    count = lax.fori_loop(0, live, collect, 0)
     for u in range(UNROLL):
         list_ref[count + u] = list_ref[0]
-    weights = weight_ref[...]
-    slot_lane = lax.broadcasted_iota(jnp.int32, (1, BLK), 1)
-    ones = jnp.ones((BLK, 128), jnp.bfloat16)
+    slot_lane = lax.broadcasted_iota(jnp.int32, (1, 128), 1)
+    ones = jnp.ones((128, 128), jnp.bfloat16)
 
     def blocks(step, carry):
         places = [step * UNROLL + u for u in range(UNROLL)]
@@ -135,11 +149,9 @@
         )
         found = []
         for u, b in enumerate(numbers):
-            start = numbers_ref[0, b]
-            slot = jnp.clip(numbers_ref[1, b] - base, 0, PER - 1)
-            chunk = start >> 6
-            offset = start & 63
-            rows = pl.ds(pl.multiple_of(slot * TILE, TILE), TILE)
+            chunk, offset = start(b)
+            tile = jnp.clip(slot(b) - base, 0, PER - 1)
+            rows = pl.ds(pl.multiple_of(tile * TILE, TILE), TILE)
             first = pltpu.roll(spec_ref[chunk, rows, :], (128 - offset) & 127, 1)
             second = pltpu.roll(spec_ref[chunk + 1, rows, :], 64 - offset, 1)
             model = jnp.where(half < 64 - offset, first, second)
@@ -157,28 +169,156 @@
     lax.fori_loop(0, (count + UNROLL - 1) // UNROLL, blocks, 0)
 
 
+def columns_back(part, rows, dual_ref, filters, rows_ref):
+    for a in range(2):
+        for j in range(SPAN // HALO + 1):
+            place = (PART // HALO) * part - 1 + j
+            inside = (place >= 0) & (place < W // HALO)
+            columns = pl.ds(pl.multiple_of(jnp.clip(place, 0, W // HALO - 1) * HALO, HALO), HALO)
+            pair = jnp.concatenate([dual_ref[2 * a + b, :rows, columns] for b in range(2)], 1)
+            across = sum(
+                lax.dot_general(
+                    pair,
+                    filters(i),
+                    (((1,), (1,)), ((), ())),
+                    preferred_element_type=jnp.float32,
+                )
+                for i in range(2)
+            )
+            across = jnp.where(inside, across, 0.0)
+            if j > 0:
+                rows_ref[a, 8 : 8 + rows, HALO * (j - 1) : HALO * j] += across[:, :HALO]
+            if j < SPAN // HALO:
+                rows_ref[a, 8 : 8 + rows, HALO * j : HALO * (j + 1)] = across[:, HALO:]
+
+
+def rows_back(first, count, tile, rows_ref):
+    value = 0.0
+    for a, taps in enumerate((LOWPASS, HIGHPASS)):
+        for k in range(8):
+            value = value + taps[k] * rows_ref[a, 8 + first + k : 8 + first + k + count, tile]
+    return value
+
+
+def write_message(
+    part_ref,
+    starts_hbm,
+    slots_hbm,
+    live_hbm,
+    weight_hbm,
+    payload_hbm,
+    dual_hbm,
+    filters_hbm,
+    out_ref,
+    starts_ref,
+    slots_ref,
+    live_ref,
+    weight_ref,
+    dual_ref,
+    filters_ref,
+    rows_ref,
+    sems,
+):
+    pairs = [
+        (dual_hbm.at[:, :TILE, :], dual_ref),
+        (filters_hbm.at[pl.ds(Q * R, 4 * HALO), :], filters_ref),
+        (starts_hbm, starts_ref),
+        (slots_hbm, slots_ref),
+        (live_hbm, live_ref),
+        (weight_hbm, weight_ref),
+        (payload_hbm, out_ref.at[pl.ds(0, BLK)]),
+    ]
+    copies = [pltpu.make_async_copy(s, d, sems.at[i]) for i, (s, d) in enumerate(pairs)]
+    for copy in copies:
+        copy.start()
+    rows_ref[:, :8, :] = jnp.zeros((2, 8, SPAN), jnp.float32)
+    copies[0].wait()
+    copies[1].wait()
+    columns_back(
+        part_ref[0],
+        TILE,
+        dual_ref,
+        lambda i: filters_ref[2 * HALO * i : 2 * HALO * (i + 1)],
+        rows_ref,
+    )
+    for i in range(SPAN // HALO // 2):
+        pair = [rows_back(-8, 8, pl.ds(HALO * (2 * i + j), HALO), rows_ref) for j in range(2)]
+        out_ref[BLK + 1 + i] = jnp.concatenate(pair, 0).astype(jnp.bfloat16)
+    for copy in copies[2:6]:
+        copy.wait()
+    row = lax.broadcasted_iota(jnp.int32, (TILE, BLK), 0)
+    starts = starts_ref[...]
+    numbers = jnp.where(row == 0, starts >> 6, starts & 63)
+    numbers = jnp.where(row == 2, slots_ref[...], numbers)
+    numbers = jnp.where(row == 3, live_ref[0, 0], numbers)
+    out_ref[BLK] = jnp.concatenate(
+        [weight_ref[...].astype(jnp.float32), numbers.astype(jnp.float32)], 1
+    ).astype(jnp.bfloat16)
+    copies[6].wait()
+
+
+def synthesis(part_ref, message_ref, dual_ref, constants_ref, synth_ref, rows_ref):
+    columns_back(
+        part_ref[0],
+        FR,
+        dual_ref,
+        lambda i: constants_ref[Q * R + 2 * HALO * i : Q * R + 2 * HALO * (i + 1)],
+        rows_ref,
+    )
+    rows_ref[:, 8 + FR :, :] = jnp.zeros((2, 8, SPAN), jnp.float32)
+    for j in range(SPAN // HALO):
+        tile = pl.ds(HALO * j, HALO)
+        synth_ref[:, tile] = rows_back(0, FR, tile, rows_ref)
+        below = message_ref[BLK + 1 + j // 2].astype(jnp.float32)
+        synth_ref[FR - 8 :, tile] += below[8 * (j % 2) : 8 * (j % 2) + 8]
+
+
 def own_pass(
-    numbers_ref,
+    starts_hbm,
+    slots_hbm,
+    live_hbm,
+    weight_hbm,
+    payload_hbm,
+    table_hbm,
+    pixels_hbm,
+    spec_ref,
+    grad_ref,
+    starts_ref,
+    slots_ref,
+    live_ref,
+    list_ref,
     weight_ref,
     payload_ref,
     table_ref,
     pixels_ref,
-    spec_ref,
-    grad_ref,
     order_ref,
-    list_ref,
     re_ref,
     im_ref,
+    sems,
 ):
+    pairs = [
+        (pixels_hbm, pixels_ref),
+        (table_hbm.at[pl.ds(0, Q * R), :], table_ref),
+        (weight_hbm, weight_ref),
+        (payload_hbm, payload_ref),
+        (starts_hbm, starts_ref),
+        (slots_hbm, slots_ref),
+        (live_hbm, live_ref),
+    ]
+    copies = [pltpu.make_async_copy(s, d, sems.at[i]) for i, (s, d) in enumerate(pairs)]
+    for copy in copies:
+        copy.start()
     lane = lax.broadcasted_iota(jnp.int32, (1, 128), 1)
     low = lane < 64
     quarter = lane >> 5
 
     order_ref[...] = residue_order()
+    copies[0].wait()
     stacked = jnp.concatenate(
-        [pixels_ref[:, PART * g : PART * (g + 1)] for g in range(4)], 0
+        [pixels_ref[:, PART * g : PART * (g + 1)].astype(jnp.bfloat16) for g in range(4)], 0
     )
     sorted_rows = jnp.dot(stacked, order_ref[...], preferred_element_type=jnp.float32)
+    copies[1].wait()
     for j in range(5):
         tiles = [sorted_rows[FR * g : FR * (g + 1), 128 * j : 128 * (j + 1)] for g in range(4)]
         for p in range(4):
@@ -191,7 +331,9 @@
                 rows = jnp.where(quarter == g, turned[g], rows)
             q = 4 * j + p
             partial = jnp.dot(
-                rows.astype(jnp.bfloat16), table_ref[q], preferred_element_type=jnp.float32
+                rows.astype(jnp.bfloat16),
+                table_ref[R * q : R * (q + 1)],
+                preferred_element_type=jnp.float32,
             )
             re_ref[q] = partial[:, :R]
             im_ref[q] = partial[:, R:]
@@ -208,29 +350,63 @@
     lax.fori_loop(0, FR // 8, forward, 0)
     spec_ref[CHUNKS] = spec_ref[0]
     grad_ref[...] = jnp.zeros_like(grad_ref)
-    add_blocks(PER, numbers_ref, weight_ref, payload_ref, spec_ref, grad_ref, list_ref)
+    for copy in copies[2:]:
+        copy.wait()
+    blank = jnp.zeros((TILE, 128 - BLK), jnp.float32)
+    weights = jnp.concatenate([weight_ref[...].astype(jnp.float32), blank], 1)
+    add_blocks(
+        PER,
+        lambda b: (starts_ref[0, b] >> 6, starts_ref[0, b] & 63),
+        lambda b: slots_ref[0, b],
+        live_ref[0, 0],
+        weights,
+        payload_ref,
+        spec_ref,
+        grad_ref,
+        list_ref,
+    )
 
 
 def below_pass(
-    numbers_ref,
-    weight_ref,
-    payload_ref,
+    message_ref,
     spec_ref,
     own_ref,
+    table_hbm,
+    out_ref,
+    list_ref,
+    numbers_ref,
+    vector_ref,
     table_ref,
     order_ref,
-    out_ref,
-    list_ref,
     re_ref,
     im_ref,
     grad_ref,
     tile_ref,
+    sems,
 ):
+    copy = pltpu.make_async_copy(table_hbm.at[pl.ds(0, Q * R), :], table_ref, sems.at[0])
+    copy.start()
+    meta = message_ref[BLK].astype(jnp.float32)
+    vector_ref[...] = meta[:8].astype(jnp.int32)
+    read = pltpu.make_async_copy(vector_ref, numbers_ref, sems.at[1])
+    read.start()
     lane = lax.broadcasted_iota(jnp.int32, (1, 128), 1)
     low = lane < 64
     quarter = lane >> 5
     grad_ref[...] = own_ref[...]
-    add_blocks(0, numbers_ref, weight_ref, payload_ref, spec_ref, grad_ref, list_ref)
+    order_ref[...] = residue_order()
+    read.wait()
+    add_blocks(
+        0,
+        lambda b: (numbers_ref[0, BLK + b], numbers_ref[1, BLK + b]),
+        lambda b: numbers_ref[2, BLK + b],
+        numbers_ref[3, BLK],
+        jnp.where(low, meta, 0.0),
+        message_ref,
+        spec_ref,
+        grad_ref,
+        list_ref,
+    )
     grad_ref[0] += grad_ref[CHUNKS]
 
     def backward(i, carry):
@@ -250,13 +426,17 @@
         return carry
 
     lax.fori_loop(0, FR // 8, backward, 0)
+    copy.wait()
     for j in range(5):
         places = [[] for _ in range(4)]
         for p in range(4):
             q = 4 * j + p
             pair = jnp.concatenate([re_ref[q], im_ref[q]], 1).astype(jnp.bfloat16)
             rows = lax.dot_general(
-                pair, table_ref[q], (((1,), (1,)), ((), ())), preferred_element_type=jnp.float32
+                pair,
+                table_ref[R * q : R * (q + 1)],
+                (((1,), (1,)), ((), ())),
+                preferred_element_type=jnp.float32,
             )
             for g in range(4):
                 places[g].append(rows if g == p else pltpu.roll(rows, (32 * (p - g)) % 128, 1))
@@ -279,49 +459,98 @@
             out_ref[g + 1, :, :HALO] = rows[:, PART - HALO :]
 
 
+HBM_SPEC = pl.BlockSpec(memory_space=pltpu.HBM)
 SMEM_SPEC = pl.BlockSpec(memory_space=pltpu.SMEM)
 VMEM_SPEC = pl.BlockSpec(memory_space=pltpu.VMEM)
 SPECTRA = jax.ShapeDtypeStruct((CHUNKS + 1, FR, 128), jnp.float32)
 
 
-def own_spectra(numbers, weights, payload, table, pixels):
+TABLE = pltpu.VMEM((Q * R, 2 * R), jnp.bfloat16)
+PARAMS = pltpu.CompilerParams(vmem_limit_bytes=VMEM_LIMIT)
+COST = pl.CostEstimate(flops=2 * 10**9, bytes_accessed=4 * 10**6, transcendentals=0)
+
+
+def message(part, starts, slots, live, weights, payload, dual, table):
+    return pl.pallas_call(
+        write_message,
+        out_shape=jax.ShapeDtypeStruct((BLK + 1 + SPAN // HALO // 2, TILE, 128), jnp.bfloat16),
+        in_specs=[SMEM_SPEC] + [HBM_SPEC] * 7,
+        out_specs=VMEM_SPEC,
+        scratch_shapes=[
+            pltpu.VMEM((1, BLK), jnp.int32),
+            pltpu.VMEM((1, BLK), jnp.int32),
+            pltpu.SMEM((1, 1), jnp.int32),
+            pltpu.VMEM((TILE, BLK), jnp.bfloat16),
+            pltpu.VMEM((4, TILE, W), jnp.bfloat16),
+            pltpu.VMEM((4 * HALO, 2 * HALO), jnp.bfloat16),
+            pltpu.VMEM((2, 8 + TILE, SPAN), jnp.float32),
+            pltpu.SemaphoreType.DMA((7,)),
+        ],
+        compiler_params=PARAMS,
+        name="message",
+    )(part, starts, slots, live, weights, payload, dual, table)
+
+
+def synthesized(part, received, dual, table):
+    return pl.pallas_call(
+        synthesis,
+        out_shape=jax.ShapeDtypeStruct((FR, SPAN), jnp.float32),
+        in_specs=[SMEM_SPEC] + [VMEM_SPEC] * 3,
+        out_specs=VMEM_SPEC,
+        scratch_shapes=[pltpu.VMEM((2, FR + 16, SPAN), jnp.float32)],
+        compiler_params=pltpu.CompilerParams(vmem_limit_bytes=16 * 1024 * 1024),
+        name="synthesized",
+    )(part, received, dual, table)
+
+
+def own_spectra(starts, slots, live, weights, payload, table, pixels):
     return pl.pallas_call(
         own_pass,
-        out_shape=(SPECTRA, SPECTRA, jax.ShapeDtypeStruct((PART, PART), jnp.bfloat16)),
-        in_specs=[SMEM_SPEC] + [VMEM_SPEC] * 4,
-        out_specs=(VMEM_SPEC,) * 3,
+        out_shape=(SPECTRA, SPECTRA),
+        in_specs=[HBM_SPEC] * 7,
+        out_specs=(VMEM_SPEC,) * 2,
         scratch_shapes=[
+            pltpu.SMEM((1, BLK), jnp.int32),
+            pltpu.SMEM((1, BLK), jnp.int32),
+            pltpu.SMEM((1, 1), jnp.int32),
             pltpu.SMEM((BLK + UNROLL,), jnp.int32),
+            pltpu.VMEM((TILE, BLK), jnp.bfloat16),
+            pltpu.VMEM((BLK, TILE, 128), jnp.bfloat16),
+            TABLE,
+            pltpu.VMEM((FR, W), jnp.float32),
+            pltpu.VMEM((PART, PART), jnp.bfloat16),
             pltpu.VMEM((Q, FR, R), jnp.float32),
             pltpu.VMEM((Q, FR, R), jnp.float32),
+            pltpu.SemaphoreType.DMA((7,)),
         ],
-        compiler_params=pltpu.CompilerParams(vmem_limit_bytes=VMEM_LIMIT),
-        cost_estimate=pl.CostEstimate(
-            flops=2 * 10**9, bytes_accessed=4 * 10**6, transcendentals=0
-        ),
+        compiler_params=PARAMS,
+        cost_estimate=COST,
         name="own_spectra",
-    )(numbers, weights, payload, table, pixels)
-
-
-def gradient_parts(numbers, weights, payload, spectra, own, table, order):
+    )(starts, slots, live, weights, payload, table, pixels)
+
+
+def gradient_parts(received, spectra, own, table):
     return pl.pallas_call(
         below_pass,
         out_shape=jax.ShapeDtypeStruct((DP, FR, SPAN), jnp.bfloat16),
-        in_specs=[SMEM_SPEC] + [VMEM_SPEC] * 6,
+        in_specs=[VMEM_SPEC] * 3 + [HBM_SPEC],
         out_specs=VMEM_SPEC,
         scratch_shapes=[
             pltpu.SMEM((BLK + UNROLL,), jnp.int32),
+            pltpu.SMEM((8, 128), jnp.int32),
+            pltpu.VMEM((8, 128), jnp.int32),
+            TABLE,
+            pltpu.VMEM((PART, PART), jnp.bfloat16),
             pltpu.VMEM((Q, FR, R), jnp.float32),
             pltpu.VMEM((Q, FR, R), jnp.float32),
             pltpu.VMEM((CHUNKS + 1, FR, 128), jnp.float32),
             pltpu.VMEM((Q, FR, R), jnp.float32),
+            pltpu.SemaphoreType.DMA((2,)),
         ],
-        compiler_params=pltpu.CompilerParams(vmem_limit_bytes=VMEM_LIMIT),
-        cost_estimate=pl.CostEstimate(
-            flops=2 * 10**9, bytes_accessed=4 * 10**6, transcendentals=0
-        ),
+        compiler_params=PARAMS,
+        cost_estimate=COST,
         name="gradient_parts",
-    )(numbers, weights, payload, spectra, own, table, order)
+    )(received, spectra, own, table)
 
 
 def hop(block, distance):
@@ -333,19 +562,6 @@
 def gathered_sum(parts):
     mixed = lax.all_to_all(parts, "dp", 0, 0)
     return jnp.sum(mixed.astype(jnp.float32), 0)
-
-
-def synthesize(dual):
-    summed = jnp.zeros((FR + 8, SPAN), jnp.float32)
-    for a, row_taps in enumerate((LOWPASS, HIGHPASS)):
-        across = jnp.zeros((FR, SPAN), jnp.float32)
-        for b, col_taps in enumerate((LOWPASS, HIGHPASS)):
-            for k in range(8):
-                across = across + col_taps[k] * dual[2 * a + b][:, k : k + SPAN]
-        padded = jnp.pad(across, ((8, 7), (0, 0)))
-        for k in range(8):
-            summed = summed + row_taps[k] * padded[k : k + FR + 8]
-    return summed
 
 
 def analyze(extra):
@@ -360,45 +576,27 @@
 
 
 def on_device(image, dual, payload, vis_weight, freq_start, tile_slot, live):
-    table = jnp.asarray(tables())
+    table = jnp.asarray(constants())
     position = lax.axis_index("dp")
     own_rows = image[0]
-    payload_below = hop(payload[0], -1)
-    meta = jnp.concatenate(
-        [
-            vis_weight[0].T.astype(jnp.float32),
-            freq_start.astype(jnp.float32),
-            tile_slot.astype(jnp.float32),
-            jnp.broadcast_to(live, (1, BLK)).astype(jnp.float32),
-        ],
-        0,
-    )
-    meta_below = hop(meta, -1)
-    numbers = jnp.concatenate([freq_start, tile_slot, jnp.broadcast_to(live, (1, BLK))], 0)
+    part = position[None]
+    weights = vis_weight[0].T
+    received = hop(
+        message(part, freq_start, tile_slot, live, weights, payload[0], dual[:, 0], table), -1
+    )
 
     left = position * PART
-    own_dual = lax.dynamic_slice_in_dim(
-        jnp.pad(dual[:, 0], ((0, 0), (0, 0), (HALO, 128))), left, SPAN + 128, 2
-    ).astype(jnp.float32)
+    own_dual = lax.dynamic_slice_in_dim(dual[:, 0], left, PART, 2).astype(jnp.float32)
     old = lax.dynamic_slice_in_dim(
         jnp.pad(own_rows, ((0, 0), (HALO, 0))), left, SPAN, 1
     )
-    synth = synthesize(own_dual)
-    synth_below = hop(synth[:8], -1)
-
-    spectra, own, order = own_spectra(
-        numbers, meta[:TILE], payload[0], table, own_rows.astype(jnp.bfloat16)
-    )
-    terms = gradient_parts(
-        meta_below[TILE:].astype(jnp.int32),
-        meta_below[:TILE],
-        payload_below,
-        spectra,
-        own,
-        table,
-        order,
-    )
-    synth = synth[8:] + jnp.pad(synth_below, ((FR - 8, 0), (0, 0)))
+
+    spectra, own = own_spectra(
+        freq_start, tile_slot, live, weights, payload[0], table, own_rows
+    )
+    terms = gradient_parts(received, spectra, own, table)
+    terms, received = lax.optimization_barrier((terms, received))
+    synth = synthesized(part, received, dual[:, 0], table)
     total = gathered_sum(terms) + synth
     new = jnp.maximum(old - TAU_STEP * total, 0.0)
     column = lax.broadcasted_iota(jnp.int32, old.shape, 1) + left
@@ -406,7 +604,7 @@
     extra_above = hop(extra[FR - 8 :].astype(jnp.bfloat16), 1).astype(jnp.float32)
     extra = jnp.concatenate([extra_above, extra], 0)
 
-    shifted = own_dual[:, :, HALO : HALO + PART] + SIGMA_STEP * analyze(extra)
+    shifted = own_dual + SIGMA_STEP * analyze(extra)
     squares = lax.all_gather((shifted * shifted).astype(jnp.bfloat16), "cube")
     norms = jnp.sqrt(jnp.sum(squares.astype(jnp.float32), 0))
     dual_part = (shifted * (RADIUS / jnp.maximum(norms, RADIUS))).astype(jnp.bfloat16)

time: 92.2 us -> 88.5 us (0.960)
  the two profiles are of different devices: /device:TPU:32 before, /device:TPU:40 now
where the time goes in v8:
time: 88.5 us; the launch traced here: 88.1 us
  blocking collectives  35.6 us (40%)
  starting transfers between devices  19.5 us (22%)
  Pallas kernels  13.9 us (16%)
  waiting for transfers between devices  12.5 us (14%)
  other arithmetic  3.3 us (4%)
  local copies, waits for them, and re-layouts  1.88 us (2%)
  between operations  1.44 us (2%)
    all_gather x1, blocking collectives, on_device(): squares = lax.all_gather((shifted * shifted).astype(jnp.bfloat16), 'cube')  21.4 us
    all_to_all x1, blocking collectives, on_device(): lax.all_to_all(jnp.broadcast_to(own_part, (DP,) + own_part.shape), 'dp',...  14.3 us
    ppermute x2, starting transfers between devices, hop(): return lax.ppermute(block, 'facet', route)  13.1 us
    ppermute x2, waiting for transfers between devices, hop(): return lax.ppermute(block, 'facet', route)  7.88 us
    all_to_all x1, starting transfers between devices, gathered_sum(): mixed = lax.all_to_all(parts, 'dp', 0, 0)  6.41 us
    pallas_call x1, Pallas kernels, gradient_parts(): pl.pallas_call(below_pass, out_shape=jax.ShapeDtypeStruct((DP, FR, SPAN),...  5.23 us
    all_to_all x1, waiting for transfers between devices, gathered_sum(): mixed = lax.all_to_all(parts, 'dp', 0, 0)  4.63 us
    pallas_call x1, Pallas kernels, own_spectra(): pl.pallas_call(own_pass, out_shape=(SPECTRA, SPECTRA), in_specs=[HBM_SPEC...  4.41 us
  transfers between devices with their start and end apart: 3, of which 2 were waited for; matrix products, arithmetic and copies ran while one was open for 0% of the time, Pallas kernels for 6%

profile of v8, /device:TPU:40, one launch (start us, length us, event | category | flops | bytes accessed | tf_op | source)
XLA Modules:
  0.0 88.1 jit_solution(2029568998773786263)
XLA Ops:
  1.3 3.0 %message.1 = bf16[68,16,128]{2,1,0:T(8,128)(2,1)} custom-call(s32[1]{0:T(128)} %bitcast.3.part_ref, s32[1,64]{1,0:T(1,128)} %starts_hbm.3, s32[1,64]{1,0:T(1,128)} %slots_hbm.3, s32[1,1]{1,0:T(1,128)S(6)} %copy.12.live_hbm, bf16[16,64]{1,0:T(8,128)(2,1)} %bitcast.60, bf16[64,16,128]{2,1,0:T(8,128)(2,1)} %bitcast.58, bf16[4,48,2560]{2,1,0:T(8,128)(2,1)} %bitcast.44, ...), custom_call_target="tpu_custom_call" | custom-call | tf_op jit(solution)/shard_map/message/pallas_call | solution.py:474
  4.3 11.1 %collective-permute-start = (bf16[68,16,128]{2,1,0:T(8,128)(2,1)}, bf16[68,16,128]{2,1,0:T(8,128)(2,1)S(1)}, u32[]{:S(2)}, u32[]{:S(2)}) collective-permute-start(bf16[68,16,128]{2,1,0:T(8,128)(2,1)} %message.1), channel_id=1, source_target_pairs={{4,0},{8,4},{12,8},{16,12},{20,16},{24,20},{28,24},{32,28},{36,32}... | collective-permute-start | bytes 835592 | tf_op jit(solution)/shard_map/ppermute | solution.py:559
  15.4 4.4 %own_spectra.1 = (f32[41,48,128]{2,1,0:T(8,128)}, f32[41,48,128]{2,1,0:T(8,128)}) custom-call(s32[1,64]{1,0:T(1,128)} %starts_hbm.3, s32[1,64]{1,0:T(1,128)} %slots_hbm.3, s32[1,1]{1,0:T(1,128)S(6)} %copy.12.live_hbm, bf16[16,64]{1,0:T(8,128)(2,1)} %bitcast.61, bf16[64,16,128]{2,1,0:T(8,128)(2,1)} %bitcast.59, ...), custom_call_target="tpu_custom_call" | custom-call | flops 2000000000 | bytes 4000000 | tf_op jit(solution)/shard_map/own_spectra/pallas_call | solution.py:507
  19.9 0.0 collective-permute-done.message_ref
  19.9 0.0 copy-start.2
  19.9 0.7 copy-done.2
  20.6 0.0 copy-start
  20.6 0.0 copy-start.1
  20.6 5.2 %gradient_parts.1 = bf16[4,48,768]{2,1,0:T(8,128)(2,1)} custom-call(bf16[68,16,128]{2,1,0:T(8,128)(2,1)} %copy-done.2, f32[41,48,128]{2,1,0:T(8,128)} %get-tuple-element.6.spec_ref, f32[41,48,128]{2,1,0:T(8,128)} %get-tuple-element.7.own_ref, bf16[3072,256]{1,0:T(8,128)(2,1)} %constant.9.clone.filters_hbm.table_hbm.constants_ref), custom_call_target="tpu_custom_call" | custom-call | flops 2000000000 | bytes 4000000 | tf_op jit(solution)/shard_map/gradient_parts/pallas_call | solution.py:533
  25.8 6.4 %all-to-all-start = ((bf16[4,48,768]{2,1,0:T(8,128)(2,1)}), bf16[4,48,768]{2,1,0:T(8,128)(2,1)S(1)}, u32[]{:S(2)}, u32[]{:S(2)}) async-start(bf16[4,48,768]{2,1,0:T(8,128)(2,1)} %gradient_parts.1), calls=%async_computation | async-start | bytes 589824 | tf_op jit(solution)/shard_map/all_to_all | solution.py:563
  32.2 0.0 copy-done
  32.2 0.0 copy-done.1
  32.3 0.0 copy-start.3
  32.3 0.9 %copy-done.3 = bf16[68,16,128]{2,1,0:T(8,128)(2,1)S(1)} copy-done((bf16[68,16,128]{2,1,0:T(8,128)(2,1)S(1)}, bf16[68,16,128]{2,1,0:T(8,128)(2,1)}, u32[]{:S(2)}) %copy-start.3) | copy-done | bytes 278552
  33.2 0.0 copy-start.4
  33.2 1.2 %synthesized.1 = f32[48,768]{1,0:T(8,128)S(1)} custom-call(s32[1]{0:T(128)} %bitcast.3.part_ref, bf16[68,16,128]{2,1,0:T(8,128)(2,1)S(1)} %copy-done.3, bf16[4,48,2560]{2,1,0:T(8,128)(2,1)S(1)} %bitcast.45, bf16[3072,256]{1,0:T(8,128)(2,1)S(1)} %copy-done), custom_call_target="tpu_custom_call" | custom-call | tf_op jit(solution)/shard_map/synthesized/pallas_call | solution.py:495
  34.5 4.6 %all-to-all-done = bf16[4,48,768]{2,1,0:T(8,128)(2,1)S(1)} async-done(((bf16[4,48,768]{2,1,0:T(8,128)(2,1)}), bf16[4,48,768]{2,1,0:T(8,128)(2,1)S(1)}, u32[]{:S(2)}, u32[]{:S(2)}) %all-to-all-start) | async-done | bytes 294944 | tf_op jit(solution)/shard_map/all_to_all | solution.py:563
  39.1 0.0 copy-done.4
  39.1 0.1 subtract_select_fusion
  39.2 1.9 %collective-permute-start.1 = (bf16[8,768]{1,0:T(8,128)(2,1)S(1)}, bf16[8,768]{1,0:T(8,128)(2,1)S(1)}, u32[]{:S(2)}, u32[]{:S(2)}) collective-permute-start(bf16[8,768]{1,0:T(8,128)(2,1)S(1)} %slice.307), channel_id=1, source_target_pairs={{0,4},{4,8},{8,12},{12,16},{16,20},{20,24},{24,28},{28,32},{32,36}... | collective-permute-start | bytes 36872 | tf_op jit(solution)/shard_map/ppermute | solution.py:559
  41.2 7.9 %collective-permute-done.1 = bf16[8,768]{1,0:T(8,128)(2,1)S(1)} collective-permute-done((bf16[8,768]{1,0:T(8,128)(2,1)S(1)}, bf16[8,768]{1,0:T(8,128)(2,1)S(1)}, u32[]{:S(2)}, u32[]{:S(2)}) %collective-permute-start.1) | collective-permute-done | bytes 12320 | tf_op jit(solution)/shard_map/ppermute | solution.py:559
  49.0 0.2 multiply_add_fusion.1
  49.3 0.3 multiply_add_fusion.5
  49.6 0.3 multiply_add_fusion.3
  49.9 0.1 fusion.6
  50.0 21.4 %all_gather.4 = bf16[4,4,48,640]{3,2,1,0:T(8,128)(2,1)S(1)} all-gather(bf16[1,4,48,640]{3,2,1,0:T(8,128)(2,1)S(1)} %fusion.6), channel_id=1, replica_groups=mesh['cube'=4,'facet'=32,'dp'=4] {'cube'}, dimensions={0}, use_global_device_ids=true | all-gather | bytes 1228800 | tf_op jit(solution)/shard_map/all_gather | solution.py:608
  71.3 0.1 convert_reduce_fusion
  71.5 0.2 fusion.3
  71.8 0.1 broadcast_in_dim.14
  71.9 14.3 %all_to_all.10 = bf16[4,5,48,640]{3,2,1,0:T(8,128)(2,1)S(1)} all-to-all(bf16[4,5,48,640]{3,2,1,0:T(8,128)(2,1)S(1)} %broadcast_in_dim.14), channel_id=1, replica_groups=mesh['cube'=4,'facet'=32,'dp'=4] {'dp'}, dimensions={0} | all-to-all | bytes 2457600 | tf_op jit(solution)/shard_map/all_to_all | solution.py:612
  86.1 0.1 slice_bitcast_fusion.3
  86.2 0.9 subtract_maximum_fusion
  87.1 1.0 %fusion = bf16[4,1,48,2560]{3,2,1,0:T(8,128)(2,1)} fusion(bf16[5,48,640]{2,1,0:T(8,128)(2,1)S(1)} %get-tuple-element.13, bf16[5,48,640]{2,1,0:T(8,128)(2,1)S(1)} %get-tuple-element.14, bf16[5,48,640]{2,1,0:T(8,128)(2,1)S(1)} %get-tuple-element.15, bf16[5,48,640]{2,1,0:T(8,128)(2,1)S(1)} %get-tuple-element.12), kind=kLoop, calls=%fused_computation.2 | loop fusion | flops 3932160 | bytes 2211840 | tf_op jit(solution)/shard_map/broadcast_in_dim | solution.py:616
  (6 shorter events, 0.1 us)
Async XLA Ops:
  4.3 15.6 %collective-permute-start = (bf16[68,16,128]{2,1,0:T(8,128)(2,1)}, bf16[68,16,128]{2,1,0:T(8,128)(2,1)S(1)}, u32[]{:S(2)}, u32[]{:S(2)}) collective-permute-start(bf16[68,16,128]{2,1,0:T(8,128)(2,1)} %message.1), channel_id=1, source_target_pairs={{4,0},{8,4},{12,8},{16,12},{20,16},{24,20},{28,24},{32,28},{36,32}... | collective-permute-start | bytes 835592 | tf_op jit(solution)/shard_map/ppermute | solution.py:559
  19.9 0.7 copy-start.2
  20.6 11.7 %copy-start = (bf16[3072,256]{1,0:T(8,128)(2,1)S(1)}, bf16[3072,256]{1,0:T(8,128)(2,1)}, u32[]{:S(2)}) copy-start(bf16[3072,256]{1,0:T(8,128)(2,1)} %constant.9.clone.filters_hbm.table_hbm.constants_ref) | copy-start | bytes 4718596
  20.6 11.7 %copy-start.1 = (bf16[4,1,48,2560]{3,2,1,0:T(8,128)(2,1)S(1)}, bf16[4,1,48,2560]{3,2,1,0:T(8,128)(2,1)}, u32[]{:S(2)}) copy-start(bf16[4,1,48,2560]{3,2,1,0:T(8,128)(2,1)} %param.9) | copy-start | bytes 2949124
  25.8 13.3 %all-to-all-start = ((bf16[4,48,768]{2,1,0:T(8,128)(2,1)}), bf16[4,48,768]{2,1,0:T(8,128)(2,1)S(1)}, u32[]{:S(2)}, u32[]{:S(2)}) async-start(bf16[4,48,768]{2,1,0:T(8,128)(2,1)} %gradient_parts.1), calls=%async_computation | async-start | bytes 589824 | tf_op jit(solution)/shard_map/all_to_all | solution.py:563
  32.3 1.0 %copy-start.3 = (bf16[68,16,128]{2,1,0:T(8,128)(2,1)S(1)}, bf16[68,16,128]{2,1,0:T(8,128)(2,1)}, u32[]{:S(2)}) copy-start(bf16[68,16,128]{2,1,0:T(8,128)(2,1)} %copy-done.2) | copy-start | bytes 835588
  33.2 5.9 %copy-start.4 = (f32[1,48,2560]{2,1,0:T(8,128)S(1)}, f32[1,48,2560]{2,1,0:T(8,128)}, u32[]{:S(2)}) copy-start(f32[1,48,2560]{2,1,0:T(8,128)} %param.8) | copy-start | bytes 1474564
  39.2 9.8 %collective-permute-start.1 = (bf16[8,768]{1,0:T(8,128)(2,1)S(1)}, bf16[8,768]{1,0:T(8,128)(2,1)S(1)}, u32[]{:S(2)}, u32[]{:S(2)}) collective-permute-start(bf16[8,768]{1,0:T(8,128)(2,1)S(1)} %slice.307), channel_id=1, source_target_pairs={{0,4},{4,8},{8,12},{12,16},{16,20},{20,24},{24,28},{28,32},{32,36}... | collective-permute-start | bytes 36872 | tf_op jit(solution)/shard_map/ppermute | solution.py:559

commit v9 on v8

--- a/solution.py
+++ b/solution.py
@@ -170,26 +170,28 @@
 
 
 def columns_back(part, rows, dual_ref, filters, rows_ref):
-    for a in range(2):
-        for j in range(SPAN // HALO + 1):
-            place = (PART // HALO) * part - 1 + j
-            inside = (place >= 0) & (place < W // HALO)
-            columns = pl.ds(pl.multiple_of(jnp.clip(place, 0, W // HALO - 1) * HALO, HALO), HALO)
+    tiles = SPAN // HALO + 1
+    blocks = []
+    for j in range(tiles):
+        place = (PART // HALO) * part - 1 + j
+        inside = (place >= 0) & (place < W // HALO)
+        columns = pl.ds(pl.multiple_of(jnp.clip(place, 0, W // HALO - 1) * HALO, HALO), HALO)
+        for a in range(2):
             pair = jnp.concatenate([dual_ref[2 * a + b, :rows, columns] for b in range(2)], 1)
-            across = sum(
-                lax.dot_general(
-                    pair,
-                    filters(i),
-                    (((1,), (1,)), ((), ())),
-                    preferred_element_type=jnp.float32,
-                )
-                for i in range(2)
+            blocks.append(jnp.where(inside, pair, jnp.zeros_like(pair)))
+    stacked = jnp.concatenate(blocks, 0)
+    across = sum(
+        lax.dot_general(
+            stacked, filters(i), (((1,), (1,)), ((), ())), preferred_element_type=jnp.float32
+        )
+        for i in range(2)
+    )
+    for j in range(tiles - 1):
+        for a in range(2):
+            here, right = [across[rows * (2 * i + a) : rows * (2 * i + a + 1)] for i in (j, j + 1)]
+            rows_ref[a, 8 : 8 + rows, HALO * j : HALO * (j + 1)] = (
+                here[:, HALO:] + right[:, :HALO]
             )
-            across = jnp.where(inside, across, 0.0)
-            if j > 0:
-                rows_ref[a, 8 : 8 + rows, HALO * (j - 1) : HALO * j] += across[:, :HALO]
-            if j < SPAN // HALO:
-                rows_ref[a, 8 : 8 + rows, HALO * j : HALO * (j + 1)] = across[:, HALO:]
 
 
 def rows_back(first, count, tile, rows_ref):
@@ -206,7 +208,6 @@
     slots_hbm,
     live_hbm,
     weight_hbm,
-    payload_hbm,
     dual_hbm,
     filters_hbm,
     out_ref,
@@ -226,7 +227,6 @@
         (slots_hbm, slots_ref),
         (live_hbm, live_ref),
         (weight_hbm, weight_ref),
-        (payload_hbm, out_ref.at[pl.ds(0, BLK)]),
     ]
     copies = [pltpu.make_async_copy(s, d, sems.at[i]) for i, (s, d) in enumerate(pairs)]
     for copy in copies:
@@ -243,18 +243,17 @@
     )
     for i in range(SPAN // HALO // 2):
         pair = [rows_back(-8, 8, pl.ds(HALO * (2 * i + j), HALO), rows_ref) for j in range(2)]
-        out_ref[BLK + 1 + i] = jnp.concatenate(pair, 0).astype(jnp.bfloat16)
-    for copy in copies[2:6]:
+        out_ref[1 + i] = jnp.concatenate(pair, 0).astype(jnp.bfloat16)
+    for copy in copies[2:]:
         copy.wait()
     row = lax.broadcasted_iota(jnp.int32, (TILE, BLK), 0)
     starts = starts_ref[...]
     numbers = jnp.where(row == 0, starts >> 6, starts & 63)
     numbers = jnp.where(row == 2, slots_ref[...], numbers)
     numbers = jnp.where(row == 3, live_ref[0, 0], numbers)
-    out_ref[BLK] = jnp.concatenate(
+    out_ref[0] = jnp.concatenate(
         [weight_ref[...].astype(jnp.float32), numbers.astype(jnp.float32)], 1
     ).astype(jnp.bfloat16)
-    copies[6].wait()
 
 
 def synthesis(part_ref, message_ref, dual_ref, constants_ref, synth_ref, rows_ref):
@@ -269,7 +268,7 @@
     for j in range(SPAN // HALO):
         tile = pl.ds(HALO * j, HALO)
         synth_ref[:, tile] = rows_back(0, FR, tile, rows_ref)
-        below = message_ref[BLK + 1 + j // 2].astype(jnp.float32)
+        below = message_ref[1 + j // 2].astype(jnp.float32)
         synth_ref[FR - 8 :, tile] += below[8 * (j % 2) : 8 * (j % 2) + 8]
 
 
@@ -368,41 +367,55 @@
 
 
 def below_pass(
-    message_ref,
-    spec_ref,
-    own_ref,
+    message_hbm,
+    payload_hbm,
+    spec_hbm,
+    own_hbm,
     table_hbm,
     out_ref,
     list_ref,
     numbers_ref,
     vector_ref,
+    message_ref,
+    payload_ref,
+    spec_ref,
+    grad_ref,
     table_ref,
     order_ref,
     re_ref,
     im_ref,
-    grad_ref,
     tile_ref,
     sems,
 ):
-    copy = pltpu.make_async_copy(table_hbm.at[pl.ds(0, Q * R), :], table_ref, sems.at[0])
-    copy.start()
-    meta = message_ref[BLK].astype(jnp.float32)
-    vector_ref[...] = meta[:8].astype(jnp.int32)
-    read = pltpu.make_async_copy(vector_ref, numbers_ref, sems.at[1])
-    read.start()
+    pairs = [
+        (message_hbm.at[0], message_ref),
+        (spec_hbm, spec_ref),
+        (own_hbm, grad_ref),
+        (payload_hbm, payload_ref),
+        (table_hbm.at[pl.ds(0, Q * R), :], table_ref),
+    ]
+    copies = [pltpu.make_async_copy(s, d, sems.at[i]) for i, (s, d) in enumerate(pairs)]
+    for copy in copies:
+        copy.start()
     lane = lax.broadcasted_iota(jnp.int32, (1, 128), 1)
     low = lane < 64
     quarter = lane >> 5
-    grad_ref[...] = own_ref[...]
+    copies[0].wait()
+    meta = message_ref[...].astype(jnp.float32)
+    vector_ref[...] = meta[:8].astype(jnp.int32)
+    read = pltpu.make_async_copy(vector_ref, numbers_ref, sems.at[5])
+    read.start()
     order_ref[...] = residue_order()
     read.wait()
+    for copy in copies[1:4]:
+        copy.wait()
     add_blocks(
         0,
         lambda b: (numbers_ref[0, BLK + b], numbers_ref[1, BLK + b]),
         lambda b: numbers_ref[2, BLK + b],
         numbers_ref[3, BLK],
         jnp.where(low, meta, 0.0),
-        message_ref,
+        payload_ref,
         spec_ref,
         grad_ref,
         list_ref,
@@ -426,7 +439,7 @@
         return carry
 
     lax.fori_loop(0, FR // 8, backward, 0)
-    copy.wait()
+    copies[4].wait()
     for j in range(5):
         places = [[] for _ in range(4)]
         for p in range(4):
@@ -470,11 +483,11 @@
 COST = pl.CostEstimate(flops=2 * 10**9, bytes_accessed=4 * 10**6, transcendentals=0)
 
 
-def message(part, starts, slots, live, weights, payload, dual, table):
+def message(part, starts, slots, live, weights, dual, table):
     return pl.pallas_call(
         write_message,
-        out_shape=jax.ShapeDtypeStruct((BLK + 1 + SPAN // HALO // 2, TILE, 128), jnp.bfloat16),
-        in_specs=[SMEM_SPEC] + [HBM_SPEC] * 7,
+        out_shape=jax.ShapeDtypeStruct((1 + SPAN // HALO // 2, TILE, 128), jnp.bfloat16),
+        in_specs=[SMEM_SPEC] + [HBM_SPEC] * 6,
         out_specs=VMEM_SPEC,
         scratch_shapes=[
             pltpu.VMEM((1, BLK), jnp.int32),
@@ -484,11 +497,11 @@
             pltpu.VMEM((4, TILE, W), jnp.bfloat16),
             pltpu.VMEM((4 * HALO, 2 * HALO), jnp.bfloat16),
             pltpu.VMEM((2, 8 + TILE, SPAN), jnp.float32),
-            pltpu.SemaphoreType.DMA((7,)),
+            pltpu.SemaphoreType.DMA((6,)),
         ],
         compiler_params=PARAMS,
         name="message",
-    )(part, starts, slots, live, weights, payload, dual, table)
+    )(part, starts, slots, live, weights, dual, table)
 
 
 def synthesized(part, received, dual, table):
@@ -529,28 +542,66 @@
     )(starts, slots, live, weights, payload, table, pixels)
 
 
-def gradient_parts(received, spectra, own, table):
+def gradient_parts(received, payload, spectra, own, table):
     return pl.pallas_call(
         below_pass,
         out_shape=jax.ShapeDtypeStruct((DP, FR, SPAN), jnp.bfloat16),
-        in_specs=[VMEM_SPEC] * 3 + [HBM_SPEC],
+        in_specs=[HBM_SPEC] * 5,
         out_specs=VMEM_SPEC,
         scratch_shapes=[
             pltpu.SMEM((BLK + UNROLL,), jnp.int32),
             pltpu.SMEM((8, 128), jnp.int32),
             pltpu.VMEM((8, 128), jnp.int32),
+            pltpu.VMEM((TILE, 128), jnp.bfloat16),
+            pltpu.VMEM((BLK, TILE, 128), jnp.bfloat16),
+            pltpu.VMEM((CHUNKS + 1, FR, 128), jnp.float32),
+            pltpu.VMEM((CHUNKS + 1, FR, 128), jnp.float32),
             TABLE,
             pltpu.VMEM((PART, PART), jnp.bfloat16),
             pltpu.VMEM((Q, FR, R), jnp.float32),
             pltpu.VMEM((Q, FR, R), jnp.float32),
-            pltpu.VMEM((CHUNKS + 1, FR, 128), jnp.float32),
             pltpu.VMEM((Q, FR, R), jnp.float32),
-            pltpu.SemaphoreType.DMA((2,)),
+            pltpu.SemaphoreType.DMA((6,)),
         ],
         compiler_params=PARAMS,
         cost_estimate=COST,
         name="gradient_parts",
-    )(received, spectra, own, table)
+    )(received, payload, spectra, own, table)
+
+
+def finish(parts_ref, pixels_ref, image_hbm, dual_hbm, image_ref, sems):
+    copies = []
+    for d in range(DP):
+        tile = pl.ds(PART * d, PART)
+        copies.append(
+            pltpu.make_async_copy(
+                parts_ref.at[d, pl.ds(0, 4)], dual_hbm.at[:, :, tile], sems.at[d]
+            )
+        )
+        copies[-1].start()
+    for d in range(DP):
+        tile = pl.ds(PART * d, PART)
+        descent = parts_ref[d, 4].astype(jnp.float32)
+        image_ref[:, tile] = jnp.maximum(pixels_ref[:, tile] - TAU_STEP * descent, 0.0)
+    copies.append(pltpu.make_async_copy(image_ref, image_hbm, sems.at[DP]))
+    copies[-1].start()
+    for copy in copies:
+        copy.wait()
+
+
+def finished(parts, pixels):
+    return pl.pallas_call(
+        finish,
+        out_shape=(
+            jax.ShapeDtypeStruct((FR, W), jnp.float32),
+            jax.ShapeDtypeStruct((4, FR, W), jnp.bfloat16),
+        ),
+        in_specs=[VMEM_SPEC] * 2,
+        out_specs=(HBM_SPEC,) * 2,
+        scratch_shapes=[pltpu.VMEM((FR, W), jnp.float32), pltpu.SemaphoreType.DMA((DP + 1,))],
+        compiler_params=pltpu.CompilerParams(vmem_limit_bytes=16 * 1024 * 1024),
+        name="finished",
+    )(parts, pixels)
 
 
 def hop(block, distance):
@@ -581,8 +632,9 @@
     own_rows = image[0]
     part = position[None]
     weights = vis_weight[0].T
+    payload_below = hop(payload[0], -1)
     received = hop(
-        message(part, freq_start, tile_slot, live, weights, payload[0], dual[:, 0], table), -1
+        message(part, freq_start, tile_slot, live, weights, dual[:, 0], table), -1
     )
 
     left = position * PART
@@ -594,7 +646,7 @@
     spectra, own = own_spectra(
         freq_start, tile_slot, live, weights, payload[0], table, own_rows
     )
-    terms = gradient_parts(received, spectra, own, table)
+    terms = gradient_parts(received, payload_below, spectra, own, table)
     terms, received = lax.optimization_barrier((terms, received))
     synth = synthesized(part, received, dual[:, 0], table)
     total = gathered_sum(terms) + synth
@@ -610,9 +662,7 @@
     dual_part = (shifted * (RADIUS / jnp.maximum(norms, RADIUS))).astype(jnp.bfloat16)
     own_part = jnp.concatenate([dual_part, total[None, :, HALO:].astype(jnp.bfloat16)], 0)
     parts = lax.all_to_all(jnp.broadcast_to(own_part, (DP,) + own_part.shape), "dp", 0, 0)
-    whole = jnp.concatenate([parts[d] for d in range(DP)], -1)
-    dual_next = whole[:4]
-    updated = jnp.maximum(own_rows - TAU_STEP * whole[4].astype(jnp.float32), 0.0)
+    updated, dual_next = finished(parts, own_rows)
     return (updated[None], dual_next[:, None])
 
 

time: 88.5 us -> 86.4 us (0.976)
  the two profiles are of different devices: /device:TPU:40 before, /device:TPU:32 now
where the time goes in v9:
time: 86.4 us; the launch traced here: 86 us
  blocking collectives  33.9 us (39%)
  starting transfers between devices  18.2 us (21%)
  waiting for transfers between devices  14.9 us (17%)
  Pallas kernels  14.4 us (17%)
  local copies, waits for them, and re-layouts  1.53 us (2%)
  between operations  1.49 us (2%)
  other arithmetic  1.43 us (2%)
    all_gather x1, blocking collectives, on_device(): squares = lax.all_gather((shifted * shifted).astype(jnp.bfloat16), 'cube')  19.7 us
    ppermute x3, starting transfers between devices, hop(): return lax.ppermute(block, 'facet', route)  14.7 us
    all_to_all x1, blocking collectives, on_device(): lax.all_to_all(jnp.broadcast_to(own_part, (DP,) + own_part.shape), 'dp',...  14.3 us
    ppermute x3, waiting for transfers between devices, hop(): return lax.ppermute(block, 'facet', route)  9.09 us
    pallas_call x1, Pallas kernels, own_spectra(): pl.pallas_call(own_pass, out_shape=(SPECTRA, SPECTRA), in_specs=[HBM_SPEC...  5.86 us
    all_to_all x1, waiting for transfers between devices, gathered_sum(): mixed = lax.all_to_all(parts, 'dp', 0, 0)  5.85 us
    pallas_call x1, Pallas kernels, gradient_parts(): pl.pallas_call(below_pass, out_shape=jax.ShapeDtypeStruct((DP, FR, SPAN),...  4.76 us
    all_to_all x1, starting transfers between devices, gathered_sum(): mixed = lax.all_to_all(parts, 'dp', 0, 0)  3.46 us
  transfers between devices with their start and end apart: 4, of which 2 were waited for; matrix products, arithmetic and copies ran while one was open for 0% of the time, Pallas kernels for 10%

profile of v9, /device:TPU:32, one launch (start us, length us, event | category | flops | bytes accessed | tf_op | source)
XLA Modules:
  0.0 86.0 jit_solution(9428366079358036341)
XLA Ops:
  0.6 10.2 %collective-permute-start.1 = (bf16[64,16,128]{2,1,0:T(8,128)(2,1)}, bf16[64,16,128]{2,1,0:T(8,128)(2,1)S(1)}, u32[]{:S(2)}, u32[]{:S(2)}) collective-permute-start(bf16[64,16,128]{2,1,0:T(8,128)(2,1)} %bitcast.57), channel_id=1, source_target_pairs={{4,0},{8,4},{12,8},{16,12},{20,16},{24,20},{28,24},{32,28},{36,32}... | collective-permute-start | bytes 786440 | tf_op jit(solution)/shard_map/ppermute | solution.py:610
  11.5 2.1 %message.1 = bf16[4,16,128]{2,1,0:T(8,128)(2,1)} custom-call(s32[1]{0:T(128)} %bitcast.3.part_ref, s32[1,64]{1,0:T(1,128)} %starts_hbm.3, s32[1,64]{1,0:T(1,128)} %slots_hbm.3, s32[1,1]{1,0:T(1,128)S(6)} %copy.14.live_hbm, bf16[16,64]{1,0:T(8,128)(2,1)} %bitcast.53, bf16[4,48,2560]{2,1,0:T(8,128)(2,1)} %bitcast.38, ...), custom_call_target="tpu_custom_call" | custom-call | tf_op jit(solution)/shard_map/message/pallas_call | solution.py:487
  13.6 2.6 %collective-permute-start = (bf16[4,16,128]{2,1,0:T(8,128)(2,1)}, bf16[4,16,128]{2,1,0:T(8,128)(2,1)S(1)}, u32[]{:S(2)}, u32[]{:S(2)}) collective-permute-start(bf16[4,16,128]{2,1,0:T(8,128)(2,1)} %message.1), channel_id=1, source_target_pairs={{4,0},{8,4},{12,8},{16,12},{20,16},{24,20},{28,24},{32,28},{36,32}... | collective-permute-start | bytes 49160 | tf_op jit(solution)/shard_map/ppermute | solution.py:610
  16.2 5.9 %own_spectra.1 = (f32[41,48,128]{2,1,0:T(8,128)}, f32[41,48,128]{2,1,0:T(8,128)}) custom-call(s32[1,64]{1,0:T(1,128)} %starts_hbm.3, s32[1,64]{1,0:T(1,128)} %slots_hbm.3, s32[1,1]{1,0:T(1,128)S(6)} %copy.14.live_hbm, bf16[16,64]{1,0:T(8,128)(2,1)} %bitcast.54, bf16[64,16,128]{2,1,0:T(8,128)(2,1)} %bitcast.58, ...), custom_call_target="tpu_custom_call" | custom-call | flops 2000000000 | bytes 4000000 | tf_op jit(solution)/shard_map/own_spectra/pallas_call | solution.py:520
  22.1 0.0 collective-permute-done.message_hbm.message_ref
  22.1 0.0 copy-start.3
  22.1 0.0 collective-permute-done.1.payload_hbm
  22.1 0.0 copy-start.5
  22.1 0.6 copy-done.3
  22.7 0.1 copy-done.5
  22.8 0.0 copy-start
  22.8 0.0 copy-start.1
  22.8 4.8 %gradient_parts.1 = bf16[4,48,768]{2,1,0:T(8,128)(2,1)} custom-call(bf16[4,16,128]{2,1,0:T(8,128)(2,1)} %copy-done.3, bf16[64,16,128]{2,1,0:T(8,128)(2,1)} %copy-done.5, f32[41,48,128]{2,1,0:T(8,128)} %get-tuple-element.8.spec_hbm, f32[41,48,128]{2,1,0:T(8,128)} %get-tuple-element.9.own_hbm, bf16[3072,256]{1,0:T(8,128)(2,1)} %constant.11.clone.filters_hbm.table_hbm.constants_ref), custom_call_target="tpu_custom_call" | custom-call | flops 2000000000 | bytes 4000000 | tf_op jit(solution)/shard_map/gradient_parts/pallas_call | solution.py:546
  27.6 3.5 %all-to-all-start = ((bf16[4,48,768]{2,1,0:T(8,128)(2,1)}), bf16[4,48,768]{2,1,0:T(8,128)(2,1)S(1)}, u32[]{:S(2)}, u32[]{:S(2)}) async-start(bf16[4,48,768]{2,1,0:T(8,128)(2,1)} %gradient_parts.1), calls=%async_computation | async-start | bytes 589824 | tf_op jit(solution)/shard_map/all_to_all | solution.py:614
  31.1 0.0 copy-done
  31.1 0.0 copy-done.1
  31.1 0.0 copy-start.4
  31.1 0.7 copy-done.4
  31.8 0.0 copy-start.2
  31.8 0.6 synthesized.1
  32.4 5.9 %all-to-all-done = bf16[4,48,768]{2,1,0:T(8,128)(2,1)S(1)} async-done(((bf16[4,48,768]{2,1,0:T(8,128)(2,1)}), bf16[4,48,768]{2,1,0:T(8,128)(2,1)S(1)}, u32[]{:S(2)}, u32[]{:S(2)}) %all-to-all-start) | async-done | bytes 294944 | tf_op jit(solution)/shard_map/all_to_all | solution.py:614
  38.3 0.0 copy-done.2
  38.3 0.1 subtract_select_fusion
  38.4 1.9 %collective-permute-start.2 = (bf16[8,768]{1,0:T(8,128)(2,1)S(1)}, bf16[8,768]{1,0:T(8,128)(2,1)S(1)}, u32[]{:S(2)}, u32[]{:S(2)}) collective-permute-start(bf16[8,768]{1,0:T(8,128)(2,1)S(1)} %slice.275), channel_id=1, source_target_pairs={{0,4},{4,8},{8,12},{12,16},{16,20},{20,24},{24,28},{28,32},{32,36}... | collective-permute-start | bytes 36872 | tf_op jit(solution)/shard_map/ppermute | solution.py:610
  40.3 9.1 %collective-permute-done.2 = bf16[8,768]{1,0:T(8,128)(2,1)S(1)} collective-permute-done((bf16[8,768]{1,0:T(8,128)(2,1)S(1)}, bf16[8,768]{1,0:T(8,128)(2,1)S(1)}, u32[]{:S(2)}, u32[]{:S(2)}) %collective-permute-start.2) | collective-permute-done | bytes 12320 | tf_op jit(solution)/shard_map/ppermute | solution.py:610
  49.4 0.2 multiply_add_fusion.1
  49.7 0.3 multiply_add_fusion.5
  50.0 0.3 multiply_add_fusion.3
  50.3 0.1 fusion.5
  50.4 19.7 %all_gather.4 = bf16[4,4,48,640]{3,2,1,0:T(8,128)(2,1)S(1)} all-gather(bf16[1,4,48,640]{3,2,1,0:T(8,128)(2,1)S(1)} %fusion.5), channel_id=1, replica_groups=mesh['cube'=4,'facet'=32,'dp'=4] {'cube'}, dimensions={0}, use_global_device_ids=true | all-gather | bytes 1228800 | tf_op jit(solution)/shard_map/all_gather | solution.py:660
  70.0 0.1 convert_reduce_fusion
  70.2 0.3 fusion.2
  70.5 0.1 broadcast_in_dim.16
  70.6 14.3 %all_to_all.10.parts_ref = bf16[4,5,48,640]{3,2,1,0:T(8,128)(2,1)S(1)} all-to-all(bf16[4,5,48,640]{3,2,1,0:T(8,128)(2,1)S(1)} %broadcast_in_dim.16), channel_id=1, replica_groups=mesh['cube'=4,'facet'=32,'dp'=4] {'dp'}, dimensions={0} | all-to-all | bytes 2457600 | tf_op jit(solution)/shard_map/all_to_all | solution.py:664
  84.8 1.1 %finished.1 = (f32[48,2560]{1,0:T(8,128)}, bf16[4,48,2560]{2,1,0:T(8,128)(2,1)}) custom-call(bf16[4,5,48,640]{3,2,1,0:T(8,128)(2,1)S(1)} %all_to_all.10.parts_ref, f32[48,2560]{1,0:T(8,128)S(1)} %bitcast.44), custom_call_target="tpu_custom_call" | custom-call | tf_op jit(solution)/shard_map/finished/pallas_call | solution.py:593
  (6 shorter events, 0.1 us)
Async XLA Ops:
  0.6 21.5 %collective-permute-start.1 = (bf16[64,16,128]{2,1,0:T(8,128)(2,1)}, bf16[64,16,128]{2,1,0:T(8,128)(2,1)S(1)}, u32[]{:S(2)}, u32[]{:S(2)}) collective-permute-start(bf16[64,16,128]{2,1,0:T(8,128)(2,1)} %bitcast.57), channel_id=1, source_target_pairs={{4,0},{8,4},{12,8},{16,12},{20,16},{24,20},{28,24},{32,28},{36,32}... | collective-permute-start | bytes 786440 | tf_op jit(solution)/shard_map/ppermute | solution.py:610
  13.6 8.5 %collective-permute-start = (bf16[4,16,128]{2,1,0:T(8,128)(2,1)}, bf16[4,16,128]{2,1,0:T(8,128)(2,1)S(1)}, u32[]{:S(2)}, u32[]{:S(2)}) collective-permute-start(bf16[4,16,128]{2,1,0:T(8,128)(2,1)} %message.1), channel_id=1, source_target_pairs={{4,0},{8,4},{12,8},{16,12},{20,16},{24,20},{28,24},{32,28},{36,32}... | collective-permute-start | bytes 49160 | tf_op jit(solution)/shard_map/ppermute | solution.py:610
  22.1 0.6 copy-start.3
  22.1 0.7 copy-start.5
  22.8 8.3 %copy-start = (bf16[3072,256]{1,0:T(8,128)(2,1)S(1)}, bf16[3072,256]{1,0:T(8,128)(2,1)}, u32[]{:S(2)}) copy-start(bf16[3072,256]{1,0:T(8,128)(2,1)} %constant.11.clone.filters_hbm.table_hbm.constants_ref) | copy-start | bytes 4718596
  22.8 8.3 %copy-start.1 = (bf16[4,1,48,2560]{3,2,1,0:T(8,128)(2,1)S(1)}, bf16[4,1,48,2560]{3,2,1,0:T(8,128)(2,1)}, u32[]{:S(2)}) copy-start(bf16[4,1,48,2560]{3,2,1,0:T(8,128)(2,1)} %param.9) | copy-start | bytes 2949124
  27.6 10.7 %all-to-all-start = ((bf16[4,48,768]{2,1,0:T(8,128)(2,1)}), bf16[4,48,768]{2,1,0:T(8,128)(2,1)S(1)}, u32[]{:S(2)}, u32[]{:S(2)}) async-start(bf16[4,48,768]{2,1,0:T(8,128)(2,1)} %gradient_parts.1), calls=%async_computation | async-start | bytes 589824 | tf_op jit(solution)/shard_map/all_to_all | solution.py:614
  31.1 0.7 copy-start.4
  31.8 6.5 %copy-start.2 = (f32[1,48,2560]{2,1,0:T(8,128)S(1)}, f32[1,48,2560]{2,1,0:T(8,128)}, u32[]{:S(2)}) copy-start(f32[1,48,2560]{2,1,0:T(8,128)} %param.8) | copy-start | bytes 1474564
  38.4 11.0 %collective-permute-start.2 = (bf16[8,768]{1,0:T(8,128)(2,1)S(1)}, bf16[8,768]{1,0:T(8,128)(2,1)S(1)}, u32[]{:S(2)}, u32[]{:S(2)}) collective-permute-start(bf16[8,768]{1,0:T(8,128)(2,1)S(1)} %slice.275), channel_id=1, source_target_pairs={{0,4},{4,8},{8,12},{12,16},{16,20},{20,24},{24,28},{28,32},{32,36}... | collective-permute-start | bytes 36872 | tf_op jit(solution)/shard_map/ppermute | solution.py:610

commit v10 on v9

--- a/solution.py
+++ b/solution.py
@@ -45,7 +45,7 @@
 HALO = 128
 SPAN = PART + HALO
 CHUNKS = W // 64
-UNROLL = 4
+UNROLL = 8
 VMEM_LIMIT = 60 * 1024 * 1024
 NORM = 1.0 / math.sqrt(W)
 C1, C2 = math.cos(2 * math.pi / 5), math.cos(4 * math.pi / 5)
@@ -60,7 +60,12 @@
 
 
 def constants():
-    return np.concatenate([tables().reshape(Q * R, 2 * R), column_filters().reshape(-1, 2 * HALO)])
+    table = tables()
+    return np.concatenate([table.reshape(Q * R, 2 * R), column_filters().reshape(-1, 2 * HALO)])
+
+
+def flipped_table():
+    return tables().transpose(0, 2, 1).reshape(2 * Q * R, R)
 
 
 def column_filters():
@@ -119,6 +124,16 @@
     target = (y - Q * group) * 32 + group
     lane = lax.broadcasted_iota(jnp.int32, (PART, 128), 1)
     tiles = [jnp.where(target == lane + 128 * j, 1.0, 0.0) for j in range(PART // 128)]
+    return jnp.concatenate(tiles, 1).astype(jnp.bfloat16)
+
+
+def natural_order():
+    row = lax.broadcasted_iota(jnp.int32, (PART, 128), 0)
+    tiles = []
+    for j in range(PART // 128):
+        y = lax.broadcasted_iota(jnp.int32, (1, 128), 1) + 128 * j
+        group = ((y.astype(jnp.float32) + 0.5) * (1.0 / Q)).astype(jnp.int32)
+        tiles.append(jnp.where(row == (y - Q * group) * 32 + group, 1.0, 0.0))
     return jnp.concatenate(tiles, 1).astype(jnp.bfloat16)
 
 
@@ -152,8 +167,8 @@
             chunk, offset = start(b)
             tile = jnp.clip(slot(b) - base, 0, PER - 1)
             rows = pl.ds(pl.multiple_of(tile * TILE, TILE), TILE)
-            first = pltpu.roll(spec_ref[chunk, rows, :], (128 - offset) & 127, 1)
-            second = pltpu.roll(spec_ref[chunk + 1, rows, :], 64 - offset, 1)
+            first = pltpu.roll(spec_ref[chunk, rows, :].astype(jnp.float32), (128 - offset) & 127, 1)
+            second = pltpu.roll(spec_ref[chunk + 1, rows, :].astype(jnp.float32), 64 - offset, 1)
             model = jnp.where(half < 64 - offset, first, second)
             misfit = factors[TILE * u : TILE * (u + 1)] * (
                 model - payload_ref[b].astype(jnp.float32)
@@ -281,7 +296,7 @@
     table_hbm,
     pixels_hbm,
     spec_ref,
-    grad_ref,
+    own_ref,
     starts_ref,
     slots_ref,
     live_ref,
@@ -293,6 +308,7 @@
     order_ref,
     re_ref,
     im_ref,
+    grad_ref,
     sems,
 ):
     pairs = [
@@ -338,15 +354,17 @@
             im_ref[q] = partial[:, R:]
 
     def forward(i, carry):
-        rows = pl.ds(pl.multiple_of(i * 8, 8), 8)
-        spectrum = dft20([(re_ref[q, rows, :], im_ref[q, rows, :]) for q in range(Q)], -1)
-        for k, (re, im) in enumerate(spectrum):
-            re, im = re * NORM, im * NORM
-            spec_ref[2 * k, rows, :] = jnp.where(low, re, pltpu.roll(im, 64, 1))
-            spec_ref[2 * k + 1, rows, :] = jnp.where(low, pltpu.roll(re, 64, 1), im)
+        for j in range(2):
+            rows = pl.ds(pl.multiple_of(i * TILE + 8 * j, 8), 8)
+            spectrum = dft20([(re_ref[q, rows, :], im_ref[q, rows, :]) for q in range(Q)], -1)
+            for k, (re, im) in enumerate(spectrum):
+                re, im = re * NORM, im * NORM
+                grad_ref[2 * k, rows, :] = jnp.where(low, re, pltpu.roll(im, 64, 1))
+                grad_ref[2 * k + 1, rows, :] = jnp.where(low, pltpu.roll(re, 64, 1), im)
         return carry
 
-    lax.fori_loop(0, FR // 8, forward, 0)
+    lax.fori_loop(0, FR // TILE, forward, 0)
+    spec_ref[:CHUNKS] = grad_ref[:CHUNKS].astype(jnp.bfloat16)
     spec_ref[CHUNKS] = spec_ref[0]
     grad_ref[...] = jnp.zeros_like(grad_ref)
     for copy in copies[2:]:
@@ -364,6 +382,7 @@
         grad_ref,
         list_ref,
     )
+    own_ref[...] = grad_ref[...].astype(jnp.bfloat16)
 
 
 def below_pass(
@@ -379,6 +398,7 @@
     message_ref,
     payload_ref,
     spec_ref,
+    own_ref,
     grad_ref,
     table_ref,
     order_ref,
@@ -390,9 +410,9 @@
     pairs = [
         (message_hbm.at[0], message_ref),
         (spec_hbm, spec_ref),
-        (own_hbm, grad_ref),
+        (own_hbm, own_ref),
         (payload_hbm, payload_ref),
-        (table_hbm.at[pl.ds(0, Q * R), :], table_ref),
+        (table_hbm, table_ref),
     ]
     copies = [pltpu.make_async_copy(s, d, sems.at[i]) for i, (s, d) in enumerate(pairs)]
     for copy in copies:
@@ -405,10 +425,11 @@
     vector_ref[...] = meta[:8].astype(jnp.int32)
     read = pltpu.make_async_copy(vector_ref, numbers_ref, sems.at[5])
     read.start()
-    order_ref[...] = residue_order()
+    order_ref[...] = natural_order()
     read.wait()
     for copy in copies[1:4]:
         copy.wait()
+    grad_ref[...] = own_ref[...].astype(jnp.float32)
     add_blocks(
         0,
         lambda b: (numbers_ref[0, BLK + b], numbers_ref[1, BLK + b]),
@@ -445,11 +466,8 @@
         for p in range(4):
             q = 4 * j + p
             pair = jnp.concatenate([re_ref[q], im_ref[q]], 1).astype(jnp.bfloat16)
-            rows = lax.dot_general(
-                pair,
-                table_ref[R * q : R * (q + 1)],
-                (((1,), (1,)), ((), ())),
-                preferred_element_type=jnp.float32,
+            rows = jnp.dot(
+                pair, table_ref[2 * R * q : 2 * R * (q + 1)], preferred_element_type=jnp.float32
             )
             for g in range(4):
                 places[g].append(rows if g == p else pltpu.roll(rows, (32 * (p - g)) % 128, 1))
@@ -461,8 +479,8 @@
     mixed = jnp.concatenate(
         [jnp.concatenate([tile_ref[5 * g + j] for j in range(5)], 1) for g in range(4)], 0
     ).astype(jnp.bfloat16)
-    natural = lax.dot_general(
-        mixed, order_ref[...], (((1,), (1,)), ((), ())), preferred_element_type=jnp.float32
+    natural = jnp.dot(
+        mixed, order_ref[...], preferred_element_type=jnp.float32
     ).astype(jnp.bfloat16)
     out_ref[0, :, :HALO] = jnp.zeros((FR, HALO), jnp.bfloat16)
     for g in range(4):
@@ -475,7 +493,7 @@
 HBM_SPEC = pl.BlockSpec(memory_space=pltpu.HBM)
 SMEM_SPEC = pl.BlockSpec(memory_space=pltpu.SMEM)
 VMEM_SPEC = pl.BlockSpec(memory_space=pltpu.VMEM)
-SPECTRA = jax.ShapeDtypeStruct((CHUNKS + 1, FR, 128), jnp.float32)
+SPECTRA = jax.ShapeDtypeStruct((CHUNKS + 1, FR, 128), jnp.bfloat16)
 
 
 TABLE = pltpu.VMEM((Q * R, 2 * R), jnp.bfloat16)
@@ -534,6 +552,7 @@
             pltpu.VMEM((PART, PART), jnp.bfloat16),
             pltpu.VMEM((Q, FR, R), jnp.float32),
             pltpu.VMEM((Q, FR, R), jnp.float32),
+            pltpu.VMEM((CHUNKS + 1, FR, 128), jnp.float32),
             pltpu.SemaphoreType.DMA((7,)),
         ],
         compiler_params=PARAMS,
@@ -554,9 +573,10 @@
             pltpu.VMEM((8, 128), jnp.int32),
             pltpu.VMEM((TILE, 128), jnp.bfloat16),
             pltpu.VMEM((BLK, TILE, 128), jnp.bfloat16),
+            pltpu.VMEM((CHUNKS + 1, FR, 128), jnp.bfloat16),
+            pltpu.VMEM((CHUNKS + 1, FR, 128), jnp.bfloat16),
             pltpu.VMEM((CHUNKS + 1, FR, 128), jnp.float32),
-            pltpu.VMEM((CHUNKS + 1, FR, 128), jnp.float32),
-            TABLE,
+            pltpu.VMEM((2 * Q * R, R), jnp.bfloat16),
             pltpu.VMEM((PART, PART), jnp.bfloat16),
             pltpu.VMEM((Q, FR, R), jnp.float32),
             pltpu.VMEM((Q, FR, R), jnp.float32),
@@ -627,7 +647,7 @@
 
 
 def on_device(image, dual, payload, vis_weight, freq_start, tile_slot, live):
-    table = jnp.asarray(constants())
+    table, flipped = jnp.asarray(constants()), jnp.asarray(flipped_table())
     position = lax.axis_index("dp")
     own_rows = image[0]
     part = position[None]
@@ -646,7 +666,7 @@
     spectra, own = own_spectra(
         freq_start, tile_slot, live, weights, payload[0], table, own_rows
     )
-    terms = gradient_parts(received, payload_below, spectra, own, table)
+    terms = gradient_parts(received, payload_below, spectra, own, flipped)
     terms, received = lax.optimization_barrier((terms, received))
     synth = synthesized(part, received, dual[:, 0], table)
     total = gathered_sum(terms) + synth

time: 86.4 us -> 84.6 us (0.979)
  the two profiles are of different devices: /device:TPU:32 before, /device:TPU:1 now
where the time goes in v10:
time: 84.6 us; the launch traced here: 83.4 us
  blocking collectives  39.4 us (47%)
  starting transfers between devices  18.9 us (22%)
  Pallas kernels  12.2 us (14%)
  waiting for transfers between devices  8.39 us (10%)
  local copies, waits for them, and re-layouts  1.53 us (2%)
  between operations  1.46 us (2%)
  other arithmetic  1.43 us (2%)
    all_to_all x1, blocking collectives, on_device(): lax.all_to_all(jnp.broadcast_to(own_part, (DP,) + own_part.shape), 'dp',...  19.7 us
    all_gather x1, blocking collectives, on_device(): squares = lax.all_gather((shifted * shifted).astype(jnp.bfloat16), 'cube')  19.7 us
    ppermute x3, starting transfers between devices, hop(): return lax.ppermute(block, 'facet', route)  15.5 us
    all_to_all x1, waiting for transfers between devices, gathered_sum(): mixed = lax.all_to_all(parts, 'dp', 0, 0)  4.32 us
    pallas_call x1, Pallas kernels, own_spectra(): pl.pallas_call(own_pass, out_shape=(SPECTRA, SPECTRA), in_specs=[HBM_SPEC...  4.28 us
    pallas_call x1, Pallas kernels, gradient_parts(): pl.pallas_call(below_pass, out_shape=jax.ShapeDtypeStruct((DP, FR, SPAN),...  4.13 us
    ppermute x3, waiting for transfers between devices, hop(): return lax.ppermute(block, 'facet', route)  4.07 us
    all_to_all x1, starting transfers between devices, gathered_sum(): mixed = lax.all_to_all(parts, 'dp', 0, 0)  3.46 us
  transfers between devices with their start and end apart: 4, of which 3 were waited for; matrix products, arithmetic and copies ran while one was open for 0% of the time, Pallas kernels for 8%

profile of v10, /device:TPU:1, one launch (start us, length us, event | category | flops | bytes accessed | tf_op | source)
XLA Modules:
  0.0 83.4 jit_solution(6262829632408902002)
XLA Ops:
  0.6 8.8 %collective-permute-start.1 = (bf16[64,16,128]{2,1,0:T(8,128)(2,1)}, bf16[64,16,128]{2,1,0:T(8,128)(2,1)S(1)}, u32[]{:S(2)}, u32[]{:S(2)}) collective-permute-start(bf16[64,16,128]{2,1,0:T(8,128)(2,1)} %bitcast.57), channel_id=1, source_target_pairs={{4,0},{8,4},{12,8},{16,12},{20,16},{24,20},{28,24},{32,28},{36,32}... | collective-permute-start | bytes 786440 | tf_op jit(solution)/shard_map/ppermute | solution.py:630
  10.1 2.1 %message.1 = bf16[4,16,128]{2,1,0:T(8,128)(2,1)} custom-call(s32[1]{0:T(128)} %bitcast.3.part_ref, s32[1,64]{1,0:T(1,128)} %starts_hbm.3, s32[1,64]{1,0:T(1,128)} %slots_hbm.3, s32[1,1]{1,0:T(1,128)S(6)} %copy.15.live_hbm, bf16[16,64]{1,0:T(8,128)(2,1)} %bitcast.53, bf16[4,48,2560]{2,1,0:T(8,128)(2,1)} %bitcast.38, ...), custom_call_target="tpu_custom_call" | custom-call | tf_op jit(solution)/shard_map/message/pallas_call | solution.py:505
  12.2 1.9 %collective-permute-start = (bf16[4,16,128]{2,1,0:T(8,128)(2,1)}, bf16[4,16,128]{2,1,0:T(8,128)(2,1)S(1)}, u32[]{:S(2)}, u32[]{:S(2)}) collective-permute-start(bf16[4,16,128]{2,1,0:T(8,128)(2,1)} %message.1), channel_id=1, source_target_pairs={{4,0},{8,4},{12,8},{16,12},{20,16},{24,20},{28,24},{32,28},{36,32}... | collective-permute-start | bytes 49160 | tf_op jit(solution)/shard_map/ppermute | solution.py:630
  14.1 4.3 %own_spectra.1 = (bf16[41,48,128]{2,1,0:T(8,128)(2,1)}, bf16[41,48,128]{2,1,0:T(8,128)(2,1)}) custom-call(s32[1,64]{1,0:T(1,128)} %starts_hbm.3, s32[1,64]{1,0:T(1,128)} %slots_hbm.3, s32[1,1]{1,0:T(1,128)S(6)} %copy.15.live_hbm, bf16[16,64]{1,0:T(8,128)(2,1)} %bitcast.54, bf16[64,16,128]{2,1,0:T(8,128)(2,1)} %bitcast.58, ...), custom_call_target="tpu_custom_call" | custom-call | flops 2000000000 | bytes 4000000 | tf_op jit(solution)/shard_map/own_spectra/pallas_call | solution.py:538
  18.4 3.3 %collective-permute-done.message_hbm.message_ref = bf16[4,16,128]{2,1,0:T(8,128)(2,1)S(1)} collective-permute-done((bf16[4,16,128]{2,1,0:T(8,128)(2,1)}, bf16[4,16,128]{2,1,0:T(8,128)(2,1)S(1)}, u32[]{:S(2)}, u32[]{:S(2)}) %collective-permute-start) | collective-permute-done | bytes 16416 | tf_op jit(solution)/shard_map/ppermute | solution.py:630
  21.7 0.0 copy-start.3
  21.7 0.0 collective-permute-done.1.payload_hbm
  21.7 0.0 copy-start.5
  21.7 0.6 copy-done.3
  22.3 0.1 copy-done.5
  22.4 0.0 copy-start
  22.4 0.0 copy-start.1
  22.4 4.1 %gradient_parts.1 = bf16[4,48,768]{2,1,0:T(8,128)(2,1)} custom-call(bf16[4,16,128]{2,1,0:T(8,128)(2,1)} %copy-done.3, bf16[64,16,128]{2,1,0:T(8,128)(2,1)} %copy-done.5, bf16[41,48,128]{2,1,0:T(8,128)(2,1)} %get-tuple-element.8.spec_hbm, bf16[41,48,128]{2,1,0:T(8,128)(2,1)} %get-tuple-element.9.own_hbm, bf16[5120,128]{1,0:T(8,128)(2,1)} %constant.13.clone.table_hbm), custom_call_target="tpu_custom_call" | custom-call | flops 2000000000 | bytes 4000000 | tf_op jit(solution)/shard_map/gradient_parts/pallas_call | solution.py:565
  26.5 3.5 %all-to-all-start = ((bf16[4,48,768]{2,1,0:T(8,128)(2,1)}), bf16[4,48,768]{2,1,0:T(8,128)(2,1)S(1)}, u32[]{:S(2)}, u32[]{:S(2)}) async-start(bf16[4,48,768]{2,1,0:T(8,128)(2,1)} %gradient_parts.1), calls=%async_computation | async-start | bytes 589824 | tf_op jit(solution)/shard_map/all_to_all | solution.py:634
  30.0 0.0 copy-done
  30.0 0.0 copy-done.1
  30.0 0.0 copy-start.4
  30.0 0.7 copy-done.4
  30.7 0.0 copy-start.2
  30.7 0.6 synthesized.1
  31.3 4.3 %all-to-all-done = bf16[4,48,768]{2,1,0:T(8,128)(2,1)S(1)} async-done(((bf16[4,48,768]{2,1,0:T(8,128)(2,1)}), bf16[4,48,768]{2,1,0:T(8,128)(2,1)S(1)}, u32[]{:S(2)}, u32[]{:S(2)}) %all-to-all-start) | async-done | bytes 294944 | tf_op jit(solution)/shard_map/all_to_all | solution.py:634
  35.7 0.0 copy-done.2
  35.7 0.1 subtract_select_fusion
  35.8 4.8 %collective-permute-start.2 = (bf16[8,768]{1,0:T(8,128)(2,1)S(1)}, bf16[8,768]{1,0:T(8,128)(2,1)S(1)}, u32[]{:S(2)}, u32[]{:S(2)}) collective-permute-start(bf16[8,768]{1,0:T(8,128)(2,1)S(1)} %slice.275), channel_id=1, source_target_pairs={{0,4},{4,8},{8,12},{12,16},{16,20},{20,24},{24,28},{28,32},{32,36}... | collective-permute-start | bytes 36872 | tf_op jit(solution)/shard_map/ppermute | solution.py:630
  40.6 0.8 collective-permute-done.2
  41.4 0.2 multiply_add_fusion.1
  41.6 0.3 multiply_add_fusion.5
  41.9 0.3 multiply_add_fusion.3
  42.2 0.1 fusion.5
  42.3 19.7 %all_gather.4 = bf16[4,4,48,640]{3,2,1,0:T(8,128)(2,1)S(1)} all-gather(bf16[1,4,48,640]{3,2,1,0:T(8,128)(2,1)S(1)} %fusion.5), channel_id=1, replica_groups=mesh['cube'=4,'facet'=32,'dp'=4] {'cube'}, dimensions={0}, use_global_device_ids=true | all-gather | bytes 1228800 | tf_op jit(solution)/shard_map/all_gather | solution.py:680
  62.0 0.1 convert_reduce_fusion
  62.1 0.3 fusion.2
  62.4 0.1 broadcast_in_dim.16
  62.5 19.7 %all_to_all.10.parts_ref = bf16[4,5,48,640]{3,2,1,0:T(8,128)(2,1)S(1)} all-to-all(bf16[4,5,48,640]{3,2,1,0:T(8,128)(2,1)S(1)} %broadcast_in_dim.16), channel_id=1, replica_groups=mesh['cube'=4,'facet'=32,'dp'=4] {'dp'}, dimensions={0} | all-to-all | bytes 2457600 | tf_op jit(solution)/shard_map/all_to_all | solution.py:684
  82.3 1.1 %finished.1 = (f32[48,2560]{1,0:T(8,128)}, bf16[4,48,2560]{2,1,0:T(8,128)(2,1)}) custom-call(bf16[4,5,48,640]{3,2,1,0:T(8,128)(2,1)S(1)} %all_to_all.10.parts_ref, f32[48,2560]{1,0:T(8,128)S(1)} %bitcast.44), custom_call_target="tpu_custom_call" | custom-call | tf_op jit(solution)/shard_map/finished/pallas_call | solution.py:613
  (6 shorter events, 0.1 us)
Async XLA Ops:
  0.6 21.0 %collective-permute-start.1 = (bf16[64,16,128]{2,1,0:T(8,128)(2,1)}, bf16[64,16,128]{2,1,0:T(8,128)(2,1)S(1)}, u32[]{:S(2)}, u32[]{:S(2)}) collective-permute-start(bf16[64,16,128]{2,1,0:T(8,128)(2,1)} %bitcast.57), channel_id=1, source_target_pairs={{4,0},{8,4},{12,8},{16,12},{20,16},{24,20},{28,24},{32,28},{36,32}... | collective-permute-start | bytes 786440 | tf_op jit(solution)/shard_map/ppermute | solution.py:630
  12.2 9.5 %collective-permute-start = (bf16[4,16,128]{2,1,0:T(8,128)(2,1)}, bf16[4,16,128]{2,1,0:T(8,128)(2,1)S(1)}, u32[]{:S(2)}, u32[]{:S(2)}) collective-permute-start(bf16[4,16,128]{2,1,0:T(8,128)(2,1)} %message.1), channel_id=1, source_target_pairs={{4,0},{8,4},{12,8},{16,12},{20,16},{24,20},{28,24},{32,28},{36,32}... | collective-permute-start | bytes 49160 | tf_op jit(solution)/shard_map/ppermute | solution.py:630
  21.7 0.6 copy-start.3
  21.7 0.7 copy-start.5
  22.4 7.6 %copy-start = (bf16[3072,256]{1,0:T(8,128)(2,1)S(1)}, bf16[3072,256]{1,0:T(8,128)(2,1)}, u32[]{:S(2)}) copy-start(bf16[3072,256]{1,0:T(8,128)(2,1)} %constant.12.clone.filters_hbm.table_hbm.constants_ref) | copy-start | bytes 4718596
  22.4 7.6 %copy-start.1 = (bf16[4,1,48,2560]{3,2,1,0:T(8,128)(2,1)S(1)}, bf16[4,1,48,2560]{3,2,1,0:T(8,128)(2,1)}, u32[]{:S(2)}) copy-start(bf16[4,1,48,2560]{3,2,1,0:T(8,128)(2,1)} %param.10) | copy-start | bytes 2949124
  26.5 9.1 %all-to-all-start = ((bf16[4,48,768]{2,1,0:T(8,128)(2,1)}), bf16[4,48,768]{2,1,0:T(8,128)(2,1)S(1)}, u32[]{:S(2)}, u32[]{:S(2)}) async-start(bf16[4,48,768]{2,1,0:T(8,128)(2,1)} %gradient_parts.1), calls=%async_computation | async-start | bytes 589824 | tf_op jit(solution)/shard_map/all_to_all | solution.py:634
  30.0 0.7 copy-start.4
  30.7 5.0 %copy-start.2 = (f32[1,48,2560]{2,1,0:T(8,128)S(1)}, f32[1,48,2560]{2,1,0:T(8,128)}, u32[]{:S(2)}) copy-start(f32[1,48,2560]{2,1,0:T(8,128)} %param.9) | copy-start | bytes 1474564
  35.8 5.6 %collective-permute-start.2 = (bf16[8,768]{1,0:T(8,128)(2,1)S(1)}, bf16[8,768]{1,0:T(8,128)(2,1)S(1)}, u32[]{:S(2)}, u32[]{:S(2)}) collective-permute-start(bf16[8,768]{1,0:T(8,128)(2,1)S(1)} %slice.275), channel_id=1, source_target_pairs={{0,4},{4,8},{8,12},{12,16},{16,20},{20,24},{24,28},{28,32},{32,36}... | collective-permute-start | bytes 36872 | tf_op jit(solution)/shard_map/ppermute | solution.py:630

commit v11 on v10

--- a/solution.py
+++ b/solution.py
@@ -45,7 +45,7 @@
 HALO = 128
 SPAN = PART + HALO
 CHUNKS = W // 64
-UNROLL = 8
+UNROLL = 16
 VMEM_LIMIT = 60 * 1024 * 1024
 NORM = 1.0 / math.sqrt(W)
 C1, C2 = math.cos(2 * math.pi / 5), math.cos(4 * math.pi / 5)
@@ -217,40 +217,10 @@
     return value
 
 
-def write_message(
-    part_ref,
-    starts_hbm,
-    slots_hbm,
-    live_hbm,
-    weight_hbm,
-    dual_hbm,
-    filters_hbm,
-    out_ref,
-    starts_ref,
-    slots_ref,
-    live_ref,
-    weight_ref,
-    dual_ref,
-    filters_ref,
-    rows_ref,
-    sems,
-):
-    pairs = [
-        (dual_hbm.at[:, :TILE, :], dual_ref),
-        (filters_hbm.at[pl.ds(Q * R, 4 * HALO), :], filters_ref),
-        (starts_hbm, starts_ref),
-        (slots_hbm, slots_ref),
-        (live_hbm, live_ref),
-        (weight_hbm, weight_ref),
-    ]
-    copies = [pltpu.make_async_copy(s, d, sems.at[i]) for i, (s, d) in enumerate(pairs)]
-    for copy in copies:
-        copy.start()
+def fill_message(part, starts, slots, live, weights, dual_ref, filters_ref, rows_ref, out_ref):
     rows_ref[:, :8, :] = jnp.zeros((2, 8, SPAN), jnp.float32)
-    copies[0].wait()
-    copies[1].wait()
     columns_back(
-        part_ref[0],
+        part,
         TILE,
         dual_ref,
         lambda i: filters_ref[2 * HALO * i : 2 * HALO * (i + 1)],
@@ -259,16 +229,11 @@
     for i in range(SPAN // HALO // 2):
         pair = [rows_back(-8, 8, pl.ds(HALO * (2 * i + j), HALO), rows_ref) for j in range(2)]
         out_ref[1 + i] = jnp.concatenate(pair, 0).astype(jnp.bfloat16)
-    for copy in copies[2:]:
-        copy.wait()
     row = lax.broadcasted_iota(jnp.int32, (TILE, BLK), 0)
-    starts = starts_ref[...]
     numbers = jnp.where(row == 0, starts >> 6, starts & 63)
-    numbers = jnp.where(row == 2, slots_ref[...], numbers)
-    numbers = jnp.where(row == 3, live_ref[0, 0], numbers)
-    out_ref[0] = jnp.concatenate(
-        [weight_ref[...].astype(jnp.float32), numbers.astype(jnp.float32)], 1
-    ).astype(jnp.bfloat16)
+    numbers = jnp.where(row == 2, slots, numbers)
+    numbers = jnp.where(row == 3, live, numbers)
+    out_ref[0] = jnp.concatenate([weights, numbers.astype(jnp.float32)], 1).astype(jnp.bfloat16)
 
 
 def synthesis(part_ref, message_ref, dual_ref, constants_ref, synth_ref, rows_ref):
@@ -288,6 +253,7 @@
 
 
 def own_pass(
+    part_ref,
     starts_hbm,
     slots_hbm,
     live_hbm,
@@ -295,12 +261,19 @@
     payload_hbm,
     table_hbm,
     pixels_hbm,
+    dual_hbm,
     spec_ref,
     own_ref,
+    message_ref,
     starts_ref,
     slots_ref,
     live_ref,
     list_ref,
+    starts_vec,
+    slots_vec,
+    dual_ref,
+    filters_ref,
+    rows_ref,
     weight_ref,
     payload_ref,
     table_ref,
@@ -319,6 +292,10 @@
         (starts_hbm, starts_ref),
         (slots_hbm, slots_ref),
         (live_hbm, live_ref),
+        (starts_hbm, starts_vec),
+        (slots_hbm, slots_vec),
+        (dual_hbm.at[:, :TILE, :], dual_ref),
+        (table_hbm.at[pl.ds(Q * R, 4 * HALO), :], filters_ref),
     ]
     copies = [pltpu.make_async_copy(s, d, sems.at[i]) for i, (s, d) in enumerate(pairs)]
     for copy in copies:
@@ -370,7 +347,19 @@
     for copy in copies[2:]:
         copy.wait()
     blank = jnp.zeros((TILE, 128 - BLK), jnp.float32)
-    weights = jnp.concatenate([weight_ref[...].astype(jnp.float32), blank], 1)
+    weights = weight_ref[...].astype(jnp.float32)
+    fill_message(
+        part_ref[0],
+        starts_vec[...],
+        slots_vec[...],
+        live_ref[0, 0],
+        weights,
+        dual_ref,
+        filters_ref,
+        rows_ref,
+        message_ref,
+    )
+    weights = jnp.concatenate([weights, blank], 1)
     add_blocks(
         PER,
         lambda b: (starts_ref[0, b] >> 6, starts_ref[0, b] & 63),
@@ -501,27 +490,6 @@
 COST = pl.CostEstimate(flops=2 * 10**9, bytes_accessed=4 * 10**6, transcendentals=0)
 
 
-def message(part, starts, slots, live, weights, dual, table):
-    return pl.pallas_call(
-        write_message,
-        out_shape=jax.ShapeDtypeStruct((1 + SPAN // HALO // 2, TILE, 128), jnp.bfloat16),
-        in_specs=[SMEM_SPEC] + [HBM_SPEC] * 6,
-        out_specs=VMEM_SPEC,
-        scratch_shapes=[
-            pltpu.VMEM((1, BLK), jnp.int32),
-            pltpu.VMEM((1, BLK), jnp.int32),
-            pltpu.SMEM((1, 1), jnp.int32),
-            pltpu.VMEM((TILE, BLK), jnp.bfloat16),
-            pltpu.VMEM((4, TILE, W), jnp.bfloat16),
-            pltpu.VMEM((4 * HALO, 2 * HALO), jnp.bfloat16),
-            pltpu.VMEM((2, 8 + TILE, SPAN), jnp.float32),
-            pltpu.SemaphoreType.DMA((6,)),
-        ],
-        compiler_params=PARAMS,
-        name="message",
-    )(part, starts, slots, live, weights, dual, table)
-
-
 def synthesized(part, received, dual, table):
     return pl.pallas_call(
         synthesis,
@@ -534,17 +502,26 @@
     )(part, received, dual, table)
 
 
-def own_spectra(starts, slots, live, weights, payload, table, pixels):
+def own_spectra(part, starts, slots, live, weights, payload, table, pixels, dual):
     return pl.pallas_call(
         own_pass,
-        out_shape=(SPECTRA, SPECTRA),
-        in_specs=[HBM_SPEC] * 7,
-        out_specs=(VMEM_SPEC,) * 2,
+        out_shape=(
+            SPECTRA,
+            SPECTRA,
+            jax.ShapeDtypeStruct((1 + SPAN // HALO // 2, TILE, 128), jnp.bfloat16),
+        ),
+        in_specs=[SMEM_SPEC] + [HBM_SPEC] * 8,
+        out_specs=(VMEM_SPEC,) * 3,
         scratch_shapes=[
             pltpu.SMEM((1, BLK), jnp.int32),
             pltpu.SMEM((1, BLK), jnp.int32),
             pltpu.SMEM((1, 1), jnp.int32),
             pltpu.SMEM((BLK + UNROLL,), jnp.int32),
+            pltpu.VMEM((1, BLK), jnp.int32),
+            pltpu.VMEM((1, BLK), jnp.int32),
+            pltpu.VMEM((4, TILE, W), jnp.bfloat16),
+            pltpu.VMEM((4 * HALO, 2 * HALO), jnp.bfloat16),
+            pltpu.VMEM((2, 8 + TILE, SPAN), jnp.float32),
             pltpu.VMEM((TILE, BLK), jnp.bfloat16),
             pltpu.VMEM((BLK, TILE, 128), jnp.bfloat16),
             TABLE,
@@ -553,12 +530,12 @@
             pltpu.VMEM((Q, FR, R), jnp.float32),
             pltpu.VMEM((Q, FR, R), jnp.float32),
             pltpu.VMEM((CHUNKS + 1, FR, 128), jnp.float32),
-            pltpu.SemaphoreType.DMA((7,)),
+            pltpu.SemaphoreType.DMA((11,)),
         ],
         compiler_params=PARAMS,
         cost_estimate=COST,
         name="own_spectra",
-    )(starts, slots, live, weights, payload, table, pixels)
+    )(part, starts, slots, live, weights, payload, table, pixels, dual)
 
 
 def gradient_parts(received, payload, spectra, own, table):
@@ -653,19 +630,16 @@
     part = position[None]
     weights = vis_weight[0].T
     payload_below = hop(payload[0], -1)
-    received = hop(
-        message(part, freq_start, tile_slot, live, weights, dual[:, 0], table), -1
-    )
-
     left = position * PART
     own_dual = lax.dynamic_slice_in_dim(dual[:, 0], left, PART, 2).astype(jnp.float32)
     old = lax.dynamic_slice_in_dim(
         jnp.pad(own_rows, ((0, 0), (HALO, 0))), left, SPAN, 1
     )
 
-    spectra, own = own_spectra(
-        freq_start, tile_slot, live, weights, payload[0], table, own_rows
-    )
+    spectra, own, sent = own_spectra(
+        part, freq_start, tile_slot, live, weights, payload[0], table, own_rows, dual[:, 0]
+    )
+    received = hop(sent, -1)
     terms = gradient_parts(received, payload_below, spectra, own, flipped)
     terms, received = lax.optimization_barrier((terms, received))
     synth = synthesized(part, received, dual[:, 0], table)

time: 84.6 us -> 84.2 us (level)
  waiting for transfers between devices: 8.39 us -> 12.5 us
  Pallas kernels: 12.2 us -> 9.95 us
  starting transfers between devices: 18.9 us -> 17.7 us
  blocking collectives: 39.4 us -> 38.5 us
    ppermute x3, waiting for transfers between devices: 4.07 us -> 8.17 us  [hop(): return lax.ppermute(block, 'facet', route)]
    pallas_call x2 -> x1, Pallas kernels: 6.38 us -> 3.94 us  [own_spectra(): pl.pallas_call(own_pass, out_shape=(SPECTRA, SPECTRA, jax.ShapeDtypeStruc...]
    ppermute x3, starting transfers between devices: 15.5 us -> 14.3 us  [hop(): return lax.ppermute(block, 'facet', route)]
  transfers between devices with their start and end apart: 4 -> 4, of which waited for: 3 -> 3; matrix products, arithmetic and copies ran while one was open for 0% -> 0% of each run, Pallas kernels for 8% -> 5%
where the time goes in v11:
time: 84.2 us; the launch traced here: 83.1 us
  blocking collectives  38.5 us (46%)
  starting transfers between devices  17.7 us (21%)
  waiting for transfers between devices  12.5 us (15%)
  Pallas kernels  9.95 us (12%)
  local copies, waits for them, and re-layouts  1.53 us (2%)
  between operations  1.45 us (2%)
  other arithmetic  1.42 us (2%)
    all_gather x1, blocking collectives, on_device(): squares = lax.all_gather((shifted * shifted).astype(jnp.bfloat16), 'cube')  19.6 us
    all_to_all x1, blocking collectives, on_device(): lax.all_to_all(jnp.broadcast_to(own_part, (DP,) + own_part.shape), 'dp',...  18.9 us
    ppermute x3, starting transfers between devices, hop(): return lax.ppermute(block, 'facet', route)  14.3 us
    ppermute x3, waiting for transfers between devices, hop(): return lax.ppermute(block, 'facet', route)  8.17 us
    all_to_all x1, waiting for transfers between devices, gathered_sum(): mixed = lax.all_to_all(parts, 'dp', 0, 0)  4.32 us
    pallas_call x1, Pallas kernels, gradient_parts(): pl.pallas_call(below_pass, out_shape=jax.ShapeDtypeStruct((DP, FR, SPAN),...  4.29 us
    pallas_call x1, Pallas kernels, own_spectra(): pl.pallas_call(own_pass, out_shape=(SPECTRA, SPECTRA, jax.ShapeDtypeStruc...  3.94 us
    all_to_all x1, starting transfers between devices, gathered_sum(): mixed = lax.all_to_all(parts, 'dp', 0, 0)  3.46 us
  transfers between devices with their start and end apart: 4, of which 3 were waited for; matrix products, arithmetic and copies ran while one was open for 0% of the time, Pallas kernels for 5%

profile of v11, /device:TPU:1, one launch (start us, length us, event | category | flops | bytes accessed | tf_op | source)
XLA Modules:
  0.0 83.1 jit_solution(7788125089284575171)
XLA Ops:
  0.6 8.8 %collective-permute-start.1 = (bf16[64,16,128]{2,1,0:T(8,128)(2,1)}, bf16[64,16,128]{2,1,0:T(8,128)(2,1)S(1)}, u32[]{:S(2)}, u32[]{:S(2)}) collective-permute-start(bf16[64,16,128]{2,1,0:T(8,128)(2,1)} %bitcast.55), channel_id=1, source_target_pairs={{4,0},{8,4},{12,8},{16,12},{20,16},{24,20},{28,24},{32,28},{36,32}... | collective-permute-start | bytes 786440 | tf_op jit(solution)/shard_map/ppermute | solution.py:607
  10.1 3.9 %own_spectra.1 = (bf16[41,48,128]{2,1,0:T(8,128)(2,1)}, bf16[41,48,128]{2,1,0:T(8,128)(2,1)}, bf16[4,16,128]{2,1,0:T(8,128)(2,1)}) custom-call(s32[1]{0:T(128)} %bitcast.3.part_ref, s32[1,64]{1,0:T(1,128)} %starts_hbm.1, s32[1,64]{1,0:T(1,128)} %slots_hbm.1, s32[1,1]{1,0:T(1,128)S(6)} %copy.15.live_hbm, bf16[16,64]{1,0:T(8,128)(2,1)} %bitcast.57, ...), custom_call_target="tpu_custom_call" | custom-call | flops 2000000000 | bytes 4000000 | tf_op jit(solution)/shard_map/own_spectra/pallas_call | solution.py:506
  14.0 1.9 %collective-permute-start = (bf16[4,16,128]{2,1,0:T(8,128)(2,1)}, bf16[4,16,128]{2,1,0:T(8,128)(2,1)S(1)}, u32[]{:S(2)}, u32[]{:S(2)}) collective-permute-start(bf16[4,16,128]{2,1,0:T(8,128)(2,1)} %get-tuple-element.9), channel_id=1, source_target_pairs={{4,0},{8,4},{12,8},{16,12},{20,16},{24,20},{28,24},{32,28},{36,32}... | collective-permute-start | bytes 49160 | tf_op jit(solution)/shard_map/ppermute | solution.py:607
  15.9 7.4 %collective-permute-done.message_hbm.message_ref = bf16[4,16,128]{2,1,0:T(8,128)(2,1)S(1)} collective-permute-done((bf16[4,16,128]{2,1,0:T(8,128)(2,1)}, bf16[4,16,128]{2,1,0:T(8,128)(2,1)S(1)}, u32[]{:S(2)}, u32[]{:S(2)}) %collective-permute-start) | collective-permute-done | bytes 16416 | tf_op jit(solution)/shard_map/ppermute | solution.py:607
  23.3 0.0 copy-start.3
  23.3 0.0 collective-permute-done.1.payload_hbm
  23.3 0.0 copy-start.5
  23.3 0.6 copy-done.3
  23.9 0.1 copy-done.5
  24.0 0.0 copy-start
  24.0 0.0 copy-start.2
  24.0 4.3 %gradient_parts.1 = bf16[4,48,768]{2,1,0:T(8,128)(2,1)} custom-call(bf16[4,16,128]{2,1,0:T(8,128)(2,1)} %copy-done.3, bf16[64,16,128]{2,1,0:T(8,128)(2,1)} %copy-done.5, bf16[41,48,128]{2,1,0:T(8,128)(2,1)} %get-tuple-element.10.spec_hbm, bf16[41,48,128]{2,1,0:T(8,128)(2,1)} %get-tuple-element.11.own_hbm, bf16[5120,128]{1,0:T(8,128)(2,1)} %constant.13.clone.table_hbm), custom_call_target="tpu_custom_call" | custom-call | flops 2000000000 | bytes 4000000 | tf_op jit(solution)/shard_map/gradient_parts/pallas_call | solution.py:542
  28.3 3.5 %all-to-all-start = ((bf16[4,48,768]{2,1,0:T(8,128)(2,1)}), bf16[4,48,768]{2,1,0:T(8,128)(2,1)S(1)}, u32[]{:S(2)}, u32[]{:S(2)}) async-start(bf16[4,48,768]{2,1,0:T(8,128)(2,1)} %gradient_parts.1), calls=%async_computation | async-start | bytes 589824 | tf_op jit(solution)/shard_map/all_to_all | solution.py:611
  31.8 0.0 copy-done
  31.8 0.0 copy-done.2
  31.8 0.0 copy-start.4
  31.8 0.7 copy-done.4
  32.6 0.0 copy-start.1
  32.6 0.6 synthesized.1
  33.1 4.3 %all-to-all-done = bf16[4,48,768]{2,1,0:T(8,128)(2,1)S(1)} async-done(((bf16[4,48,768]{2,1,0:T(8,128)(2,1)}), bf16[4,48,768]{2,1,0:T(8,128)(2,1)S(1)}, u32[]{:S(2)}, u32[]{:S(2)}) %all-to-all-start) | async-done | bytes 294944 | tf_op jit(solution)/shard_map/all_to_all | solution.py:611
  37.5 0.0 copy-done.1
  37.5 0.1 subtract_select_fusion
  37.6 3.5 %collective-permute-start.2 = (bf16[8,768]{1,0:T(8,128)(2,1)S(1)}, bf16[8,768]{1,0:T(8,128)(2,1)S(1)}, u32[]{:S(2)}, u32[]{:S(2)}) collective-permute-start(bf16[8,768]{1,0:T(8,128)(2,1)S(1)} %slice.275), channel_id=1, source_target_pairs={{0,4},{4,8},{8,12},{12,16},{16,20},{20,24},{24,28},{28,32},{32,36}... | collective-permute-start | bytes 36872 | tf_op jit(solution)/shard_map/ppermute | solution.py:607
  41.2 0.8 collective-permute-done.2
  42.0 0.2 multiply_add_fusion.1
  42.2 0.3 multiply_add_fusion.5
  42.5 0.3 multiply_add_fusion.3
  42.8 0.1 fusion.5
  42.9 19.6 %all_gather.4 = bf16[4,4,48,640]{3,2,1,0:T(8,128)(2,1)S(1)} all-gather(bf16[1,4,48,640]{3,2,1,0:T(8,128)(2,1)S(1)} %fusion.5), channel_id=1, replica_groups=mesh['cube'=4,'facet'=32,'dp'=4] {'cube'}, dimensions={0}, use_global_device_ids=true | all-gather | bytes 1228800 | tf_op jit(solution)/shard_map/all_gather | solution.py:654
  62.5 0.1 convert_reduce_fusion
  62.6 0.2 fusion.2
  62.9 0.1 broadcast_in_dim.16
  63.0 18.9 %all_to_all.10.parts_ref = bf16[4,5,48,640]{3,2,1,0:T(8,128)(2,1)S(1)} all-to-all(bf16[4,5,48,640]{3,2,1,0:T(8,128)(2,1)S(1)} %broadcast_in_dim.16), channel_id=1, replica_groups=mesh['cube'=4,'facet'=32,'dp'=4] {'dp'}, dimensions={0} | all-to-all | bytes 2457600 | tf_op jit(solution)/shard_map/all_to_all | solution.py:658
  82.0 1.1 %finished.1 = (f32[48,2560]{1,0:T(8,128)}, bf16[4,48,2560]{2,1,0:T(8,128)(2,1)}) custom-call(bf16[4,5,48,640]{3,2,1,0:T(8,128)(2,1)S(1)} %all_to_all.10.parts_ref, f32[48,2560]{1,0:T(8,128)S(1)} %bitcast.44), custom_call_target="tpu_custom_call" | custom-call | tf_op jit(solution)/shard_map/finished/pallas_call | solution.py:590
  (6 shorter events, 0.1 us)
Async XLA Ops:
  0.6 22.7 %collective-permute-start.1 = (bf16[64,16,128]{2,1,0:T(8,128)(2,1)}, bf16[64,16,128]{2,1,0:T(8,128)(2,1)S(1)}, u32[]{:S(2)}, u32[]{:S(2)}) collective-permute-start(bf16[64,16,128]{2,1,0:T(8,128)(2,1)} %bitcast.55), channel_id=1, source_target_pairs={{4,0},{8,4},{12,8},{16,12},{20,16},{24,20},{28,24},{32,28},{36,32}... | collective-permute-start | bytes 786440 | tf_op jit(solution)/shard_map/ppermute | solution.py:607
  14.0 9.3 %collective-permute-start = (bf16[4,16,128]{2,1,0:T(8,128)(2,1)}, bf16[4,16,128]{2,1,0:T(8,128)(2,1)S(1)}, u32[]{:S(2)}, u32[]{:S(2)}) collective-permute-start(bf16[4,16,128]{2,1,0:T(8,128)(2,1)} %get-tuple-element.9), channel_id=1, source_target_pairs={{4,0},{8,4},{12,8},{16,12},{20,16},{24,20},{28,24},{32,28},{36,32}... | collective-permute-start | bytes 49160 | tf_op jit(solution)/shard_map/ppermute | solution.py:607
  23.3 0.6 copy-start.3
  23.3 0.7 copy-start.5
  24.0 7.8 %copy-start = (bf16[4,1,48,2560]{3,2,1,0:T(8,128)(2,1)S(1)}, bf16[4,1,48,2560]{3,2,1,0:T(8,128)(2,1)}, u32[]{:S(2)}) copy-start(bf16[4,1,48,2560]{3,2,1,0:T(8,128)(2,1)} %param.10) | copy-start | bytes 2949124
  24.0 7.8 %copy-start.2 = (bf16[3072,256]{1,0:T(8,128)(2,1)S(1)}, bf16[3072,256]{1,0:T(8,128)(2,1)}, u32[]{:S(2)}) copy-start(bf16[3072,256]{1,0:T(8,128)(2,1)} %constant.12.clone.table_hbm.constants_ref) | copy-start | bytes 4718596
  28.3 9.1 %all-to-all-start = ((bf16[4,48,768]{2,1,0:T(8,128)(2,1)}), bf16[4,48,768]{2,1,0:T(8,128)(2,1)S(1)}, u32[]{:S(2)}, u32[]{:S(2)}) async-start(bf16[4,48,768]{2,1,0:T(8,128)(2,1)} %gradient_parts.1), calls=%async_computation | async-start | bytes 589824 | tf_op jit(solution)/shard_map/all_to_all | solution.py:611
  31.8 0.7 copy-start.4
  32.6 5.0 %copy-start.1 = (f32[1,48,2560]{2,1,0:T(8,128)S(1)}, f32[1,48,2560]{2,1,0:T(8,128)}, u32[]{:S(2)}) copy-start(f32[1,48,2560]{2,1,0:T(8,128)} %param.9) | copy-start | bytes 1474564
  37.6 4.4 %collective-permute-start.2 = (bf16[8,768]{1,0:T(8,128)(2,1)S(1)}, bf16[8,768]{1,0:T(8,128)(2,1)S(1)}, u32[]{:S(2)}, u32[]{:S(2)}) collective-permute-start(bf16[8,768]{1,0:T(8,128)(2,1)S(1)} %slice.275), channel_id=1, source_target_pairs={{0,4},{4,8},{8,12},{12,16},{16,20},{20,24},{24,28},{28,32},{32,36}... | collective-permute-start | bytes 36872 | tf_op jit(solution)/shard_map/ppermute | solution.py:607

commit v12 on v11

--- a/solution.py
+++ b/solution.py
@@ -612,10 +612,10 @@
     return jnp.sum(mixed.astype(jnp.float32), 0)
 
 
-def analyze(extra):
+def analyze(extra, first, count):
     subbands = []
     for row_taps in (LOWPASS, HIGHPASS):
-        filtered = sum(row_taps[k] * extra[8 - k : 8 - k + FR] for k in range(8))
+        filtered = sum(row_taps[k] * extra[first - k : first - k + count] for k in range(8))
         for col_taps in (LOWPASS, HIGHPASS):
             subbands.append(
                 sum(col_taps[k] * filtered[:, HALO - k : HALO - k + PART] for k in range(8))
@@ -648,9 +648,11 @@
     column = lax.broadcasted_iota(jnp.int32, old.shape, 1) + left
     extra = jnp.where(column >= HALO, 2.0 * new - old, 0.0)
     extra_above = hop(extra[FR - 8 :].astype(jnp.bfloat16), 1).astype(jnp.float32)
-    extra = jnp.concatenate([extra_above, extra], 0)
-
-    shifted = own_dual + SIGMA_STEP * analyze(extra)
+    lower = own_dual[:, 8:] + SIGMA_STEP * analyze(extra, 8, FR - 8)
+    lower, extra_above = lax.optimization_barrier((lower, extra_above))
+    top = jnp.concatenate([extra_above, extra[:8]], 0)
+    upper = own_dual[:, :8] + SIGMA_STEP * analyze(top, 8, 8)
+    shifted = jnp.concatenate([upper, lower], 1)
     squares = lax.all_gather((shifted * shifted).astype(jnp.bfloat16), "cube")
     norms = jnp.sqrt(jnp.sum(squares.astype(jnp.float32), 0))
     dual_part = (shifted * (RADIUS / jnp.maximum(norms, RADIUS))).astype(jnp.bfloat16)

time: 84.2 us -> 84.1 us (level)
  blocking collectives: 38.5 us -> 39.5 us
  other arithmetic: 1.42 us -> 2.38 us
  transfers between devices with their start and end apart: 4 -> 4, of which waited for: 3 -> 3; matrix products, arithmetic and copies ran while one was open for 0% -> 2% of each run, Pallas kernels for 5% -> 6%
where the time goes in v12:
time: 84.1 us; the launch traced here: 83.7 us
  blocking collectives  39.5 us (47%)
  starting transfers between devices  17.7 us (21%)
  waiting for transfers between devices  11.8 us (14%)
  Pallas kernels  10 us (12%)
  other arithmetic  2.38 us (3%)
  between operations  1.51 us (2%)
    all_gather x1, blocking collectives, on_device(): squares = lax.all_gather((shifted * shifted).astype(jnp.bfloat16), 'cube')  19.8 us
    all_to_all x1, blocking collectives, on_device(): lax.all_to_all(jnp.broadcast_to(own_part, (DP,) + own_part.shape), 'dp',...  19.7 us
    ppermute x3, starting transfers between devices, hop(): return lax.ppermute(block, 'facet', route)  14.2 us
    ppermute x3, waiting for transfers between devices, hop(): return lax.ppermute(block, 'facet', route)  7.56 us
    pallas_call x1, Pallas kernels, own_spectra(): pl.pallas_call(own_pass, out_shape=(SPECTRA, SPECTRA, jax.ShapeDtypeStruc...  4.38 us
    all_to_all x1, waiting for transfers between devices, gathered_sum(): mixed = lax.all_to_all(parts, 'dp', 0, 0)  4.23 us
    pallas_call x1, Pallas kernels, gradient_parts(): pl.pallas_call(below_pass, out_shape=jax.ShapeDtypeStruct((DP, FR, SPAN),...  3.89 us
    all_to_all x1, starting transfers between devices, gathered_sum(): mixed = lax.all_to_all(parts, 'dp', 0, 0)  3.46 us
  transfers between devices with their start and end apart: 4, of which 3 were waited for; matrix products, arithmetic and copies ran while one was open for 2% of the time, Pallas kernels for 6%

profile of v12, /device:TPU:1, one launch (start us, length us, event | category | flops | bytes accessed | tf_op | source)
XLA Modules:
  0.0 83.7 jit_solution(12359419760572194263)
XLA Ops:
  0.6 8.8 %collective-permute-start.1 = (bf16[64,16,128]{2,1,0:T(8,128)(2,1)}, bf16[64,16,128]{2,1,0:T(8,128)(2,1)S(1)}, u32[]{:S(2)}, u32[]{:S(2)}) collective-permute-start(bf16[64,16,128]{2,1,0:T(8,128)(2,1)} %bitcast.45), channel_id=1, source_target_pairs={{4,0},{8,4},{12,8},{16,12},{20,16},{24,20},{28,24},{32,28},{36,32}... | collective-permute-start | bytes 786440 | tf_op jit(solution)/shard_map/ppermute | solution.py:607
  10.1 4.4 %own_spectra.1 = (bf16[41,48,128]{2,1,0:T(8,128)(2,1)}, bf16[41,48,128]{2,1,0:T(8,128)(2,1)}, bf16[4,16,128]{2,1,0:T(8,128)(2,1)}) custom-call(s32[1]{0:T(128)} %bitcast.3.part_ref, s32[1,64]{1,0:T(1,128)} %starts_hbm.1, s32[1,64]{1,0:T(1,128)} %slots_hbm.1, s32[1,1]{1,0:T(1,128)S(6)} %copy.15.live_hbm, bf16[16,64]{1,0:T(8,128)(2,1)} %bitcast.47, ...), custom_call_target="tpu_custom_call" | custom-call | flops 2000000000 | bytes 4000000 | tf_op jit(solution)/shard_map/own_spectra/pallas_call | solution.py:506
  14.5 1.9 %collective-permute-start = (bf16[4,16,128]{2,1,0:T(8,128)(2,1)}, bf16[4,16,128]{2,1,0:T(8,128)(2,1)S(1)}, u32[]{:S(2)}, u32[]{:S(2)}) collective-permute-start(bf16[4,16,128]{2,1,0:T(8,128)(2,1)} %get-tuple-element.11), channel_id=1, source_target_pairs={{4,0},{8,4},{12,8},{16,12},{20,16},{24,20},{28,24},{32,28},{36,32}... | collective-permute-start | bytes 49160 | tf_op jit(solution)/shard_map/ppermute | solution.py:607
  16.4 7.4 %collective-permute-done.message_hbm.message_ref = bf16[4,16,128]{2,1,0:T(8,128)(2,1)S(1)} collective-permute-done((bf16[4,16,128]{2,1,0:T(8,128)(2,1)}, bf16[4,16,128]{2,1,0:T(8,128)(2,1)S(1)}, u32[]{:S(2)}, u32[]{:S(2)}) %collective-permute-start) | collective-permute-done | bytes 16416 | tf_op jit(solution)/shard_map/ppermute | solution.py:607
  23.8 0.0 copy-start.3
  23.8 0.0 collective-permute-done.1.payload_hbm
  23.8 0.0 copy-start.6
  23.8 0.6 copy-done.3
  24.4 0.1 copy-done.6
  24.5 0.0 copy-start.2
  24.5 0.0 copy-start.1
  24.5 3.9 %gradient_parts.1 = bf16[4,48,768]{2,1,0:T(8,128)(2,1)} custom-call(bf16[4,16,128]{2,1,0:T(8,128)(2,1)} %copy-done.3, bf16[64,16,128]{2,1,0:T(8,128)(2,1)} %copy-done.6, bf16[41,48,128]{2,1,0:T(8,128)(2,1)} %get-tuple-element.12.spec_hbm, bf16[41,48,128]{2,1,0:T(8,128)(2,1)} %get-tuple-element.13.own_hbm, bf16[5120,128]{1,0:T(8,128)(2,1)} %constant.47.clone.table_hbm), custom_call_target="tpu_custom_call" | custom-call | flops 2000000000 | bytes 4000000 | tf_op jit(solution)/shard_map/gradient_parts/pallas_call | solution.py:542
  28.4 0.0 copy-start.4
  28.4 3.5 %all-to-all-start = ((bf16[4,48,768]{2,1,0:T(8,128)(2,1)}), bf16[4,48,768]{2,1,0:T(8,128)(2,1)S(1)}, u32[]{:S(2)}, u32[]{:S(2)}) async-start(bf16[4,48,768]{2,1,0:T(8,128)(2,1)} %gradient_parts.1), calls=%async_computation | async-start | bytes 589824 | tf_op jit(solution)/shard_map/all_to_all | solution.py:611
  31.9 0.0 copy-done.2
  31.9 0.8 bitcast_convert_fusion
  32.7 0.0 copy-done.1
  32.7 0.0 copy-done.4
  32.7 0.0 copy-start
  32.7 0.6 synthesized.1
  33.3 4.2 %all-to-all-done = bf16[4,48,768]{2,1,0:T(8,128)(2,1)S(1)} async-done(((bf16[4,48,768]{2,1,0:T(8,128)(2,1)}), bf16[4,48,768]{2,1,0:T(8,128)(2,1)S(1)}, u32[]{:S(2)}, u32[]{:S(2)}) %all-to-all-start) | async-done | bytes 294944 | tf_op jit(solution)/shard_map/all_to_all | solution.py:611
  37.6 0.0 copy-done
  37.6 0.1 subtract_select_fusion
  37.6 0.2 multiply_add_fusion.1
  37.8 0.0 copy-start.5
  37.8 3.5 %collective-permute-start.2 = (bf16[8,768]{1,0:T(8,128)(2,1)S(1)}, bf16[8,768]{1,0:T(8,128)(2,1)S(1)}, u32[]{:S(2)}, u32[]{:S(2)}) collective-permute-start(bf16[8,768]{1,0:T(8,128)(2,1)S(1)} %slice.484), channel_id=1, source_target_pairs={{0,4},{4,8},{8,12},{12,16},{16,20},{20,24},{24,28},{28,32},{32,36}... | collective-permute-start | bytes 36872 | tf_op jit(solution)/shard_map/ppermute | solution.py:607
  41.3 0.3 add_bitcast_fusion.3
  41.6 0.3 add_bitcast_fusion.1
  41.9 0.0 copy-done.5
  41.9 0.1 slice_add_fusion
  42.0 0.2 collective-permute-done.2
  42.2 0.1 multiply_add_fusion.3
  42.2 0.1 add_bitcast_fusion.7
  42.3 0.1 add_bitcast_fusion.5
  42.5 19.8 %all_gather.4 = bf16[4,4,48,640]{3,2,1,0:T(8,128)(2,1)S(1)} all-gather(bf16[1,4,48,640]{3,2,1,0:T(8,128)(2,1)S(1)} %fusion.1), channel_id=1, replica_groups=mesh['cube'=4,'facet'=32,'dp'=4] {'cube'}, dimensions={0}, use_global_device_ids=true | all-gather | bytes 1228800 | tf_op jit(solution)/shard_map/all_gather | solution.py:656
  62.4 0.1 convert_reduce_fusion
  62.5 0.2 fusion
  62.8 0.1 broadcast_in_dim.16
  62.9 19.7 %all_to_all.10.parts_ref = bf16[4,5,48,640]{3,2,1,0:T(8,128)(2,1)S(1)} all-to-all(bf16[4,5,48,640]{3,2,1,0:T(8,128)(2,1)S(1)} %broadcast_in_dim.16), channel_id=1, replica_groups=mesh['cube'=4,'facet'=32,'dp'=4] {'dp'}, dimensions={0} | all-to-all | bytes 2457600 | tf_op jit(solution)/shard_map/all_to_all | solution.py:660
  82.5 1.1 %finished.1 = (f32[48,2560]{1,0:T(8,128)}, bf16[4,48,2560]{2,1,0:T(8,128)(2,1)}) custom-call(bf16[4,5,48,640]{3,2,1,0:T(8,128)(2,1)S(1)} %all_to_all.10.parts_ref, f32[48,2560]{1,0:T(8,128)S(1)} %bitcast.38), custom_call_target="tpu_custom_call" | custom-call | tf_op jit(solution)/shard_map/finished/pallas_call | solution.py:590
  (10 shorter events, 0.2 us)
Async XLA Ops:
  0.6 23.1 %collective-permute-start.1 = (bf16[64,16,128]{2,1,0:T(8,128)(2,1)}, bf16[64,16,128]{2,1,0:T(8,128)(2,1)S(1)}, u32[]{:S(2)}, u32[]{:S(2)}) collective-permute-start(bf16[64,16,128]{2,1,0:T(8,128)(2,1)} %bitcast.45), channel_id=1, source_target_pairs={{4,0},{8,4},{12,8},{16,12},{20,16},{24,20},{28,24},{32,28},{36,32}... | collective-permute-start | bytes 786440 | tf_op jit(solution)/shard_map/ppermute | solution.py:607
  14.5 9.3 %collective-permute-start = (bf16[4,16,128]{2,1,0:T(8,128)(2,1)}, bf16[4,16,128]{2,1,0:T(8,128)(2,1)S(1)}, u32[]{:S(2)}, u32[]{:S(2)}) collective-permute-start(bf16[4,16,128]{2,1,0:T(8,128)(2,1)} %get-tuple-element.11), channel_id=1, source_target_pairs={{4,0},{8,4},{12,8},{16,12},{20,16},{24,20},{28,24},{32,28},{36,32}... | collective-permute-start | bytes 49160 | tf_op jit(solution)/shard_map/ppermute | solution.py:607
  23.8 0.6 copy-start.3
  23.8 0.7 copy-start.6
  24.5 7.4 %copy-start.2 = (bf16[4,1,48,2560]{3,2,1,0:T(8,128)(2,1)S(1)}, bf16[4,1,48,2560]{3,2,1,0:T(8,128)(2,1)}, u32[]{:S(2)}) copy-start(bf16[4,1,48,2560]{3,2,1,0:T(8,128)(2,1)} %param.10) | copy-start | bytes 2949124
  24.5 8.2 %copy-start.1 = (bf16[3072,256]{1,0:T(8,128)(2,1)S(1)}, bf16[3072,256]{1,0:T(8,128)(2,1)}, u32[]{:S(2)}) copy-start(bf16[3072,256]{1,0:T(8,128)(2,1)} %constant.46.clone.table_hbm.constants_ref) | copy-start | bytes 4718596
  28.4 4.3 %copy-start.4 = (bf16[4,16,128]{2,1,0:T(8,128)(2,1)S(1)}, bf16[4,16,128]{2,1,0:T(8,128)(2,1)}, u32[]{:S(2)}) copy-start(bf16[4,16,128]{2,1,0:T(8,128)(2,1)} %copy-done.3) | copy-start | bytes 49156
  28.4 9.1 %all-to-all-start = ((bf16[4,48,768]{2,1,0:T(8,128)(2,1)}), bf16[4,48,768]{2,1,0:T(8,128)(2,1)S(1)}, u32[]{:S(2)}, u32[]{:S(2)}) async-start(bf16[4,48,768]{2,1,0:T(8,128)(2,1)} %gradient_parts.1), calls=%async_computation | async-start | bytes 589824 | tf_op jit(solution)/shard_map/all_to_all | solution.py:611
  32.7 4.9 %copy-start = (f32[1,48,2560]{2,1,0:T(8,128)S(1)}, f32[1,48,2560]{2,1,0:T(8,128)}, u32[]{:S(2)}) copy-start(f32[1,48,2560]{2,1,0:T(8,128)} %param.9) | copy-start | bytes 1474564
  37.8 4.0 %copy-start.5 = (f32[4,48,640]{2,1,0:T(8,128)S(1)}, f32[4,48,640]{2,1,0:T(8,128)}, u32[]{:S(2)}) copy-start(f32[4,48,640]{2,1,0:T(8,128)} %bitcast_convert_fusion) | copy-start | bytes 1474564
  37.8 4.3 %collective-permute-start.2 = (bf16[8,768]{1,0:T(8,128)(2,1)S(1)}, bf16[8,768]{1,0:T(8,128)(2,1)S(1)}, u32[]{:S(2)}, u32[]{:S(2)}) collective-permute-start(bf16[8,768]{1,0:T(8,128)(2,1)S(1)} %slice.484), channel_id=1, source_target_pairs={{0,4},{4,8},{8,12},{12,16},{16,20},{20,24},{24,28},{28,32},{32,36}... | collective-permute-start | bytes 36872 | tf_op jit(solution)/shard_map/ppermute | solution.py:607

commit v13 on v10

--- a/solution.py
+++ b/solution.py
@@ -45,7 +45,7 @@
 HALO = 128
 SPAN = PART + HALO
 CHUNKS = W // 64
-UNROLL = 8
+UNROLL = 16
 VMEM_LIMIT = 60 * 1024 * 1024
 NORM = 1.0 / math.sqrt(W)
 C1, C2 = math.cos(2 * math.pi / 5), math.cos(4 * math.pi / 5)
@@ -635,10 +635,10 @@
     return jnp.sum(mixed.astype(jnp.float32), 0)
 
 
-def analyze(extra):
+def analyze(extra, first, count):
     subbands = []
     for row_taps in (LOWPASS, HIGHPASS):
-        filtered = sum(row_taps[k] * extra[8 - k : 8 - k + FR] for k in range(8))
+        filtered = sum(row_taps[k] * extra[first - k : first - k + count] for k in range(8))
         for col_taps in (LOWPASS, HIGHPASS):
             subbands.append(
                 sum(col_taps[k] * filtered[:, HALO - k : HALO - k + PART] for k in range(8))
@@ -674,9 +674,11 @@
     column = lax.broadcasted_iota(jnp.int32, old.shape, 1) + left
     extra = jnp.where(column >= HALO, 2.0 * new - old, 0.0)
     extra_above = hop(extra[FR - 8 :].astype(jnp.bfloat16), 1).astype(jnp.float32)
-    extra = jnp.concatenate([extra_above, extra], 0)
-
-    shifted = own_dual + SIGMA_STEP * analyze(extra)
+    lower = own_dual[:, 8:] + SIGMA_STEP * analyze(extra, 8, FR - 8)
+    lower, extra_above = lax.optimization_barrier((lower, extra_above))
+    top = jnp.concatenate([extra_above, extra[:8]], 0)
+    upper = own_dual[:, :8] + SIGMA_STEP * analyze(top, 8, 8)
+    shifted = jnp.concatenate([upper, lower], 1)
     squares = lax.all_gather((shifted * shifted).astype(jnp.bfloat16), "cube")
     norms = jnp.sqrt(jnp.sum(squares.astype(jnp.float32), 0))
     dual_part = (shifted * (RADIUS / jnp.maximum(norms, RADIUS))).astype(jnp.bfloat16)

time: 84.6 us -> 83.9 us (level)
  blocking collectives: 39.4 us -> 38.2 us
  other arithmetic: 1.43 us -> 2.4 us
  Pallas kernels: 12.2 us -> 13.1 us
    pallas_call x1, Pallas kernels: 4.13 us -> 5.13 us  [gradient_parts(): pl.pallas_call(below_pass, out_shape=jax.ShapeDtypeStruct((DP, FR, SPAN),...]
  transfers between devices with their start and end apart: 4 -> 4, of which waited for: 3 -> 3; matrix products, arithmetic and copies ran while one was open for 0% -> 2% of each run, Pallas kernels for 8% -> 8%
where the time goes in v13:
time: 83.9 us; the launch traced here: 82.8 us
  blocking collectives  38.2 us (46%)
  starting transfers between devices  19 us (23%)
  Pallas kernels  13.1 us (16%)
  waiting for transfers between devices  7.78 us (9%)
  other arithmetic  2.4 us (3%)
  between operations  1.51 us (2%)
  local copies, waits for them, and re-layouts  0.84 us (1%)
    all_to_all x1, blocking collectives, on_device(): lax.all_to_all(jnp.broadcast_to(own_part, (DP,) + own_part.shape), 'dp',...  19.2 us
    all_gather x1, blocking collectives, on_device(): squares = lax.all_gather((shifted * shifted).astype(jnp.bfloat16), 'cube')  19 us
    ppermute x3, starting transfers between devices, hop(): return lax.ppermute(block, 'facet', route)  15.5 us
    pallas_call x1, Pallas kernels, gradient_parts(): pl.pallas_call(below_pass, out_shape=jax.ShapeDtypeStruct((DP, FR, SPAN),...  5.13 us
    all_to_all x1, waiting for transfers between devices, gathered_sum(): mixed = lax.all_to_all(parts, 'dp', 0, 0)  4.23 us
    pallas_call x1, Pallas kernels, own_spectra(): pl.pallas_call(own_pass, out_shape=(SPECTRA, SPECTRA), in_specs=[HBM_SPEC...  4.18 us
    ppermute x3, waiting for transfers between devices, hop(): return lax.ppermute(block, 'facet', route)  3.55 us
    all_to_all x1, starting transfers between devices, gathered_sum(): mixed = lax.all_to_all(parts, 'dp', 0, 0)  3.46 us
  transfers between devices with their start and end apart: 4, of which 3 were waited for; matrix products, arithmetic and copies ran while one was open for 2% of the time, Pallas kernels for 8%

profile of v13, /device:TPU:1, one launch (start us, length us, event | category | flops | bytes accessed | tf_op | source)
XLA Modules:
  0.0 82.8 jit_solution(8127890613686051582)
XLA Ops:
  0.6 8.8 %collective-permute-start.1 = (bf16[64,16,128]{2,1,0:T(8,128)(2,1)}, bf16[64,16,128]{2,1,0:T(8,128)(2,1)S(1)}, u32[]{:S(2)}, u32[]{:S(2)}) collective-permute-start(bf16[64,16,128]{2,1,0:T(8,128)(2,1)} %bitcast.47), channel_id=1, source_target_pairs={{4,0},{8,4},{12,8},{16,12},{20,16},{24,20},{28,24},{32,28},{36,32}... | collective-permute-start | bytes 786440 | tf_op jit(solution)/shard_map/ppermute | solution.py:630
  10.1 2.1 %message.1 = bf16[4,16,128]{2,1,0:T(8,128)(2,1)} custom-call(s32[1]{0:T(128)} %bitcast.3.part_ref, s32[1,64]{1,0:T(1,128)} %starts_hbm.3, s32[1,64]{1,0:T(1,128)} %slots_hbm.3, s32[1,1]{1,0:T(1,128)S(6)} %copy.15.live_hbm, bf16[16,64]{1,0:T(8,128)(2,1)} %bitcast.43, bf16[4,48,2560]{2,1,0:T(8,128)(2,1)} %bitcast.36, ...), custom_call_target="tpu_custom_call" | custom-call | tf_op jit(solution)/shard_map/message/pallas_call | solution.py:505
  12.2 1.9 %collective-permute-start = (bf16[4,16,128]{2,1,0:T(8,128)(2,1)}, bf16[4,16,128]{2,1,0:T(8,128)(2,1)S(1)}, u32[]{:S(2)}, u32[]{:S(2)}) collective-permute-start(bf16[4,16,128]{2,1,0:T(8,128)(2,1)} %message.1), channel_id=1, source_target_pairs={{4,0},{8,4},{12,8},{16,12},{20,16},{24,20},{28,24},{32,28},{36,32}... | collective-permute-start | bytes 49160 | tf_op jit(solution)/shard_map/ppermute | solution.py:630
  14.1 4.2 %own_spectra.1 = (bf16[41,48,128]{2,1,0:T(8,128)(2,1)}, bf16[41,48,128]{2,1,0:T(8,128)(2,1)}) custom-call(s32[1,64]{1,0:T(1,128)} %starts_hbm.3, s32[1,64]{1,0:T(1,128)} %slots_hbm.3, s32[1,1]{1,0:T(1,128)S(6)} %copy.15.live_hbm, bf16[16,64]{1,0:T(8,128)(2,1)} %bitcast.44, bf16[64,16,128]{2,1,0:T(8,128)(2,1)} %bitcast.48, ...), custom_call_target="tpu_custom_call" | custom-call | flops 2000000000 | bytes 4000000 | tf_op jit(solution)/shard_map/own_spectra/pallas_call | solution.py:538
  18.3 3.4 %collective-permute-done.message_hbm.message_ref = bf16[4,16,128]{2,1,0:T(8,128)(2,1)S(1)} collective-permute-done((bf16[4,16,128]{2,1,0:T(8,128)(2,1)}, bf16[4,16,128]{2,1,0:T(8,128)(2,1)S(1)}, u32[]{:S(2)}, u32[]{:S(2)}) %collective-permute-start) | collective-permute-done | bytes 16416 | tf_op jit(solution)/shard_map/ppermute | solution.py:630
  21.7 0.0 copy-start.3
  21.7 0.0 collective-permute-done.1.payload_hbm
  21.7 0.0 copy-start.6
  21.7 0.6 copy-done.3
  22.3 0.1 copy-done.6
  22.4 0.0 copy-start.1
  22.4 0.0 copy-start
  22.4 5.1 %gradient_parts.1 = bf16[4,48,768]{2,1,0:T(8,128)(2,1)} custom-call(bf16[4,16,128]{2,1,0:T(8,128)(2,1)} %copy-done.3, bf16[64,16,128]{2,1,0:T(8,128)(2,1)} %copy-done.6, bf16[41,48,128]{2,1,0:T(8,128)(2,1)} %get-tuple-element.10.spec_hbm, bf16[41,48,128]{2,1,0:T(8,128)(2,1)} %get-tuple-element.11.own_hbm, bf16[5120,128]{1,0:T(8,128)(2,1)} %constant.47.clone.table_hbm), custom_call_target="tpu_custom_call" | custom-call | flops 2000000000 | bytes 4000000 | tf_op jit(solution)/shard_map/gradient_parts/pallas_call | solution.py:565
  27.5 0.0 copy-start.4
  27.5 3.5 %all-to-all-start = ((bf16[4,48,768]{2,1,0:T(8,128)(2,1)}), bf16[4,48,768]{2,1,0:T(8,128)(2,1)S(1)}, u32[]{:S(2)}, u32[]{:S(2)}) async-start(bf16[4,48,768]{2,1,0:T(8,128)(2,1)} %gradient_parts.1), calls=%async_computation | async-start | bytes 589824 | tf_op jit(solution)/shard_map/all_to_all | solution.py:634
  31.0 0.0 copy-done.1
  31.0 0.8 bitcast_convert_fusion
  31.8 0.0 copy-done
  31.8 0.0 copy-done.4
  31.8 0.0 copy-start.2
  31.8 0.6 synthesized.1
  32.4 4.2 %all-to-all-done = bf16[4,48,768]{2,1,0:T(8,128)(2,1)S(1)} async-done(((bf16[4,48,768]{2,1,0:T(8,128)(2,1)}), bf16[4,48,768]{2,1,0:T(8,128)(2,1)S(1)}, u32[]{:S(2)}, u32[]{:S(2)}) %all-to-all-start) | async-done | bytes 294944 | tf_op jit(solution)/shard_map/all_to_all | solution.py:634
  36.7 0.0 copy-done.2
  36.7 0.1 subtract_select_fusion
  36.8 0.2 multiply_add_fusion.1
  37.0 0.0 copy-start.5
  37.0 4.8 %collective-permute-start.2 = (bf16[8,768]{1,0:T(8,128)(2,1)S(1)}, bf16[8,768]{1,0:T(8,128)(2,1)S(1)}, u32[]{:S(2)}, u32[]{:S(2)}) collective-permute-start(bf16[8,768]{1,0:T(8,128)(2,1)S(1)} %slice.484), channel_id=1, source_target_pairs={{0,4},{4,8},{8,12},{12,16},{16,20},{20,24},{24,28},{28,32},{32,36}... | collective-permute-start | bytes 36872 | tf_op jit(solution)/shard_map/ppermute | solution.py:630
  41.8 0.3 add_bitcast_fusion.3
  42.0 0.3 add_bitcast_fusion.1
  42.3 0.0 copy-done.5
  42.3 0.1 slice_add_fusion
  42.4 0.2 collective-permute-done.2
  42.6 0.1 multiply_add_fusion.3
  42.7 0.1 add_bitcast_fusion.7
  42.8 0.1 add_bitcast_fusion.5
  43.0 19.0 %all_gather.4 = bf16[4,4,48,640]{3,2,1,0:T(8,128)(2,1)S(1)} all-gather(bf16[1,4,48,640]{3,2,1,0:T(8,128)(2,1)S(1)} %fusion.1), channel_id=1, replica_groups=mesh['cube'=4,'facet'=32,'dp'=4] {'cube'}, dimensions={0}, use_global_device_ids=true | all-gather | bytes 1228800 | tf_op jit(solution)/shard_map/all_gather | solution.py:682
  62.0 0.1 convert_reduce_fusion
  62.1 0.2 fusion
  62.4 0.1 broadcast_in_dim.16
  62.5 19.2 %all_to_all.10.parts_ref = bf16[4,5,48,640]{3,2,1,0:T(8,128)(2,1)S(1)} all-to-all(bf16[4,5,48,640]{3,2,1,0:T(8,128)(2,1)S(1)} %broadcast_in_dim.16), channel_id=1, replica_groups=mesh['cube'=4,'facet'=32,'dp'=4] {'dp'}, dimensions={0} | all-to-all | bytes 2457600 | tf_op jit(solution)/shard_map/all_to_all | solution.py:686
  81.7 1.1 %finished.1 = (f32[48,2560]{1,0:T(8,128)}, bf16[4,48,2560]{2,1,0:T(8,128)(2,1)}) custom-call(bf16[4,5,48,640]{3,2,1,0:T(8,128)(2,1)S(1)} %all_to_all.10.parts_ref, f32[48,2560]{1,0:T(8,128)S(1)} %bitcast.41), custom_call_target="tpu_custom_call" | custom-call | tf_op jit(solution)/shard_map/finished/pallas_call | solution.py:613
  (10 shorter events, 0.2 us)
Async XLA Ops:
  0.6 21.0 %collective-permute-start.1 = (bf16[64,16,128]{2,1,0:T(8,128)(2,1)}, bf16[64,16,128]{2,1,0:T(8,128)(2,1)S(1)}, u32[]{:S(2)}, u32[]{:S(2)}) collective-permute-start(bf16[64,16,128]{2,1,0:T(8,128)(2,1)} %bitcast.47), channel_id=1, source_target_pairs={{4,0},{8,4},{12,8},{16,12},{20,16},{24,20},{28,24},{32,28},{36,32}... | collective-permute-start | bytes 786440 | tf_op jit(solution)/shard_map/ppermute | solution.py:630
  12.2 9.5 %collective-permute-start = (bf16[4,16,128]{2,1,0:T(8,128)(2,1)}, bf16[4,16,128]{2,1,0:T(8,128)(2,1)S(1)}, u32[]{:S(2)}, u32[]{:S(2)}) collective-permute-start(bf16[4,16,128]{2,1,0:T(8,128)(2,1)} %message.1), channel_id=1, source_target_pairs={{4,0},{8,4},{12,8},{16,12},{20,16},{24,20},{28,24},{32,28},{36,32}... | collective-permute-start | bytes 49160 | tf_op jit(solution)/shard_map/ppermute | solution.py:630
  21.7 0.6 copy-start.3
  21.7 0.7 copy-start.6
  22.4 8.6 %copy-start.1 = (bf16[4,1,48,2560]{3,2,1,0:T(8,128)(2,1)S(1)}, bf16[4,1,48,2560]{3,2,1,0:T(8,128)(2,1)}, u32[]{:S(2)}) copy-start(bf16[4,1,48,2560]{3,2,1,0:T(8,128)(2,1)} %param.10) | copy-start | bytes 2949124
  22.4 9.5 %copy-start = (bf16[3072,256]{1,0:T(8,128)(2,1)S(1)}, bf16[3072,256]{1,0:T(8,128)(2,1)}, u32[]{:S(2)}) copy-start(bf16[3072,256]{1,0:T(8,128)(2,1)} %constant.46.clone.filters_hbm.table_hbm.constants_ref) | copy-start | bytes 4718596
  27.5 4.3 %copy-start.4 = (bf16[4,16,128]{2,1,0:T(8,128)(2,1)S(1)}, bf16[4,16,128]{2,1,0:T(8,128)(2,1)}, u32[]{:S(2)}) copy-start(bf16[4,16,128]{2,1,0:T(8,128)(2,1)} %copy-done.3) | copy-start | bytes 49156
  27.5 9.1 %all-to-all-start = ((bf16[4,48,768]{2,1,0:T(8,128)(2,1)}), bf16[4,48,768]{2,1,0:T(8,128)(2,1)S(1)}, u32[]{:S(2)}, u32[]{:S(2)}) async-start(bf16[4,48,768]{2,1,0:T(8,128)(2,1)} %gradient_parts.1), calls=%async_computation | async-start | bytes 589824 | tf_op jit(solution)/shard_map/all_to_all | solution.py:634
  31.8 4.9 %copy-start.2 = (f32[1,48,2560]{2,1,0:T(8,128)S(1)}, f32[1,48,2560]{2,1,0:T(8,128)}, u32[]{:S(2)}) copy-start(f32[1,48,2560]{2,1,0:T(8,128)} %param.9) | copy-start | bytes 1474564
  37.0 5.3 %copy-start.5 = (f32[4,48,640]{2,1,0:T(8,128)S(1)}, f32[4,48,640]{2,1,0:T(8,128)}, u32[]{:S(2)}) copy-start(f32[4,48,640]{2,1,0:T(8,128)} %bitcast_convert_fusion) | copy-start | bytes 1474564
  37.0 5.6 %collective-permute-start.2 = (bf16[8,768]{1,0:T(8,128)(2,1)S(1)}, bf16[8,768]{1,0:T(8,128)(2,1)S(1)}, u32[]{:S(2)}, u32[]{:S(2)}) collective-permute-start(bf16[8,768]{1,0:T(8,128)(2,1)S(1)} %slice.484), channel_id=1, source_target_pairs={{0,4},{4,8},{8,12},{12,16},{16,20},{20,24},{24,28},{28,32},{32,36}... | collective-permute-start | bytes 36872 | tf_op jit(solution)/shard_map/ppermute | solution.py:630

commit v14 on v12

--- a/solution.py
+++ b/solution.py
@@ -580,8 +580,10 @@
         tile = pl.ds(PART * d, PART)
         descent = parts_ref[d, 4].astype(jnp.float32)
         image_ref[:, tile] = jnp.maximum(pixels_ref[:, tile] - TAU_STEP * descent, 0.0)
-    copies.append(pltpu.make_async_copy(image_ref, image_hbm, sems.at[DP]))
-    copies[-1].start()
+        copies.append(
+            pltpu.make_async_copy(image_ref.at[:, tile], image_hbm.at[:, tile], sems.at[DP + d])
+        )
+        copies[-1].start()
     for copy in copies:
         copy.wait()
 
@@ -595,7 +597,7 @@
         ),
         in_specs=[VMEM_SPEC] * 2,
         out_specs=(HBM_SPEC,) * 2,
-        scratch_shapes=[pltpu.VMEM((FR, W), jnp.float32), pltpu.SemaphoreType.DMA((DP + 1,))],
+        scratch_shapes=[pltpu.VMEM((FR, W), jnp.float32), pltpu.SemaphoreType.DMA((2 * DP,))],
         compiler_params=pltpu.CompilerParams(vmem_limit_bytes=16 * 1024 * 1024),
         name="finished",
     )(parts, pixels)

time: 84.1 us -> 84 us (level)
  no operation moved by 1% of the time
where the time goes in v14:
time: 84 us
  blocking collectives  39.5 us (47%)
  starting transfers between devices  17.5 us (21%)
  waiting for transfers between devices  11.8 us (14%)
  Pallas kernels  10.4 us (12%)
  other arithmetic  2.38 us (3%)
  between operations  1.51 us (2%)
  local copies, waits for them, and re-layouts  0.84 us (1%)
    all_gather x1, blocking collectives, on_device(): squares = lax.all_gather((shifted * shifted).astype(jnp.bfloat16), 'cube')  20 us
    all_to_all x1, blocking collectives, on_device(): lax.all_to_all(jnp.broadcast_to(own_part, (DP,) + own_part.shape), 'dp',...  19.5 us
    ppermute x3, starting transfers between devices, hop(): return lax.ppermute(block, 'facet', route)  14 us
    ppermute x3, waiting for transfers between devices, hop(): return lax.ppermute(block, 'facet', route)  7.56 us
    pallas_call x1, Pallas kernels, own_spectra(): pl.pallas_call(own_pass, out_shape=(SPECTRA, SPECTRA, jax.ShapeDtypeStruc...  4.41 us
    pallas_call x1, Pallas kernels, gradient_parts(): pl.pallas_call(below_pass, out_shape=jax.ShapeDtypeStruct((DP, FR, SPAN),...  4.27 us
    all_to_all x1, waiting for transfers between devices, gathered_sum(): mixed = lax.all_to_all(parts, 'dp', 0, 0)  4.23 us
    all_to_all x1, starting transfers between devices, gathered_sum(): mixed = lax.all_to_all(parts, 'dp', 0, 0)  3.46 us
  transfers between devices with their start and end apart: 4, of which 3 were waited for; matrix products, arithmetic and copies ran while one was open for 2% of the time, Pallas kernels for 6%

profile of v14, /device:TPU:1, one launch (start us, length us, event | category | flops | bytes accessed | tf_op | source)
XLA Modules:
  0.0 84.0 jit_solution(1780149840173897652)
XLA Ops:
  0.6 8.8 %collective-permute-start.1 = (bf16[64,16,128]{2,1,0:T(8,128)(2,1)}, bf16[64,16,128]{2,1,0:T(8,128)(2,1)S(1)}, u32[]{:S(2)}, u32[]{:S(2)}) collective-permute-start(bf16[64,16,128]{2,1,0:T(8,128)(2,1)} %bitcast.45), channel_id=1, source_target_pairs={{4,0},{8,4},{12,8},{16,12},{20,16},{24,20},{28,24},{32,28},{36,32}... | collective-permute-start | bytes 786440 | tf_op jit(solution)/shard_map/ppermute | solution.py:609
  10.1 4.4 %own_spectra.1 = (bf16[41,48,128]{2,1,0:T(8,128)(2,1)}, bf16[41,48,128]{2,1,0:T(8,128)(2,1)}, bf16[4,16,128]{2,1,0:T(8,128)(2,1)}) custom-call(s32[1]{0:T(128)} %bitcast.3.part_ref, s32[1,64]{1,0:T(1,128)} %starts_hbm.1, s32[1,64]{1,0:T(1,128)} %slots_hbm.1, s32[1,1]{1,0:T(1,128)S(6)} %copy.15.live_hbm, bf16[16,64]{1,0:T(8,128)(2,1)} %bitcast.47, ...), custom_call_target="tpu_custom_call" | custom-call | flops 2000000000 | bytes 4000000 | tf_op jit(solution)/shard_map/own_spectra/pallas_call | solution.py:506
  14.5 1.9 %collective-permute-start = (bf16[4,16,128]{2,1,0:T(8,128)(2,1)}, bf16[4,16,128]{2,1,0:T(8,128)(2,1)S(1)}, u32[]{:S(2)}, u32[]{:S(2)}) collective-permute-start(bf16[4,16,128]{2,1,0:T(8,128)(2,1)} %get-tuple-element.11), channel_id=1, source_target_pairs={{4,0},{8,4},{12,8},{16,12},{20,16},{24,20},{28,24},{32,28},{36,32}... | collective-permute-start | bytes 49160 | tf_op jit(solution)/shard_map/ppermute | solution.py:609
  16.4 7.4 %collective-permute-done.message_hbm.message_ref = bf16[4,16,128]{2,1,0:T(8,128)(2,1)S(1)} collective-permute-done((bf16[4,16,128]{2,1,0:T(8,128)(2,1)}, bf16[4,16,128]{2,1,0:T(8,128)(2,1)S(1)}, u32[]{:S(2)}, u32[]{:S(2)}) %collective-permute-start) | collective-permute-done | bytes 16416 | tf_op jit(solution)/shard_map/ppermute | solution.py:609
  23.8 0.0 copy-start.3
  23.8 0.0 collective-permute-done.1.payload_hbm
  23.8 0.0 copy-start.6
  23.8 0.6 copy-done.3
  24.4 0.1 copy-done.6
  24.5 0.0 copy-start.2
  24.5 0.0 copy-start.1
  24.5 4.3 %gradient_parts.1 = bf16[4,48,768]{2,1,0:T(8,128)(2,1)} custom-call(bf16[4,16,128]{2,1,0:T(8,128)(2,1)} %copy-done.3, bf16[64,16,128]{2,1,0:T(8,128)(2,1)} %copy-done.6, bf16[41,48,128]{2,1,0:T(8,128)(2,1)} %get-tuple-element.12.spec_hbm, bf16[41,48,128]{2,1,0:T(8,128)(2,1)} %get-tuple-element.13.own_hbm, bf16[5120,128]{1,0:T(8,128)(2,1)} %constant.47.clone.table_hbm), custom_call_target="tpu_custom_call" | custom-call | flops 2000000000 | bytes 4000000 | tf_op jit(solution)/shard_map/gradient_parts/pallas_call | solution.py:542
  28.8 0.0 copy-start.4
  28.8 3.5 %all-to-all-start = ((bf16[4,48,768]{2,1,0:T(8,128)(2,1)}), bf16[4,48,768]{2,1,0:T(8,128)(2,1)S(1)}, u32[]{:S(2)}, u32[]{:S(2)}) async-start(bf16[4,48,768]{2,1,0:T(8,128)(2,1)} %gradient_parts.1), calls=%async_computation | async-start | bytes 589824 | tf_op jit(solution)/shard_map/all_to_all | solution.py:613
  32.3 0.0 copy-done.2
  32.3 0.8 bitcast_convert_fusion
  33.1 0.0 copy-done.1
  33.1 0.0 copy-done.4
  33.1 0.0 copy-start
  33.1 0.6 synthesized.1
  33.7 4.2 %all-to-all-done = bf16[4,48,768]{2,1,0:T(8,128)(2,1)S(1)} async-done(((bf16[4,48,768]{2,1,0:T(8,128)(2,1)}), bf16[4,48,768]{2,1,0:T(8,128)(2,1)S(1)}, u32[]{:S(2)}, u32[]{:S(2)}) %all-to-all-start) | async-done | bytes 294944 | tf_op jit(solution)/shard_map/all_to_all | solution.py:613
  38.0 0.0 copy-done
  38.0 0.1 subtract_select_fusion
  38.1 0.2 multiply_add_fusion.1
  38.2 0.0 copy-start.5
  38.3 3.3 %collective-permute-start.2 = (bf16[8,768]{1,0:T(8,128)(2,1)S(1)}, bf16[8,768]{1,0:T(8,128)(2,1)S(1)}, u32[]{:S(2)}, u32[]{:S(2)}) collective-permute-start(bf16[8,768]{1,0:T(8,128)(2,1)S(1)} %slice.484), channel_id=1, source_target_pairs={{0,4},{4,8},{8,12},{12,16},{16,20},{20,24},{24,28},{28,32},{32,36}... | collective-permute-start | bytes 36872 | tf_op jit(solution)/shard_map/ppermute | solution.py:609
  41.6 0.3 add_bitcast_fusion.3
  41.8 0.3 add_bitcast_fusion.1
  42.1 0.0 copy-done.5
  42.1 0.1 slice_add_fusion
  42.2 0.2 collective-permute-done.2
  42.4 0.1 multiply_add_fusion.3
  42.5 0.1 add_bitcast_fusion.7
  42.6 0.1 add_bitcast_fusion.5
  42.8 20.0 %all_gather.4 = bf16[4,4,48,640]{3,2,1,0:T(8,128)(2,1)S(1)} all-gather(bf16[1,4,48,640]{3,2,1,0:T(8,128)(2,1)S(1)} %fusion.1), channel_id=1, replica_groups=mesh['cube'=4,'facet'=32,'dp'=4] {'cube'}, dimensions={0}, use_global_device_ids=true | all-gather | bytes 1228800 | tf_op jit(solution)/shard_map/all_gather | solution.py:658
  62.8 0.1 convert_reduce_fusion
  62.9 0.2 fusion
  63.2 0.1 broadcast_in_dim.16
  63.3 19.5 %all_to_all.10.parts_ref = bf16[4,5,48,640]{3,2,1,0:T(8,128)(2,1)S(1)} all-to-all(bf16[4,5,48,640]{3,2,1,0:T(8,128)(2,1)S(1)} %broadcast_in_dim.16), channel_id=1, replica_groups=mesh['cube'=4,'facet'=32,'dp'=4] {'dp'}, dimensions={0} | all-to-all | bytes 2457600 | tf_op jit(solution)/shard_map/all_to_all | solution.py:662
  82.8 1.2 %finished.1 = (f32[48,2560]{1,0:T(8,128)}, bf16[4,48,2560]{2,1,0:T(8,128)(2,1)}) custom-call(bf16[4,5,48,640]{3,2,1,0:T(8,128)(2,1)S(1)} %all_to_all.10.parts_ref, f32[48,2560]{1,0:T(8,128)S(1)} %bitcast.38), custom_call_target="tpu_custom_call" | custom-call | tf_op jit(solution)/shard_map/finished/pallas_call | solution.py:592
  (10 shorter events, 0.2 us)
Async XLA Ops:
  0.6 23.2 %collective-permute-start.1 = (bf16[64,16,128]{2,1,0:T(8,128)(2,1)}, bf16[64,16,128]{2,1,0:T(8,128)(2,1)S(1)}, u32[]{:S(2)}, u32[]{:S(2)}) collective-permute-start(bf16[64,16,128]{2,1,0:T(8,128)(2,1)} %bitcast.45), channel_id=1, source_target_pairs={{4,0},{8,4},{12,8},{16,12},{20,16},{24,20},{28,24},{32,28},{36,32}... | collective-permute-start | bytes 786440 | tf_op jit(solution)/shard_map/ppermute | solution.py:609
  14.5 9.3 %collective-permute-start = (bf16[4,16,128]{2,1,0:T(8,128)(2,1)}, bf16[4,16,128]{2,1,0:T(8,128)(2,1)S(1)}, u32[]{:S(2)}, u32[]{:S(2)}) collective-permute-start(bf16[4,16,128]{2,1,0:T(8,128)(2,1)} %get-tuple-element.11), channel_id=1, source_target_pairs={{4,0},{8,4},{12,8},{16,12},{20,16},{24,20},{28,24},{32,28},{36,32}... | collective-permute-start | bytes 49160 | tf_op jit(solution)/shard_map/ppermute | solution.py:609
  23.8 0.6 copy-start.3
  23.8 0.7 copy-start.6
  24.5 7.8 %copy-start.2 = (bf16[4,1,48,2560]{3,2,1,0:T(8,128)(2,1)S(1)}, bf16[4,1,48,2560]{3,2,1,0:T(8,128)(2,1)}, u32[]{:S(2)}) copy-start(bf16[4,1,48,2560]{3,2,1,0:T(8,128)(2,1)} %param.10) | copy-start | bytes 2949124
  24.5 8.6 %copy-start.1 = (bf16[3072,256]{1,0:T(8,128)(2,1)S(1)}, bf16[3072,256]{1,0:T(8,128)(2,1)}, u32[]{:S(2)}) copy-start(bf16[3072,256]{1,0:T(8,128)(2,1)} %constant.46.clone.table_hbm.constants_ref) | copy-start | bytes 4718596
  28.8 4.3 %copy-start.4 = (bf16[4,16,128]{2,1,0:T(8,128)(2,1)S(1)}, bf16[4,16,128]{2,1,0:T(8,128)(2,1)}, u32[]{:S(2)}) copy-start(bf16[4,16,128]{2,1,0:T(8,128)(2,1)} %copy-done.3) | copy-start | bytes 49156
  28.8 9.1 %all-to-all-start = ((bf16[4,48,768]{2,1,0:T(8,128)(2,1)}), bf16[4,48,768]{2,1,0:T(8,128)(2,1)S(1)}, u32[]{:S(2)}, u32[]{:S(2)}) async-start(bf16[4,48,768]{2,1,0:T(8,128)(2,1)} %gradient_parts.1), calls=%async_computation | async-start | bytes 589824 | tf_op jit(solution)/shard_map/all_to_all | solution.py:613
  33.1 4.9 %copy-start = (f32[1,48,2560]{2,1,0:T(8,128)S(1)}, f32[1,48,2560]{2,1,0:T(8,128)}, u32[]{:S(2)}) copy-start(f32[1,48,2560]{2,1,0:T(8,128)} %param.9) | copy-start | bytes 1474564
  38.2 3.9 %copy-start.5 = (f32[4,48,640]{2,1,0:T(8,128)S(1)}, f32[4,48,640]{2,1,0:T(8,128)}, u32[]{:S(2)}) copy-start(f32[4,48,640]{2,1,0:T(8,128)} %bitcast_convert_fusion) | copy-start | bytes 1474564
  38.3 4.1 %collective-permute-start.2 = (bf16[8,768]{1,0:T(8,128)(2,1)S(1)}, bf16[8,768]{1,0:T(8,128)(2,1)S(1)}, u32[]{:S(2)}, u32[]{:S(2)}) collective-permute-start(bf16[8,768]{1,0:T(8,128)(2,1)S(1)} %slice.484), channel_id=1, source_target_pairs={{0,4},{4,8},{8,12},{12,16},{16,20},{20,24},{24,28},{28,32},{32,36}... | collective-permute-start | bytes 36872 | tf_op jit(solution)/shard_map/ppermute | solution.py:609

commit v15 on v14

--- a/solution.py
+++ b/solution.py
@@ -45,7 +45,7 @@
 HALO = 128
 SPAN = PART + HALO
 CHUNKS = W // 64
-UNROLL = 16
+UNROLL = 20
 VMEM_LIMIT = 60 * 1024 * 1024
 NORM = 1.0 / math.sqrt(W)
 C1, C2 = math.cos(2 * math.pi / 5), math.cos(4 * math.pi / 5)

time: 84 us -> 84.1 us (level)
  no operation moved by 1% of the time
where the time goes in v15:
time: 84.1 us; the launch traced here: 83.4 us
  blocking collectives  39 us (46%)
  starting transfers between devices  17.3 us (21%)
  waiting for transfers between devices  11.8 us (14%)
  Pallas kernels  10.6 us (13%)
  other arithmetic  2.38 us (3%)
  between operations  1.51 us (2%)
    all_gather x1, blocking collectives, on_device(): squares = lax.all_gather((shifted * shifted).astype(jnp.bfloat16), 'cube')  20.1 us
    all_to_all x1, blocking collectives, on_device(): lax.all_to_all(jnp.broadcast_to(own_part, (DP,) + own_part.shape), 'dp',...  18.9 us
    ppermute x3, starting transfers between devices, hop(): return lax.ppermute(block, 'facet', route)  13.8 us
    ppermute x3, waiting for transfers between devices, hop(): return lax.ppermute(block, 'facet', route)  7.56 us
    pallas_call x1, Pallas kernels, gradient_parts(): pl.pallas_call(below_pass, out_shape=jax.ShapeDtypeStruct((DP, FR, SPAN),...  4.48 us
    pallas_call x1, Pallas kernels, own_spectra(): pl.pallas_call(own_pass, out_shape=(SPECTRA, SPECTRA, jax.ShapeDtypeStruc...  4.41 us
    all_to_all x1, waiting for transfers between devices, gathered_sum(): mixed = lax.all_to_all(parts, 'dp', 0, 0)  4.23 us
    all_to_all x1, starting transfers between devices, gathered_sum(): mixed = lax.all_to_all(parts, 'dp', 0, 0)  3.46 us
  transfers between devices with their start and end apart: 4, of which 3 were waited for; matrix products, arithmetic and copies ran while one was open for 2% of the time, Pallas kernels for 6%

profile of v15, /device:TPU:1, one launch (start us, length us, event | category | flops | bytes accessed | tf_op | source)
XLA Modules:
  0.0 83.4 jit_solution(5504448633136013307)
XLA Ops:
  0.6 8.8 %collective-permute-start.1 = (bf16[64,16,128]{2,1,0:T(8,128)(2,1)}, bf16[64,16,128]{2,1,0:T(8,128)(2,1)S(1)}, u32[]{:S(2)}, u32[]{:S(2)}) collective-permute-start(bf16[64,16,128]{2,1,0:T(8,128)(2,1)} %bitcast.45), channel_id=1, source_target_pairs={{4,0},{8,4},{12,8},{16,12},{20,16},{24,20},{28,24},{32,28},{36,32}... | collective-permute-start | bytes 786440 | tf_op jit(solution)/shard_map/ppermute | solution.py:609
  10.1 4.4 %own_spectra.1 = (bf16[41,48,128]{2,1,0:T(8,128)(2,1)}, bf16[41,48,128]{2,1,0:T(8,128)(2,1)}, bf16[4,16,128]{2,1,0:T(8,128)(2,1)}) custom-call(s32[1]{0:T(128)} %bitcast.3.part_ref, s32[1,64]{1,0:T(1,128)} %starts_hbm.1, s32[1,64]{1,0:T(1,128)} %slots_hbm.1, s32[1,1]{1,0:T(1,128)S(6)} %copy.15.live_hbm, bf16[16,64]{1,0:T(8,128)(2,1)} %bitcast.47, ...), custom_call_target="tpu_custom_call" | custom-call | flops 2000000000 | bytes 4000000 | tf_op jit(solution)/shard_map/own_spectra/pallas_call | solution.py:506
  14.5 1.9 %collective-permute-start = (bf16[4,16,128]{2,1,0:T(8,128)(2,1)}, bf16[4,16,128]{2,1,0:T(8,128)(2,1)S(1)}, u32[]{:S(2)}, u32[]{:S(2)}) collective-permute-start(bf16[4,16,128]{2,1,0:T(8,128)(2,1)} %get-tuple-element.11), channel_id=1, source_target_pairs={{4,0},{8,4},{12,8},{16,12},{20,16},{24,20},{28,24},{32,28},{36,32}... | collective-permute-start | bytes 49160 | tf_op jit(solution)/shard_map/ppermute | solution.py:609
  16.4 7.4 %collective-permute-done.message_hbm.message_ref = bf16[4,16,128]{2,1,0:T(8,128)(2,1)S(1)} collective-permute-done((bf16[4,16,128]{2,1,0:T(8,128)(2,1)}, bf16[4,16,128]{2,1,0:T(8,128)(2,1)S(1)}, u32[]{:S(2)}, u32[]{:S(2)}) %collective-permute-start) | collective-permute-done | bytes 16416 | tf_op jit(solution)/shard_map/ppermute | solution.py:609
  23.8 0.0 copy-start.3
  23.8 0.0 collective-permute-done.1.payload_hbm
  23.8 0.0 copy-start.6
  23.8 0.6 copy-done.3
  24.4 0.1 copy-done.6
  24.5 0.0 copy-start.2
  24.5 0.0 copy-start.1
  24.5 4.5 %gradient_parts.1 = bf16[4,48,768]{2,1,0:T(8,128)(2,1)} custom-call(bf16[4,16,128]{2,1,0:T(8,128)(2,1)} %copy-done.3, bf16[64,16,128]{2,1,0:T(8,128)(2,1)} %copy-done.6, bf16[41,48,128]{2,1,0:T(8,128)(2,1)} %get-tuple-element.12.spec_hbm, bf16[41,48,128]{2,1,0:T(8,128)(2,1)} %get-tuple-element.13.own_hbm, bf16[5120,128]{1,0:T(8,128)(2,1)} %constant.47.clone.table_hbm), custom_call_target="tpu_custom_call" | custom-call | flops 2000000000 | bytes 4000000 | tf_op jit(solution)/shard_map/gradient_parts/pallas_call | solution.py:542
  29.0 0.0 copy-start.4
  29.0 3.5 %all-to-all-start = ((bf16[4,48,768]{2,1,0:T(8,128)(2,1)}), bf16[4,48,768]{2,1,0:T(8,128)(2,1)S(1)}, u32[]{:S(2)}, u32[]{:S(2)}) async-start(bf16[4,48,768]{2,1,0:T(8,128)(2,1)} %gradient_parts.1), calls=%async_computation | async-start | bytes 589824 | tf_op jit(solution)/shard_map/all_to_all | solution.py:613
  32.5 0.0 copy-done.2
  32.5 0.8 bitcast_convert_fusion
  33.3 0.0 copy-done.1
  33.3 0.0 copy-done.4
  33.3 0.0 copy-start
  33.3 0.6 synthesized.1
  33.9 4.2 %all-to-all-done = bf16[4,48,768]{2,1,0:T(8,128)(2,1)S(1)} async-done(((bf16[4,48,768]{2,1,0:T(8,128)(2,1)}), bf16[4,48,768]{2,1,0:T(8,128)(2,1)S(1)}, u32[]{:S(2)}, u32[]{:S(2)}) %all-to-all-start) | async-done | bytes 294944 | tf_op jit(solution)/shard_map/all_to_all | solution.py:613
  38.2 0.0 copy-done
  38.2 0.1 subtract_select_fusion
  38.3 0.2 multiply_add_fusion.1
  38.4 0.0 copy-start.5
  38.5 3.1 %collective-permute-start.2 = (bf16[8,768]{1,0:T(8,128)(2,1)S(1)}, bf16[8,768]{1,0:T(8,128)(2,1)S(1)}, u32[]{:S(2)}, u32[]{:S(2)}) collective-permute-start(bf16[8,768]{1,0:T(8,128)(2,1)S(1)} %slice.484), channel_id=1, source_target_pairs={{0,4},{4,8},{8,12},{12,16},{16,20},{20,24},{24,28},{28,32},{32,36}... | collective-permute-start | bytes 36872 | tf_op jit(solution)/shard_map/ppermute | solution.py:609
  41.6 0.3 add_bitcast_fusion.3
  41.8 0.3 add_bitcast_fusion.1
  42.1 0.0 copy-done.5
  42.1 0.1 slice_add_fusion
  42.2 0.2 collective-permute-done.2
  42.4 0.1 multiply_add_fusion.3
  42.5 0.1 add_bitcast_fusion.7
  42.6 0.1 add_bitcast_fusion.5
  42.8 20.1 %all_gather.4 = bf16[4,4,48,640]{3,2,1,0:T(8,128)(2,1)S(1)} all-gather(bf16[1,4,48,640]{3,2,1,0:T(8,128)(2,1)S(1)} %fusion.1), channel_id=1, replica_groups=mesh['cube'=4,'facet'=32,'dp'=4] {'cube'}, dimensions={0}, use_global_device_ids=true | all-gather | bytes 1228800 | tf_op jit(solution)/shard_map/all_gather | solution.py:658
  62.9 0.1 convert_reduce_fusion
  63.0 0.2 fusion
  63.2 0.1 broadcast_in_dim.16
  63.3 18.9 %all_to_all.10.parts_ref = bf16[4,5,48,640]{3,2,1,0:T(8,128)(2,1)S(1)} all-to-all(bf16[4,5,48,640]{3,2,1,0:T(8,128)(2,1)S(1)} %broadcast_in_dim.16), channel_id=1, replica_groups=mesh['cube'=4,'facet'=32,'dp'=4] {'dp'}, dimensions={0} | all-to-all | bytes 2457600 | tf_op jit(solution)/shard_map/all_to_all | solution.py:662
  82.2 1.2 %finished.1 = (f32[48,2560]{1,0:T(8,128)}, bf16[4,48,2560]{2,1,0:T(8,128)(2,1)}) custom-call(bf16[4,5,48,640]{3,2,1,0:T(8,128)(2,1)S(1)} %all_to_all.10.parts_ref, f32[48,2560]{1,0:T(8,128)S(1)} %bitcast.38), custom_call_target="tpu_custom_call" | custom-call | tf_op jit(solution)/shard_map/finished/pallas_call | solution.py:592
  (10 shorter events, 0.2 us)
Async XLA Ops:
  0.6 23.2 %collective-permute-start.1 = (bf16[64,16,128]{2,1,0:T(8,128)(2,1)}, bf16[64,16,128]{2,1,0:T(8,128)(2,1)S(1)}, u32[]{:S(2)}, u32[]{:S(2)}) collective-permute-start(bf16[64,16,128]{2,1,0:T(8,128)(2,1)} %bitcast.45), channel_id=1, source_target_pairs={{4,0},{8,4},{12,8},{16,12},{20,16},{24,20},{28,24},{32,28},{36,32}... | collective-permute-start | bytes 786440 | tf_op jit(solution)/shard_map/ppermute | solution.py:609
  14.5 9.3 %collective-permute-start = (bf16[4,16,128]{2,1,0:T(8,128)(2,1)}, bf16[4,16,128]{2,1,0:T(8,128)(2,1)S(1)}, u32[]{:S(2)}, u32[]{:S(2)}) collective-permute-start(bf16[4,16,128]{2,1,0:T(8,128)(2,1)} %get-tuple-element.11), channel_id=1, source_target_pairs={{4,0},{8,4},{12,8},{16,12},{20,16},{24,20},{28,24},{32,28},{36,32}... | collective-permute-start | bytes 49160 | tf_op jit(solution)/shard_map/ppermute | solution.py:609
  23.8 0.6 copy-start.3
  23.8 0.7 copy-start.6
  24.5 8.0 %copy-start.2 = (bf16[4,1,48,2560]{3,2,1,0:T(8,128)(2,1)S(1)}, bf16[4,1,48,2560]{3,2,1,0:T(8,128)(2,1)}, u32[]{:S(2)}) copy-start(bf16[4,1,48,2560]{3,2,1,0:T(8,128)(2,1)} %param.10) | copy-start | bytes 2949124
  24.5 8.8 %copy-start.1 = (bf16[3072,256]{1,0:T(8,128)(2,1)S(1)}, bf16[3072,256]{1,0:T(8,128)(2,1)}, u32[]{:S(2)}) copy-start(bf16[3072,256]{1,0:T(8,128)(2,1)} %constant.46.clone.table_hbm.constants_ref) | copy-start | bytes 4718596
  29.0 4.3 %copy-start.4 = (bf16[4,16,128]{2,1,0:T(8,128)(2,1)S(1)}, bf16[4,16,128]{2,1,0:T(8,128)(2,1)}, u32[]{:S(2)}) copy-start(bf16[4,16,128]{2,1,0:T(8,128)(2,1)} %copy-done.3) | copy-start | bytes 49156
  29.0 9.1 %all-to-all-start = ((bf16[4,48,768]{2,1,0:T(8,128)(2,1)}), bf16[4,48,768]{2,1,0:T(8,128)(2,1)S(1)}, u32[]{:S(2)}, u32[]{:S(2)}) async-start(bf16[4,48,768]{2,1,0:T(8,128)(2,1)} %gradient_parts.1), calls=%async_computation | async-start | bytes 589824 | tf_op jit(solution)/shard_map/all_to_all | solution.py:613
  33.3 4.9 %copy-start = (f32[1,48,2560]{2,1,0:T(8,128)S(1)}, f32[1,48,2560]{2,1,0:T(8,128)}, u32[]{:S(2)}) copy-start(f32[1,48,2560]{2,1,0:T(8,128)} %param.9) | copy-start | bytes 1474564
  38.4 3.7 %copy-start.5 = (f32[4,48,640]{2,1,0:T(8,128)S(1)}, f32[4,48,640]{2,1,0:T(8,128)}, u32[]{:S(2)}) copy-start(f32[4,48,640]{2,1,0:T(8,128)} %bitcast_convert_fusion) | copy-start | bytes 1474564
  38.5 3.9 %collective-permute-start.2 = (bf16[8,768]{1,0:T(8,128)(2,1)S(1)}, bf16[8,768]{1,0:T(8,128)(2,1)S(1)}, u32[]{:S(2)}, u32[]{:S(2)}) collective-permute-start(bf16[8,768]{1,0:T(8,128)(2,1)S(1)} %slice.484), channel_id=1, source_target_pairs={{0,4},{4,8},{8,12},{12,16},{16,20},{20,24},{24,28},{28,32},{32,36}... | collective-permute-start | bytes 36872 | tf_op jit(solution)/shard_map/ppermute | solution.py:609
